TPU v7x, 32 devices: a whole 2x2x4 slice. The times are simulated.
32 devices in a mesh: groups: 2 (over y), row: 4 (over z), col: 2 (over x), rep: 2 (over core).
Axes of the slice: x: 2, y: 2, z: 4, core: 2. Of those that a mesh axis runs over, the one named last changes fastest.
Arguments:
- sep_inverse: float32 [6144, 3072], P(('groups', 'row'), ('col', 'rep')), parts along dimension 0, may hold values from -6 to 6
- row_tiles: int32 [12], replicated, may hold values from 0 to 23, as said below
- panel_rows: float32 [3072, 512], P(('groups', 'row')), parts along dimension 0, may hold values from -0.15625 to 0.15625
- diag_inverse: float32 [1024, 512], P('groups'), parts along dimension 0, as said below
Outputs:
- sigma_rows: float32 [3072, 512], P(('groups', 'row', 'col', 'rep')), parts along dimension 0
- sigma_diag: float32 [1024, 512], P(('groups', 'col', 'rep')), parts along dimension 0
- variances: float32 [1024], P(('groups', 'col', 'rep')), parts along dimension 0
There are 2 independent parts, one for each index of `groups`. A program takes and returns all parts, laid end to end along the dimension named above; an argument that names none is the same for every part. Nothing has to cross between parts.
Inputs may be any that keep to these rules, and one draw needn't show every extreme that they name: row_tiles holds, for each aligned block of 6 separator tiles, 3 distinct tiles of that block in increasing order; slot k lies in block k // 3. diag_inverse is lower triangular with a positive diagonal.
All inputs are finite; a program needn't handle non-finite values.
Results may differ from a plain program's by a relative error of at most 0.000071.
Values sent between devices are 32-bit elements; how exact they have to be, the bound alone decides.
No kernel may reach another device: no remote copies, remote signals or barrier semaphores. Data moves between devices by JAX's collectives and lax.ppermute only.
A program may use at most 64 MiB of HBM per device.

v0:
```python
import jax
import jax.numpy as jnp
from jax import lax
from jax.sharding import PartitionSpec as P

TILE = 128


def broadcast(x, axis, root):
    mine = lax.axis_index(axis) == root
    return lax.psum(jnp.where(mine, x, jnp.zeros_like(x)), axis)


def contract_rows(left, right):
    return lax.dot_general(
        left,
        right,
        (((0,), (0,)), ((), ())),
        precision=lax.Precision.HIGHEST,
        preferred_element_type=jnp.float32,
    )


def per_device(sep_inverse, row_tiles, panel_rows, diag_inverse):
    highest = lax.Precision.HIGHEST
    members = lax.axis_size(("col", "rep"))
    column_index = lax.axis_index(("col", "rep"))
    row_index = lax.axis_index("row")
    block_slots = panel_rows.shape[0] // TILE
    block_tiles = sep_inverse.shape[0] // TILE
    width = panel_rows.shape[1]
    own_tiles = (
        lax.dynamic_slice_in_dim(row_tiles, row_index * block_slots, block_slots)
        - row_index * block_tiles
    )
    far_tiles = (
        lax.dynamic_slice_in_dim(row_tiles, column_index * block_slots, block_slots)
        - column_index * block_tiles
    )
    tiled = sep_inverse.reshape(block_tiles, TILE, block_tiles, TILE)
    picked = jnp.take(jnp.take(tiled, own_tiles, axis=0), far_tiles, axis=2)
    picked = picked.reshape(block_slots * TILE, block_slots * TILE)
    own_white = jnp.dot(
        panel_rows, diag_inverse, precision=highest, preferred_element_type=jnp.float32
    )
    far_white = broadcast(own_white, "row", column_index)
    partial_value = -jnp.dot(
        picked, far_white, precision=highest, preferred_element_type=jnp.float32
    )
    piece = partial_value.shape[0] // members
    count = width // members
    first = column_index * count
    sigma_rows = lax.psum_scatter(partial_value, ("col", "rep"), scatter_dimension=0, tiled=True)
    white_mine = lax.dynamic_slice_in_dim(own_white, column_index * piece, piece, 0)
    local_block = lax.psum_scatter(
        contract_rows(sigma_rows, white_mine), ("col", "rep"), scatter_dimension=0, tiled=True
    )
    summed = lax.psum(local_block, "row")
    inverse_cols = lax.dynamic_slice_in_dim(diag_inverse, first, count, 1)
    sigma_diag = contract_rows(inverse_cols, diag_inverse) - summed
    variances = jnp.diagonal(lax.dynamic_slice_in_dim(sigma_diag, first, count, 1))
    return (sigma_rows, sigma_diag, variances)


def solution(mesh):
    return jax.shard_map(
        per_device,
        mesh=mesh,
        in_specs=(
            P(("groups", "row"), ("col", "rep")),
            P(),
            P(("groups", "row"), None),
            P("groups", None),
        ),
        out_specs=(
            P(("groups", "row", "col", "rep"), None),
            P(("groups", "col", "rep"), None),
            P(("groups", "col", "rep")),
        ),
        check_vma=False,
    )
```

profile of v0, /device:TPU:0, one launch (start us, length us, event | category | flops | bytes accessed | tf_op | source)
XLA Modules:
  0.0 160.8 jit_solution(3202599929707270344)
XLA Ops:
  7.2 0.0 all-reduce.3.cloned.1.call-start
  7.2 1.2 copy-done
  8.4 3.9 %broadcast_select_fusion.1 = (f32[384,512]{1,0:T(8,128)}, f32[384,512]{1,0:T(8,128)}) fusion(pred[]{:T(512)S(6)} %eq.3, f32[384,512]{1,0:T(8,128)} %param.6, f32[512,512]{1,0:T(8,128)S(1)} %copy-done), kind=kOutput, calls=%fused_computation.8 | convolution fusion | flops 1208156160 | bytes 3407873 | tf_op jit(solution)/shard_map/dot_general | solution.py:43
  12.3 0.0 all-reduce.3.cloned.1.call-update
  12.3 0.0 reduce-scatter.3.cloned.1.call-start
  12.4 1.8 %reshape.22 = f32[6,128,6,128]{3,2,1,0:T(8,128)} reshape(f32[768,768]{1,0:T(8,128)S(1)} %copy-done.1) | data formatting | bytes 4718592 | tf_op jit(solution)/shard_map/reshape | solution.py:40
  14.2 2.3 %copy.8 = f32[6,128,6,128]{3,1,2,0:T(8,128)S(1)} copy(f32[6,128,6,128]{3,2,1,0:T(8,128)} %reshape.22) | data formatting | bytes 4718592 | tf_op jit(solution)/shard_map/reshape | solution.py:40
  16.6 0.1 compare_and_fusion.1
  16.7 1.6 %gather_fusion = f32[3,128,6,128]{3,1,2,0:T(8,128)} fusion(f32[6,128,6,128]{3,1,2,0:T(8,128)S(1)} %copy.8, s32[1024]{0:T(1024)S(1)} %get-tuple-element.12), kind=kCustom, calls=%fused_computation | custom fusion | bytes 2359308 | tf_op jit(solution)/shard_map/jit(_take)/gather | solution.py:41
  18.3 1.4 broadcast_select_fusion
  19.8 0.6 gather_fusion.1
  20.4 0.4 copy.9
  20.8 0.1 broadcast_bitcast_fusion
  20.8 38.0 %all-reduce.3.cloned.1.call-done = f32[384,512]{1,0:T(8,128)} async-done(((f32[384,512]{1,0:T(8,128)}), f32[384,512]{1,0:T(8,128)}) %all-reduce.3.cloned.1.call-update) | async-done | bytes 786448 | tf_op jit(solution)/shard_map/psum | solution.py:11
  58.9 3.4 %convolution_negate_fusion = f32[384,512]{1,0:T(8,128)} fusion(f32[384,512]{1,0:T(8,128)} %all-reduce.3.cloned.1.call-done, f32[48,8,3,128]{3,2,1,0:T(4,128)S(1)} %bitcast.16, pred[384]{0:T(512)(128)(4,1)S(1)} %broadcast_bitcast_fusion), kind=kOutput, calls=%fused_computation.3 | convolution fusion | flops 906313728 | bytes 2163072 | tf_op jit(solution)/shard_map/dot_general | solution.py:47
  62.3 0.0 reduce-scatter.3.cloned.1.call-update
  62.3 0.0 reduce-scatter.5.cloned.1.call-start
  62.4 22.7 %reduce-scatter.3.cloned.1.call-done = f32[96,512]{1,0:T(8,128)} async-done(((f32[384,512]{1,0:T(8,128)}), f32[96,512]{1,0:T(8,128)}) %reduce-scatter.3.cloned.1.call-update) | async-done | bytes 196624 | tf_op jit(solution)/shard_map/reduce_scatter | solution.py:53
  85.1 3.0 %fusion.4 = f32[512,512]{1,0:T(8,128)} fusion(f32[96,512]{1,0:T(8,128)} %reduce-scatter.3.cloned.1.call-done, f32[384,512]{1,0:T(8,128)} %get-tuple-element.10, s32[]{:T(128)S(6)} %select_n.52), kind=kOutput, calls=%fused_computation.12 | convolution fusion | flops 301989888 | bytes 1441796 | tf_op jit(solution)/shard_map/dot_general | solution.py:15
  88.1 0.0 all-reduce.5.cloned.1.call-start
  88.2 25.0 %reduce-scatter.5.cloned.1.call-done = f32[128,512]{1,0:T(8,128)} async-done(((f32[512,512]{1,0:T(8,128)}), f32[128,512]{1,0:T(8,128)}) %reduce-scatter.5.cloned.1.call-update) | async-done | bytes 262160 | tf_op jit(solution)/shard_map/reduce_scatter | solution.py:55
  113.2 37.5 %all-reduce.5.cloned.1.call-done = f32[128,512]{1,0:T(8,128)} async-done(((f32[128,512]{1,0:T(8,128)}), f32[128,512]{1,0:T(8,128)}) %all-reduce.5.cloned.1.call-update) | async-done | bytes 262160 | tf_op jit(solution)/shard_map/psum | solution.py:58
  150.7 1.7 %convolution_subtract_fusion = f32[128,512]{1,0:T(8,128)S(1)} fusion(f32[128,512]{1,0:T(8,128)} %all-reduce.5.cloned.1.call-done, f32[512,512]{1,0:T(8,128)S(1)} %copy-done, s32[]{:T(128)S(6)} %select_n.51), kind=kOutput, calls=%fused_computation.4 | convolution fusion | flops 402718720 | bytes 1835012 | tf_op jit(solution)/shard_map/dot_general | solution.py:15
  152.5 1.8 %gather_fusion.2 = f32[128]{0:T(128)} fusion(f32[128,128]{1,0:T(8,128)S(1)} %constant_dynamic-slice_fusion, s32[128]{0:T(128)S(1)} %or_bitcast_fusion), kind=kCustom, calls=%fused_computation.2 | custom fusion | bytes 2048 | tf_op jit(solution)/shard_map/jit(diagonal)/cond/branch_0_fun/gather | solution.py:61
  (12 shorter events, 0.1 us)
Async XLA Ops:
  7.2 1.2 copy-start
  7.2 51.7 %all-reduce.3.cloned.1.call-start = ((), (), s32[]{:S(2)}) async-start(), calls=%async_computation.2 | async-start | bytes 1572864 | tf_op jit(solution)/shard_map/psum | solution.py:11
  8.4 4.0 %copy-start.1 = (f32[768,768]{1,0:T(8,128)S(1)}, f32[768,768]{1,0:T(8,128)}, u32[]{:S(2)}) copy-start(f32[768,768]{1,0:T(8,128)} %param.4) | copy-start | bytes 7077892
  12.3 72.7 %reduce-scatter.3.cloned.1.call-start = ((), (), s32[]{:S(2)}) async-start(), calls=%async_computation.3 | async-start | bytes 983040 | tf_op jit(solution)/shard_map/reduce_scatter | solution.py:53
  14.2 2.3 %copy-start.3 = (s32[12]{0:T(128)S(1)}, s32[12]{0:T(128)}, u32[]{:S(2)}) copy-start(s32[12]{0:T(128)} %param.5) | copy-start | bytes 148
  62.3 50.8 %reduce-scatter.5.cloned.1.call-start = ((), (), s32[]{:S(2)}) async-start(), calls=%async_computation.4 | async-start | bytes 1310720 | tf_op jit(solution)/shard_map/reduce_scatter | solution.py:55
  88.1 62.6 %all-reduce.5.cloned.1.call-start = ((), (), s32[]{:S(2)}) async-start(), calls=%async_computation.5 | async-start | bytes 524288 | tf_op jit(solution)/shard_map/psum | solution.py:58
  152.4 1.8 %copy-start.2 = (f32[128,512]{1,0:T(8,128)}, f32[128,512]{1,0:T(8,128)S(1)}, u32[]{:S(2)}) copy-start(f32[128,512]{1,0:T(8,128)S(1)} %convolution_subtract_fusion) | copy-start | bytes 786436
Sparse Core Ops, SparseCore 0:
  12.5 46.3 all-reduce.2
  62.4 22.5 reduce-scatter.2
  88.2 24.8 reduce-scatter.4
  115.3 35.3 all-reduce.4
where the time goes:
time: 161 us
  waiting for transfers between devices  123 us (76%)
  between operations  13.9 us (9%)
  matrix products  12.1 us (8%)
  local copies, waits for them, and re-layouts  9.83 us (6%)
    psum x1, waiting for transfers between devices, broadcast(): return lax.psum(jnp.where(mine, x, jnp.zeros_like(x)), axis)  38 us
    psum x1, waiting for transfers between devices, per_device(): summed = lax.psum(local_block, 'row')  37.5 us
    reduce_scatter x1, waiting for transfers between devices, per_device(): lax.psum_scatter(contract_rows(sigma_rows, white_mine), ('col', 'rep'), s...  25 us
    reduce_scatter x1, waiting for transfers between devices, per_device(): lax.psum_scatter(partial_value, ('col', 'rep'), scatter_dimension=0, tile...  22.7 us
    dot_general x2, matrix products, contract_rows(): lax.dot_general(left, right, (((0,), (0,)), ((), ())), precision=lax.Prec...  4.73 us
    reshape x2, local copies, waits for them, and re-layouts, per_device(): tiled = sep_inverse.reshape(block_tiles, TILE, block_tiles, TILE)  4.15 us
    dot_general x1, matrix products, per_device(): jnp.dot(panel_rows, diag_inverse, precision=highest, preferred_element_ty...  3.91 us
    dot_general x1, matrix products, per_device(): jnp.dot(picked, far_white, precision=highest, preferred_element_type=jnp....  3.43 us
  transfers between devices with their start and end apart: 4, of which 4 were waited for; matrix products, arithmetic and copies ran while one was open for 5% of the time, Pallas kernels for 0%

commit v1 on v0

--- a/solution.py
+++ b/solution.py
@@ -1,9 +1,15 @@
 import jax
 import jax.numpy as jnp
 from jax import lax
+from jax.experimental import pallas as pl
+from jax.experimental.pallas import tpu as pltpu
 from jax.sharding import PartitionSpec as P
 
 TILE = 128
+VMEM = pl.BlockSpec(memory_space=pltpu.VMEM)
+SMEM = pl.BlockSpec(memory_space=pltpu.SMEM)
+ANY = pl.BlockSpec(memory_space=pl.ANY)
+PARAMS = pltpu.CompilerParams(vmem_limit_bytes=32 * 1024 * 1024)
 
 
 def broadcast(x, axis, root):
@@ -21,7 +27,7 @@
     )
 
 
-def per_device(sep_inverse, row_tiles, panel_rows, diag_inverse):
+def any_mesh(sep_inverse, row_tiles, panel_rows, diag_inverse):
     highest = lax.Precision.HIGHEST
     members = lax.axis_size(("col", "rep"))
     column_index = lax.axis_index(("col", "rep"))
@@ -62,7 +68,217 @@
     return (sigma_rows, sigma_diag, variances)
 
 
+def split(x):
+    high = x.astype(jnp.bfloat16)
+    return high, (x - high.astype(jnp.float32)).astype(jnp.bfloat16)
+
+
+def dot(a, b):
+    return jnp.dot(a, b, preferred_element_type=jnp.float32)
+
+
+def dot3(a, b):
+    return dot(a[0], b[0]) + (dot(a[0], b[1]) + dot(a[1], b[0]))
+
+
+def f32(*shape):
+    return jax.ShapeDtypeStruct(shape, jnp.float32)
+
+
+def pick_kernel(tiles_ref, sep_ref, out_ref, sems):
+    row, member = lax.axis_index("row"), lax.axis_index(("col", "rep"))
+    slots, block = out_ref.shape[0] // TILE, sep_ref.shape[0] // TILE
+    copies = []
+    for i in range(slots):
+        down = (tiles_ref[row * slots + i] - row * block) * TILE
+        for j in range(slots):
+            across = (tiles_ref[member * slots + j] - member * block) * TILE
+            copies.append(
+                pltpu.make_async_copy(
+                    sep_ref.at[
+                        pl.ds(pl.multiple_of(down, TILE), TILE),
+                        pl.ds(pl.multiple_of(across, TILE), TILE),
+                    ],
+                    out_ref.at[pl.ds(i * TILE, TILE), pl.ds(j * TILE, TILE)],
+                    sems.at[i * slots + j],
+                )
+            )
+    for copy in copies:
+        copy.start()
+    for copy in copies:
+        copy.wait()
+
+
+def pick(row_tiles, sep_inverse, slots):
+    return pl.pallas_call(
+        pick_kernel,
+        out_shape=f32(slots * TILE, slots * TILE),
+        in_specs=[SMEM, ANY],
+        out_specs=ANY,
+        scratch_shapes=[pltpu.SemaphoreType.DMA((slots * slots,))],
+        compiler_params=PARAMS,
+    )(row_tiles, sep_inverse)
+
+
+def quarter_kernel(panel_ref, inverse_ref, out_ref):
+    member = lax.axis_index(("col", "rep"))
+    columns = pl.ds(pl.multiple_of(member * TILE, TILE), TILE)
+    out_ref[...] = dot3(split(panel_ref[...]), split(inverse_ref[:, columns]))
+
+
+def white_quarter(panel_rows, diag_inverse):
+    return pl.pallas_call(
+        quarter_kernel,
+        out_shape=f32(panel_rows.shape[0], TILE),
+        in_specs=[VMEM, VMEM],
+        out_specs=VMEM,
+        compiler_params=PARAMS,
+    )(panel_rows, diag_inverse)
+
+
+def whiten_kernel(panel_ref, inverse_ref, high_ref, low_ref, base_ref):
+    member = lax.axis_index(("col", "rep"))
+    columns = pl.ds(pl.multiple_of(member * TILE, TILE), TILE)
+    inverse = split(inverse_ref[...])
+    high, low = split(dot3(split(panel_ref[...]), inverse))
+    high_ref[...] = high
+    low_ref[...] = low
+    base_ref[...] = dot3(split(inverse_ref[:, columns].T), inverse)
+
+
+def whiten(panel_rows, diag_inverse):
+    shape = jax.ShapeDtypeStruct(panel_rows.shape, jnp.bfloat16)
+    return pl.pallas_call(
+        whiten_kernel,
+        out_shape=(shape, shape, f32(TILE, diag_inverse.shape[1])),
+        in_specs=[VMEM, VMEM],
+        out_specs=(VMEM,) * 3,
+        compiler_params=PARAMS,
+    )(panel_rows, diag_inverse)
+
+
+def product_kernel(*refs):
+    seps, whites, (own_high, own_low) = refs[0:4], refs[4:8], refs[8:10]
+    terms, pieces = refs[10:14], refs[14:18]
+    white_high, white_low, product = refs[18:21]
+    row, member = lax.axis_index("row"), lax.axis_index(("col", "rep"))
+    for j in range(4):
+        high, low = split(whites[j][...])
+        white_high[row ^ j] = high
+        white_low[row ^ j] = low
+    total = None
+    for i in range(4):
+        term = dot3(split(seps[i][...]), (white_high[member ^ i], white_low[member ^ i]))
+        total = term if total is None else total + term
+    product[...] = -total
+    flipped = split(total.T)
+    count = pieces[0].shape[0]
+    for j in range(4):
+        columns = pl.ds(pl.multiple_of((row ^ j) * TILE, TILE), TILE)
+        terms[j][...] = dot3(flipped, (own_high[:, columns], own_low[:, columns]))
+        pieces[j][...] = product[pl.ds(pl.multiple_of((member ^ j) * count, 8), count), :]
+
+
+def products(seps, whites, own_white):
+    depth, width = whites[0].shape
+    return pl.pallas_call(
+        product_kernel,
+        out_shape=(f32(width, TILE),) * 4 + (f32(depth // 4, width),) * 4,
+        in_specs=[VMEM] * 10,
+        out_specs=(VMEM,) * 8,
+        scratch_shapes=[
+            pltpu.VMEM((4, depth, width), jnp.bfloat16),
+            pltpu.VMEM((4, depth, width), jnp.bfloat16),
+            pltpu.VMEM((depth, width), jnp.float32),
+        ],
+        compiler_params=PARAMS,
+    )(*seps, *whites, *own_white)
+
+
+def rows_kernel(own, near, across, far, out_ref):
+    member = lax.axis_index(("col", "rep"))
+    for j, ref in enumerate((own, near, across, far)):
+        out_ref[:, pl.ds(pl.multiple_of((member ^ j) * TILE, TILE), TILE)] = ref[...]
+
+
+def rows_of(pieces):
+    count, width = pieces[0].shape
+    return pl.pallas_call(
+        rows_kernel,
+        out_shape=f32(count, 4 * width),
+        in_specs=[VMEM] * 4,
+        out_specs=VMEM,
+        compiler_params=PARAMS,
+    )(*pieces)
+
+
+def diagonal_kernel(own, one, two, three, base_ref, out_ref, variances_ref):
+    row, member = lax.axis_index("row"), lax.axis_index(("col", "rep"))
+    for j, ref in enumerate((own, one, two, three)):
+        columns = pl.ds(pl.multiple_of((row ^ j) * TILE, TILE), TILE)
+        out_ref[:, columns] = base_ref[:, columns] + ref[...]
+    square = out_ref[:, pl.ds(pl.multiple_of(member * TILE, TILE), TILE)]
+    across = lax.broadcasted_iota(jnp.int32, square.shape, 0)
+    down = lax.broadcasted_iota(jnp.int32, square.shape, 1)
+    variances_ref[...] = jnp.sum(jnp.where(across == down, square, 0.0), axis=0, keepdims=True)
+
+
+def diagonal(blocks, base):
+    return pl.pallas_call(
+        diagonal_kernel,
+        out_shape=(f32(*base.shape), f32(1, TILE)),
+        in_specs=[VMEM] * 5,
+        out_specs=(VMEM, VMEM),
+        compiler_params=PARAMS,
+    )(*blocks, base)
+
+
+def rows_apart(j):
+    return [(i, i ^ j) for i in range(4)]
+
+
+SWAP = [(0, 1), (1, 0)]
+
+
+def four_by_four(sep_inverse, row_tiles, panel_rows, diag_inverse):
+    quarter = white_quarter(panel_rows, diag_inverse)
+    whites = [quarter] + [lax.ppermute(quarter, "row", rows_apart(j)) for j in (1, 2, 3)]
+
+    own = pick(row_tiles, sep_inverse, panel_rows.shape[0] // TILE)
+    near = lax.ppermute(own, "rep", SWAP)
+    across = lax.ppermute(own, "col", SWAP)
+    far = lax.ppermute(across, "rep", SWAP)
+
+    *own_white, base = whiten(panel_rows, diag_inverse)
+    out = products((own, near, across, far), whites, own_white)
+    terms, pieces = out[:4], out[4:]
+
+    block = terms[0]
+    for j in (1, 2, 3):
+        block = block + lax.ppermute(terms[j], "row", rows_apart(j))
+    blocks = [block] + [lax.ppermute(block, "row", rows_apart(j)) for j in (1, 2, 3)]
+    sigma_diag, variances = diagonal(blocks, base)
+
+    sigma_rows = rows_of(
+        [
+            pieces[0],
+            lax.ppermute(pieces[1], "rep", SWAP),
+            lax.ppermute(pieces[2], "col", SWAP),
+            lax.ppermute(pieces[3], ("col", "rep"), rows_apart(3)),
+        ]
+    )
+    return sigma_rows, sigma_diag, variances.reshape(-1)
+
+
 def solution(mesh):
+    shape = mesh.shape
+
+    def per_device(sep_inverse, row_tiles, panel_rows, diag_inverse):
+        square = (shape["row"], shape["col"], shape["rep"]) == (4, 2, 2)
+        fits = diag_inverse.shape == (4 * TILE, 4 * TILE) and panel_rows.shape[0] % TILE == 0
+        form = four_by_four if square and fits else any_mesh
+        return form(sep_inverse, row_tiles, panel_rows, diag_inverse)
+
     return jax.shard_map(
         per_device,
         mesh=mesh,

time: 161 us -> 64.2 us (0.40)
  waiting for transfers between devices: 123 us -> 37.5 us
  starting transfers between devices: 0.16 us -> 18 us
  between operations: 13.9 us -> 0.72 us
  matrix products: 12.1 us -> 0 us
  local copies, waits for them, and re-layouts: 9.83 us -> 2.41 us
  Pallas kernels: 0 us -> 5.45 us
    psum x2 -> x0, waiting for transfers between devices: 75.6 us -> none  [the longest x1 38 us: broadcast(): return lax.psum(jnp.where(mine, x, jnp.zeros_like(x)), axis)]
    reduce_scatter x2 -> x0, waiting for transfers between devices: 47.7 us -> none  [the longest x1 25 us: per_device(): lax.psum_scatter(contract_rows(sigma_rows, white_mine), ('col', 'rep'), s...]
    ppermute x0 -> x15, waiting for transfers between devices: none -> 37.5 us  [the longest x3 15.7 us: four_by_four(): lax.ppermute(quarter, 'row', rows_apart(j))]
    ppermute x0 -> x15, starting transfers between devices: none -> 18 us  [the longest x3 4.56 us: four_by_four(): lax.ppermute(quarter, 'row', rows_apart(j))]
    dot_general x4 -> x0, matrix products: 12.1 us -> none  [the longest x2 4.73 us: contract_rows(): lax.dot_general(left, right, (((0,), (0,)), ((), ())), precision=lax.Prec...]
    pallas_call x0 -> x6, Pallas kernels: none -> 5.45 us  [the longest x1 1.76 us: products(): pl.pallas_call(product_kernel, out_shape=(f32(width, TILE),) * 4 + (f32(d...]
    gather x4 -> x0, local copies, waits for them, and re-layouts: 4.4 us -> none  [the longest x3 2.64 us: per_device(): picked = jnp.take(jnp.take(tiled, own_tiles, axis=0), far_tiles, axis=2)]
    reshape x2 -> x0, local copies, waits for them, and re-layouts: 4.15 us -> none  [per_device(): tiled = sep_inverse.reshape(block_tiles, TILE, block_tiles, TILE)]
  transfers between devices with their start and end apart: 4 -> 15, of which waited for: 4 -> 8; matrix products, arithmetic and copies ran while one was open for 5% -> 0% of each run, Pallas kernels for 0% -> 3%
where the time goes in v1:
time: 64.2 us; the launch traced here: 64.1 us
  waiting for transfers between devices  37.5 us (58%)
  starting transfers between devices  18 us (28%)
  Pallas kernels  5.45 us (8%)
  local copies, waits for them, and re-layouts  2.41 us (4%)
  between operations  0.72 us (1%)
    ppermute x3, waiting for transfers between devices, four_by_four(): lax.ppermute(quarter, 'row', rows_apart(j))  15.7 us
    ppermute x1, waiting for transfers between devices, four_by_four(): across = lax.ppermute(own, 'col', SWAP)  13.3 us
    ppermute x3, waiting for transfers between devices, four_by_four(): block = block + lax.ppermute(terms[j], 'row', rows_apart(j))  4.82 us
    ppermute x3, starting transfers between devices, four_by_four(): lax.ppermute(quarter, 'row', rows_apart(j))  4.56 us
    ppermute x3, starting transfers between devices, four_by_four(): lax.ppermute(block, 'row', rows_apart(j))  4.45 us
    ppermute x3, starting transfers between devices, four_by_four(): block = block + lax.ppermute(terms[j], 'row', rows_apart(j))  4.44 us
    ppermute x1, starting transfers between devices, four_by_four(): across = lax.ppermute(own, 'col', SWAP)  3 us
    ppermute x1, waiting for transfers between devices, four_by_four(): lax.ppermute(pieces[2], 'col', SWAP)  2.6 us
  transfers between devices with their start and end apart: 15, of which 8 were waited for; matrix products, arithmetic and copies ran while one was open for 0% of the time, Pallas kernels for 3%

profile of v1, /device:TPU:0, one launch (start us, length us, event | category | flops | bytes accessed | tf_op | source)
XLA Modules:
  0.0 64.1 jit_solution(12606482397012955191)
XLA Ops:
  0.7 1.7 %copy-done.2 = f32[768,768]{1,0:T(8,128)S(1)} copy-done((f32[768,768]{1,0:T(8,128)S(1)}, f32[768,768]{1,0:T(8,128)}, u32[]{:S(2)}) %copy-start.2) | copy-done | bytes 2359320
  2.4 0.7 %copy-done.3 = s32[12]{0:T(128)S(1)} copy-done((s32[12]{0:T(128)S(1)}, s32[12]{0:T(128)}, u32[]{:S(2)}) %copy-start.3) | copy-done | bytes 72
  3.1 0.7 %shard_map.67.refs_0_ = f32[384,384]{1,0:T(8,128)S(1)} custom-call(s32[12]{0:T(128)S(1)} %copy-done.3, f32[768,768]{1,0:T(8,128)S(1)} %copy-done.2), custom_call_target="tpu_custom_call" | custom-call | tf_op jit(solution)/shard_map/pallas_call | solution.py:113
  3.8 3.0 %collective-permute-start.1 = (f32[384,384]{1,0:T(8,128)S(1)}, f32[384,384]{1,0:T(8,128)S(1)}, u32[]{:S(2)}, u32[]{:S(2)}) collective-permute-start(f32[384,384]{1,0:T(8,128)S(1)} %shard_map.67.refs_0_), channel_id=1, source_target_pairs={{0,2},{2,0},{1,3},{3,1},{4,6},{6,4},{5,7},{7,5},{8,10},{10,8},{9,1... | collective-permute-start | bytes 1769480 | tf_op jit(solution)/shard_map/ppermute | solution.py:249
  6.8 13.3 %collective-permute-done.1.refs_2_ = f32[384,384]{1,0:T(8,128)S(1)} collective-permute-done((f32[384,384]{1,0:T(8,128)S(1)}, f32[384,384]{1,0:T(8,128)S(1)}, u32[]{:S(2)}, u32[]{:S(2)}) %collective-permute-start.1) | collective-permute-done | bytes 589856 | tf_op jit(solution)/shard_map/ppermute | solution.py:249
  20.1 0.5 shard_map.68.refs_4_
  20.6 3.9 %collective-permute-start.5 = (f32[384,128]{1,0:T(8,128)S(1)}, f32[384,128]{1,0:T(8,128)S(1)}, u32[]{:S(2)}, u32[]{:S(2)}) collective-permute-start(f32[384,128]{1,0:T(8,128)S(1)} %shard_map.68.refs_4_), channel_id=1, source_target_pairs={{0,12},{4,8},{8,4},{12,0},{1,13},{5,9},{9,5},{13,1},{2,14},{6,10},... | collective-permute-start | bytes 589832 | tf_op jit(solution)/shard_map/ppermute | solution.py:245
  24.6 0.6 collective-permute-start.3
  25.2 1.0 %shard_map.69 = (bf16[384,512]{1,0:T(8,128)(2,1)S(1)}, bf16[384,512]{1,0:T(8,128)(2,1)S(1)}, f32[128,512]{1,0:T(8,128)S(1)}) custom-call(f32[384,512]{1,0:T(8,128)S(1)} %copy-done.1, f32[512,512]{1,0:T(8,128)S(1)} %copy-done), custom_call_target="tpu_custom_call" | custom-call | tf_op jit(solution)/shard_map/pallas_call | solution.py:151
  26.2 4.2 %collective-permute-done.5.refs_7_ = f32[384,128]{1,0:T(8,128)S(1)} collective-permute-done((f32[384,128]{1,0:T(8,128)S(1)}, f32[384,128]{1,0:T(8,128)S(1)}, u32[]{:S(2)}, u32[]{:S(2)}) %collective-permute-start.5) | collective-permute-done | bytes 196640 | tf_op jit(solution)/shard_map/ppermute | solution.py:245
  30.4 11.5 %collective-permute-done.4.refs_6_ = f32[384,128]{1,0:T(8,128)S(1)} collective-permute-done((f32[384,128]{1,0:T(8,128)S(1)}, f32[384,128]{1,0:T(8,128)S(1)}, u32[]{:S(2)}, u32[]{:S(2)}) %collective-permute-start.4) | collective-permute-done | bytes 196640 | tf_op jit(solution)/shard_map/ppermute | solution.py:245
  41.9 1.8 %shard_map.70 = (f32[128,128]{1,0:T(8,128)S(1)}, f32[128,128]{1,0:T(8,128)S(1)}, f32[128,128]{1,0:T(8,128)S(1)}, f32[128,128]{1,0:T(8,128)S(1)}, f32[96,128]{1,0...) custom-call(f32[384,384]{1,0:T(8,128)S(1)} %shard_map.67.refs_0_, ...), custom_call_target="tpu_custom_call" | custom-call | tf_op jit(solution)/shard_map/pallas_call | solution.py:184
  43.8 3.0 %collective-permute-start.10 = (f32[128,128]{1,0:T(8,128)S(1)}, f32[128,128]{1,0:T(8,128)S(1)}, u32[]{:S(2)}, u32[]{:S(2)}) collective-permute-start(f32[128,128]{1,0:T(8,128)S(1)} %get-tuple-element.24), channel_id=1, source_target_pairs={{0,8},{4,12},{8,0},{12,4},{1,9},{5,13},{9,1},{13,5},{2,10},{6,14},... | collective-permute-start | bytes 196616 | tf_op jit(solution)/shard_map/ppermute | solution.py:258
  46.8 1.3 %collective-permute-start.11 = (f32[128,128]{1,0:T(8,128)S(1)}, f32[128,128]{1,0:T(8,128)S(1)}, u32[]{:S(2)}, u32[]{:S(2)}) collective-permute-start(f32[128,128]{1,0:T(8,128)S(1)} %get-tuple-element.25), channel_id=1, source_target_pairs={{0,12},{4,8},{8,4},{12,0},{1,13},{5,9},{9,5},{13,1},{2,14},{6,10},... | collective-permute-start | bytes 196616 | tf_op jit(solution)/shard_map/ppermute | solution.py:258
  48.5 3.2 %collective-permute-done.10 = f32[128,128]{1,0:T(8,128)S(1)} collective-permute-done((f32[128,128]{1,0:T(8,128)S(1)}, f32[128,128]{1,0:T(8,128)S(1)}, u32[]{:S(2)}, u32[]{:S(2)}) %collective-permute-start.10) | collective-permute-done | bytes 65568 | tf_op jit(solution)/shard_map/ppermute | solution.py:258
  51.7 1.3 %collective-permute-done.11 = f32[128,128]{1,0:T(8,128)S(1)} collective-permute-done((f32[128,128]{1,0:T(8,128)S(1)}, f32[128,128]{1,0:T(8,128)S(1)}, u32[]{:S(2)}, u32[]{:S(2)}) %collective-permute-start.11) | collective-permute-done | bytes 65568 | tf_op jit(solution)/shard_map/ppermute | solution.py:258
  53.0 1.5 %collective-permute-start.14 = (f32[128,128]{1,0:T(8,128)S(1)}, f32[128,128]{1,0:T(8,128)S(1)}, u32[]{:S(2)}, u32[]{:S(2)}) collective-permute-start(f32[128,128]{1,0:T(8,128)S(1)} %add_add_fusion.own), channel_id=1, source_target_pairs={{0,12},{4,8},{8,4},{12,0},{1,13},{5,9},{9,5},{13,1},{2,14},{6,10},... | collective-permute-start | bytes 196616 | tf_op jit(solution)/shard_map/ppermute | solution.py:259
  54.5 0.7 %collective-permute-start.13 = (f32[128,128]{1,0:T(8,128)S(1)}, f32[128,128]{1,0:T(8,128)S(1)}, u32[]{:S(2)}, u32[]{:S(2)}) collective-permute-start(f32[128,128]{1,0:T(8,128)S(1)} %add_add_fusion.own), channel_id=1, source_target_pairs={{0,8},{4,12},{8,0},{12,4},{1,9},{5,13},{9,1},{13,5},{2,10},{6,14},... | collective-permute-start | bytes 196616 | tf_op jit(solution)/shard_map/ppermute | solution.py:259
  55.2 2.2 %collective-permute-start.12 = (f32[128,128]{1,0:T(8,128)S(1)}, f32[128,128]{1,0:T(8,128)S(1)}, u32[]{:S(2)}, u32[]{:S(2)}) collective-permute-start(f32[128,128]{1,0:T(8,128)S(1)} %add_add_fusion.own), channel_id=1, source_target_pairs={{0,4},{4,0},{8,12},{12,8},{1,5},{5,1},{9,13},{13,9},{2,6},{6,2},{1... | collective-permute-start | bytes 196616 | tf_op jit(solution)/shard_map/ppermute | solution.py:259
  57.4 1.5 %collective-permute-start.7 = (f32[96,128]{1,0:T(8,128)S(1)}, f32[96,128]{1,0:T(8,128)S(1)}, u32[]{:S(2)}, u32[]{:S(2)}) collective-permute-start(f32[96,128]{1,0:T(8,128)S(1)} %get-tuple-element.20), channel_id=1, source_target_pairs={{0,2},{2,0},{1,3},{3,1},{4,6},{6,4},{5,7},{7,5},{8,10},{10,8},{9,1... | collective-permute-start | bytes 147464 | tf_op jit(solution)/shard_map/ppermute | solution.py:266
  58.9 2.6 %collective-permute-done.7.across = f32[96,128]{1,0:T(8,128)S(1)} collective-permute-done((f32[96,128]{1,0:T(8,128)S(1)}, f32[96,128]{1,0:T(8,128)S(1)}, u32[]{:S(2)}, u32[]{:S(2)}) %collective-permute-start.7) | collective-permute-done | bytes 49184 | tf_op jit(solution)/shard_map/ppermute | solution.py:266
  61.5 1.1 %collective-permute-done.8.far = f32[96,128]{1,0:T(8,128)S(1)} collective-permute-done((f32[96,128]{1,0:T(8,128)S(1)}, f32[96,128]{1,0:T(8,128)S(1)}, u32[]{:S(2)}, u32[]{:S(2)}) %collective-permute-start.8) | collective-permute-done | bytes 49184 | tf_op jit(solution)/shard_map/ppermute | solution.py:267
  62.6 0.7 %shard_map.71 = f32[96,512]{1,0:T(8,128)} custom-call(f32[96,128]{1,0:T(8,128)S(1)} %get-tuple-element.18.own, f32[96,128]{1,0:T(8,128)S(1)} %collective-permute-done.6.near, f32[96,128]{1,0:T(8,128)S(1)} %collective-permute-done.7.across, f32[96,128]{1,0:T(8,128)S(1)} %collective-permute-done.8.far), custom_call_target="tpu_custom_call" | custom-call | tf_op jit(solution)/shard_map/pallas_call | solution.py:206
  63.3 0.8 %shard_map.72 = (f32[128,512]{1,0:T(8,128)}, f32[1,128]{1,0:T(1,128)}) custom-call(f32[128,128]{1,0:T(8,128)S(1)} %add_add_fusion.own, f32[128,128]{1,0:T(8,128)S(1)} %collective-permute-done.12.one, f32[128,128]{1,0:T(8,128)S(1)} %collective-permute-done.13.two, f32[128,128]{1,0:T(8,128)S(1)} %collective-permute-done.14.three, ...), custom_call_target="tpu_custom_call" | custom-call | tf_op jit(solution)/shard_map/pallas_call | solution.py:227
  (21 shorter events, 0.5 us)
Async XLA Ops:
  0.6 19.5 %copy-start = (f32[512,512]{1,0:T(8,128)S(1)}, f32[512,512]{1,0:T(8,128)}, u32[]{:S(2)}) copy-start(f32[512,512]{1,0:T(8,128)} %inverse_ref.3) | copy-start | bytes 3145732
  0.6 1.8 %copy-start.2 = (f32[768,768]{1,0:T(8,128)S(1)}, f32[768,768]{1,0:T(8,128)}, u32[]{:S(2)}) copy-start(f32[768,768]{1,0:T(8,128)} %sep_ref.1) | copy-start | bytes 7077892
  2.4 0.7 %copy-start.3 = (s32[12]{0:T(128)S(1)}, s32[12]{0:T(128)}, u32[]{:S(2)}) copy-start(s32[12]{0:T(128)} %tiles_ref.1) | copy-start | bytes 148
  3.1 17.1 %copy-start.1 = (f32[384,512]{1,0:T(8,128)S(1)}, f32[384,512]{1,0:T(8,128)}, u32[]{:S(2)}) copy-start(f32[384,512]{1,0:T(8,128)} %panel_ref.3) | copy-start | bytes 2359300
  3.8 16.3 %collective-permute-start.1 = (f32[384,384]{1,0:T(8,128)S(1)}, f32[384,384]{1,0:T(8,128)S(1)}, u32[]{:S(2)}, u32[]{:S(2)}) collective-permute-start(f32[384,384]{1,0:T(8,128)S(1)} %shard_map.67.refs_0_), channel_id=1, source_target_pairs={{0,2},{2,0},{1,3},{3,1},{4,6},{6,4},{5,7},{7,5},{8,10},{10,8},{9,1... | collective-permute-start | bytes 1769480 | tf_op jit(solution)/shard_map/ppermute | solution.py:249
  6.8 35.1 %collective-permute-start = (f32[384,384]{1,0:T(8,128)S(1)}, f32[384,384]{1,0:T(8,128)S(1)}, u32[]{:S(2)}, u32[]{:S(2)}) collective-permute-start(f32[384,384]{1,0:T(8,128)S(1)} %shard_map.67.refs_0_), channel_id=1, source_target_pairs={{0,1},{1,0},{2,3},{3,2},{4,5},{5,4},{6,7},{7,6},{8,9},{9,8},{10,11... | collective-permute-start | bytes 1769480 | tf_op jit(solution)/shard_map/ppermute | solution.py:248
  20.1 21.8 %collective-permute-start.2 = (f32[384,384]{1,0:T(8,128)S(1)}, f32[384,384]{1,0:T(8,128)S(1)}, u32[]{:S(2)}, u32[]{:S(2)}) collective-permute-start(f32[384,384]{1,0:T(8,128)S(1)} %collective-permute-done.1.refs_2_), channel_id=1, source_target_pairs={{0,1},{1,0},{2,3},{3,2},{4,5},{5,4},{6,7},{7,6},{8,9},{9,8},{10,11... | collective-permute-start | bytes 1769480 | tf_op jit(solution)/shard_map/ppermute | solution.py:250
  20.6 9.8 %collective-permute-start.5 = (f32[384,128]{1,0:T(8,128)S(1)}, f32[384,128]{1,0:T(8,128)S(1)}, u32[]{:S(2)}, u32[]{:S(2)}) collective-permute-start(f32[384,128]{1,0:T(8,128)S(1)} %shard_map.68.refs_4_), channel_id=1, source_target_pairs={{0,12},{4,8},{8,4},{12,0},{1,13},{5,9},{9,5},{13,1},{2,14},{6,10},... | collective-permute-start | bytes 589832 | tf_op jit(solution)/shard_map/ppermute | solution.py:245
  24.5 17.4 %collective-permute-start.4 = (f32[384,128]{1,0:T(8,128)S(1)}, f32[384,128]{1,0:T(8,128)S(1)}, u32[]{:S(2)}, u32[]{:S(2)}) collective-permute-start(f32[384,128]{1,0:T(8,128)S(1)} %shard_map.68.refs_4_), channel_id=1, source_target_pairs={{0,8},{4,12},{8,0},{12,4},{1,9},{5,13},{9,1},{13,5},{2,10},{6,14},... | collective-permute-start | bytes 589832 | tf_op jit(solution)/shard_map/ppermute | solution.py:245
  24.6 17.4 %collective-permute-start.3 = (f32[384,128]{1,0:T(8,128)S(1)}, f32[384,128]{1,0:T(8,128)S(1)}, u32[]{:S(2)}, u32[]{:S(2)}) collective-permute-start(f32[384,128]{1,0:T(8,128)S(1)} %shard_map.68.refs_4_), channel_id=1, source_target_pairs={{0,4},{4,0},{8,12},{12,8},{1,5},{5,1},{9,13},{13,9},{2,6},{6,2},{1... | collective-permute-start | bytes 589832 | tf_op jit(solution)/shard_map/ppermute | solution.py:245
  43.7 4.8 %collective-permute-start.9 = (f32[128,128]{1,0:T(8,128)S(1)}, f32[128,128]{1,0:T(8,128)S(1)}, u32[]{:S(2)}, u32[]{:S(2)}) collective-permute-start(f32[128,128]{1,0:T(8,128)S(1)} %get-tuple-element.23), channel_id=1, source_target_pairs={{0,4},{4,0},{8,12},{12,8},{1,5},{5,1},{9,13},{13,9},{2,6},{6,2},{1... | collective-permute-start | bytes 196616 | tf_op jit(solution)/shard_map/ppermute | solution.py:258
  43.8 7.9 %collective-permute-start.10 = (f32[128,128]{1,0:T(8,128)S(1)}, f32[128,128]{1,0:T(8,128)S(1)}, u32[]{:S(2)}, u32[]{:S(2)}) collective-permute-start(f32[128,128]{1,0:T(8,128)S(1)} %get-tuple-element.24), channel_id=1, source_target_pairs={{0,8},{4,12},{8,0},{12,4},{1,9},{5,13},{9,1},{13,5},{2,10},{6,14},... | collective-permute-start | bytes 196616 | tf_op jit(solution)/shard_map/ppermute | solution.py:258
  46.8 6.2 %collective-permute-start.11 = (f32[128,128]{1,0:T(8,128)S(1)}, f32[128,128]{1,0:T(8,128)S(1)}, u32[]{:S(2)}, u32[]{:S(2)}) collective-permute-start(f32[128,128]{1,0:T(8,128)S(1)} %get-tuple-element.25), channel_id=1, source_target_pairs={{0,12},{4,8},{8,4},{12,0},{1,13},{5,9},{9,5},{13,1},{2,14},{6,10},... | collective-permute-start | bytes 196616 | tf_op jit(solution)/shard_map/ppermute | solution.py:258
  48.1 10.8 %collective-permute-start.6 = (f32[96,128]{1,0:T(8,128)S(1)}, f32[96,128]{1,0:T(8,128)S(1)}, u32[]{:S(2)}, u32[]{:S(2)}) collective-permute-start(f32[96,128]{1,0:T(8,128)S(1)} %get-tuple-element.19), channel_id=1, source_target_pairs={{0,1},{1,0},{2,3},{3,2},{4,5},{5,4},{6,7},{7,6},{8,9},{9,8},{10,11... | collective-permute-start | bytes 147464 | tf_op jit(solution)/shard_map/ppermute | solution.py:265
  53.0 10.3 %collective-permute-start.14 = (f32[128,128]{1,0:T(8,128)S(1)}, f32[128,128]{1,0:T(8,128)S(1)}, u32[]{:S(2)}, u32[]{:S(2)}) collective-permute-start(f32[128,128]{1,0:T(8,128)S(1)} %add_add_fusion.own), channel_id=1, source_target_pairs={{0,12},{4,8},{8,4},{12,0},{1,13},{5,9},{9,5},{13,1},{2,14},{6,10},... | collective-permute-start | bytes 196616 | tf_op jit(solution)/shard_map/ppermute | solution.py:259
  54.5 8.8 %collective-permute-start.13 = (f32[128,128]{1,0:T(8,128)S(1)}, f32[128,128]{1,0:T(8,128)S(1)}, u32[]{:S(2)}, u32[]{:S(2)}) collective-permute-start(f32[128,128]{1,0:T(8,128)S(1)} %add_add_fusion.own), channel_id=1, source_target_pairs={{0,8},{4,12},{8,0},{12,4},{1,9},{5,13},{9,1},{13,5},{2,10},{6,14},... | collective-permute-start | bytes 196616 | tf_op jit(solution)/shard_map/ppermute | solution.py:259
  55.2 8.1 %collective-permute-start.12 = (f32[128,128]{1,0:T(8,128)S(1)}, f32[128,128]{1,0:T(8,128)S(1)}, u32[]{:S(2)}, u32[]{:S(2)}) collective-permute-start(f32[128,128]{1,0:T(8,128)S(1)} %add_add_fusion.own), channel_id=1, source_target_pairs={{0,4},{4,0},{8,12},{12,8},{1,5},{5,1},{9,13},{13,9},{2,6},{6,2},{1... | collective-permute-start | bytes 196616 | tf_op jit(solution)/shard_map/ppermute | solution.py:259
  57.4 4.1 %collective-permute-start.7 = (f32[96,128]{1,0:T(8,128)S(1)}, f32[96,128]{1,0:T(8,128)S(1)}, u32[]{:S(2)}, u32[]{:S(2)}) collective-permute-start(f32[96,128]{1,0:T(8,128)S(1)} %get-tuple-element.20), channel_id=1, source_target_pairs={{0,2},{2,0},{1,3},{3,1},{4,6},{6,4},{5,7},{7,5},{8,10},{10,8},{9,1... | collective-permute-start | bytes 147464 | tf_op jit(solution)/shard_map/ppermute | solution.py:266
  58.9 3.7 %collective-permute-start.8 = (f32[96,128]{1,0:T(8,128)S(1)}, f32[96,128]{1,0:T(8,128)S(1)}, u32[]{:S(2)}, u32[]{:S(2)}) collective-permute-start(f32[96,128]{1,0:T(8,128)S(1)} %get-tuple-element.21), channel_id=1, source_target_pairs={{0,3},{1,2},{2,1},{3,0},{4,7},{5,6},{6,5},{7,4},{8,11},{9,10},{10,... | collective-permute-start | bytes 147464 | tf_op jit(solution)/shard_map/ppermute | solution.py:267

commit v2 on v1

--- a/solution.py
+++ b/solution.py
@@ -6,10 +6,11 @@
 from jax.sharding import PartitionSpec as P
 
 TILE = 128
+ORDER = (2, 3, 1)
+NS = 7
 VMEM = pl.BlockSpec(memory_space=pltpu.VMEM)
-SMEM = pl.BlockSpec(memory_space=pltpu.SMEM)
 ANY = pl.BlockSpec(memory_space=pl.ANY)
-PARAMS = pltpu.CompilerParams(vmem_limit_bytes=32 * 1024 * 1024)
+PARAMS = pltpu.CompilerParams(vmem_limit_bytes=16 * 1024 * 1024)
 
 
 def broadcast(x, axis, root):
@@ -85,114 +86,135 @@
     return jax.ShapeDtypeStruct(shape, jnp.float32)
 
 
-def pick_kernel(tiles_ref, sep_ref, out_ref, sems):
+def first_kernel(
+    tiles_hbm, sep_hbm, panel_hbm, inverse_hbm, white_ref, picked_ref, tiles, panel, inverse, sems
+):
     row, member = lax.axis_index("row"), lax.axis_index(("col", "rep"))
-    slots, block = out_ref.shape[0] // TILE, sep_ref.shape[0] // TILE
-    copies = []
+    columns = pl.ds(pl.multiple_of(member * TILE, TILE), TILE)
+    slots, block = picked_ref.shape[0] // TILE, sep_hbm.shape[0] // TILE
+    fetch = [
+        pltpu.make_async_copy(tiles_hbm, tiles, sems.at[0]),
+        pltpu.make_async_copy(panel_hbm, panel, sems.at[1]),
+        pltpu.make_async_copy(inverse_hbm.at[:, columns], inverse, sems.at[2]),
+    ]
+    for copy in fetch:
+        copy.start()
+    fetch[0].wait()
+    picks = []
     for i in range(slots):
-        down = (tiles_ref[row * slots + i] - row * block) * TILE
+        down = (tiles[row * slots + i] - row * block) * TILE
         for j in range(slots):
-            across = (tiles_ref[member * slots + j] - member * block) * TILE
-            copies.append(
+            across = (tiles[member * slots + j] - member * block) * TILE
+            picks.append(
                 pltpu.make_async_copy(
-                    sep_ref.at[
+                    sep_hbm.at[
                         pl.ds(pl.multiple_of(down, TILE), TILE),
                         pl.ds(pl.multiple_of(across, TILE), TILE),
                     ],
-                    out_ref.at[pl.ds(i * TILE, TILE), pl.ds(j * TILE, TILE)],
-                    sems.at[i * slots + j],
+                    picked_ref.at[pl.ds(i * TILE, TILE), pl.ds(j * TILE, TILE)],
+                    sems.at[3 + i * slots + j],
                 )
             )
-    for copy in copies:
+    for copy in picks:
         copy.start()
-    for copy in copies:
+    fetch[1].wait()
+    fetch[2].wait()
+    white_ref[...] = dot3(split(panel[...]), split(inverse[...]))
+    for copy in picks:
         copy.wait()
 
 
-def pick(row_tiles, sep_inverse, slots):
+def first(row_tiles, sep_inverse, panel_rows, diag_inverse):
+    slots = panel_rows.shape[0] // TILE
     return pl.pallas_call(
-        pick_kernel,
-        out_shape=f32(slots * TILE, slots * TILE),
-        in_specs=[SMEM, ANY],
-        out_specs=ANY,
-        scratch_shapes=[pltpu.SemaphoreType.DMA((slots * slots,))],
-        compiler_params=PARAMS,
-    )(row_tiles, sep_inverse)
-
-
-def quarter_kernel(panel_ref, inverse_ref, out_ref):
-    member = lax.axis_index(("col", "rep"))
-    columns = pl.ds(pl.multiple_of(member * TILE, TILE), TILE)
-    out_ref[...] = dot3(split(panel_ref[...]), split(inverse_ref[:, columns]))
-
-
-def white_quarter(panel_rows, diag_inverse):
-    return pl.pallas_call(
-        quarter_kernel,
-        out_shape=f32(panel_rows.shape[0], TILE),
-        in_specs=[VMEM, VMEM],
-        out_specs=VMEM,
-        compiler_params=PARAMS,
-    )(panel_rows, diag_inverse)
-
-
-def whiten_kernel(panel_ref, inverse_ref, high_ref, low_ref, base_ref):
+        first_kernel,
+        out_shape=(f32(panel_rows.shape[0], TILE), f32(slots * TILE, slots * TILE)),
+        in_specs=[ANY] * 4,
+        out_specs=(VMEM, VMEM),
+        scratch_shapes=[
+            pltpu.SMEM(row_tiles.shape, jnp.int32),
+            pltpu.VMEM(panel_rows.shape, jnp.float32),
+            pltpu.VMEM((diag_inverse.shape[0], TILE), jnp.float32),
+            pltpu.SemaphoreType.DMA((3 + slots * slots,)),
+        ],
+    )(row_tiles, sep_inverse, panel_rows, diag_inverse)
+
+
+def whiten_kernel(*refs):
+    panel_ref, inverse_ref, quarter_ref, own_ref, near_ref = refs[:5]
+    high_ref, low_ref, base_ref, quarter_out, own_high, own_low, near_high, near_low = refs[5:]
     member = lax.axis_index(("col", "rep"))
     columns = pl.ds(pl.multiple_of(member * TILE, TILE), TILE)
     inverse = split(inverse_ref[...])
-    high, low = split(dot3(split(panel_ref[...]), inverse))
-    high_ref[...] = high
-    low_ref[...] = low
+    high_ref[...], low_ref[...] = split(dot3(split(panel_ref[...]), inverse))
     base_ref[...] = dot3(split(inverse_ref[:, columns].T), inverse)
-
-
-def whiten(panel_rows, diag_inverse):
-    shape = jax.ShapeDtypeStruct(panel_rows.shape, jnp.bfloat16)
-    return pl.pallas_call(
+    quarter_out[:, :TILE], quarter_out[:, TILE:] = split(quarter_ref[...])
+    own_high[...], own_low[...] = split(own_ref[...])
+    near_high[...], near_low[...] = split(near_ref[...])
+
+
+def whiten(panel_rows, diag_inverse, quarter, own, near):
+    def part(*shape):
+        return jax.ShapeDtypeStruct(shape, jnp.bfloat16)
+
+    white, sep = part(*panel_rows.shape), part(*own.shape)
+    out = pl.pallas_call(
         whiten_kernel,
-        out_shape=(shape, shape, f32(TILE, diag_inverse.shape[1])),
-        in_specs=[VMEM, VMEM],
-        out_specs=(VMEM,) * 3,
+        out_shape=(
+            white,
+            white,
+            f32(TILE, diag_inverse.shape[1]),
+            part(quarter.shape[0], 2 * TILE),
+            *[sep] * 4,
+        ),
+        in_specs=[VMEM] * 5,
+        out_specs=(VMEM,) * 8,
         compiler_params=PARAMS,
-    )(panel_rows, diag_inverse)
+    )(panel_rows, diag_inverse, quarter, own, near)
+    return out[:2], out[2], out[3], out[4:]
 
 
 def product_kernel(*refs):
-    seps, whites, (own_high, own_low) = refs[0:4], refs[4:8], refs[8:10]
-    terms, pieces = refs[10:14], refs[14:18]
-    white_high, white_low, product = refs[18:21]
+    count = len(refs) - 21
+    own_high, own_low, near_high, near_low, across, quarter = refs[:6]
+    far, whites, (white_high, white_low) = refs[6 : 6 + count], refs[6 + count : 9 + count], refs[9 + count : 11 + count]
+    terms, pieces, (joined, product) = refs[-10:-6], refs[-6:-2], refs[-2:]
     row, member = lax.axis_index("row"), lax.axis_index(("col", "rep"))
-    for j in range(4):
-        high, low = split(whites[j][...])
-        white_high[row ^ j] = high
-        white_low[row ^ j] = low
-    total = None
-    for i in range(4):
-        term = dot3(split(seps[i][...]), (white_high[member ^ i], white_low[member ^ i]))
-        total = term if total is None else total + term
-    product[...] = -total
-    flipped = split(total.T)
-    count = pieces[0].shape[0]
+    joined[row] = quarter[...]
+    for j, ref in zip(ORDER, whites):
+        joined[row ^ j, :, :TILE], joined[row ^ j, :, TILE:] = split(ref[...])
+
+    def times(high, low, i):
+        wide = dot(high, joined[member ^ i])
+        return wide[:, :TILE] + (wide[:, TILE:] + dot(low, joined[member ^ i, :, :TILE]))
+
+    total = times(own_high[...], own_low[...], 0) + times(near_high[...], near_low[...], 1)
+    total += times(*split(across[...]), 2)
+    depth = far[0].shape[0]
+    for n, ref in enumerate(far):
+        rows = slice(n * depth, (n + 1) * depth)
+        product[rows, :] = -(total[rows, :] + times(*split(ref[...]), 3))
+    flipped = split(-product[...].T)
+    depth = pieces[0].shape[0]
     for j in range(4):
         columns = pl.ds(pl.multiple_of((row ^ j) * TILE, TILE), TILE)
-        terms[j][...] = dot3(flipped, (own_high[:, columns], own_low[:, columns]))
-        pieces[j][...] = product[pl.ds(pl.multiple_of((member ^ j) * count, 8), count), :]
-
-
-def products(seps, whites, own_white):
+        terms[j][...] = dot3(flipped, (white_high[:, columns], white_low[:, columns]))
+        pieces[j][...] = product[pl.ds(pl.multiple_of((member ^ j) * depth, 8), depth), :]
+
+
+def products(seps, across, quarter, far, whites, own_white):
     depth, width = whites[0].shape
     return pl.pallas_call(
         product_kernel,
         out_shape=(f32(width, TILE),) * 4 + (f32(depth // 4, width),) * 4,
-        in_specs=[VMEM] * 10,
+        in_specs=[VMEM] * (11 + len(far)),
         out_specs=(VMEM,) * 8,
         scratch_shapes=[
-            pltpu.VMEM((4, depth, width), jnp.bfloat16),
-            pltpu.VMEM((4, depth, width), jnp.bfloat16),
+            pltpu.VMEM((4, depth, 2 * width), jnp.bfloat16),
             pltpu.VMEM((depth, width), jnp.float32),
         ],
         compiler_params=PARAMS,
-    )(*seps, *whites, *own_white)
+    )(*seps, across, quarter, *far, *whites, *own_white)
 
 
 def rows_kernel(own, near, across, far, out_ref):
@@ -212,9 +234,9 @@
     )(*pieces)
 
 
-def diagonal_kernel(own, one, two, three, base_ref, out_ref, variances_ref):
+def diagonal_kernel(own, first, second, third, base_ref, out_ref, variances_ref):
     row, member = lax.axis_index("row"), lax.axis_index(("col", "rep"))
-    for j, ref in enumerate((own, one, two, three)):
+    for j, ref in zip((0,) + (2, 3, 1), (own, first, second, third)):
         columns = pl.ds(pl.multiple_of((row ^ j) * TILE, TILE), TILE)
         out_ref[:, columns] = base_ref[:, columns] + ref[...]
     square = out_ref[:, pl.ds(pl.multiple_of(member * TILE, TILE), TILE)]
@@ -241,32 +263,33 @@
 
 
 def four_by_four(sep_inverse, row_tiles, panel_rows, diag_inverse):
-    quarter = white_quarter(panel_rows, diag_inverse)
-    whites = [quarter] + [lax.ppermute(quarter, "row", rows_apart(j)) for j in (1, 2, 3)]
-
-    own = pick(row_tiles, sep_inverse, panel_rows.shape[0] // TILE)
+    quarter, own = first(row_tiles, sep_inverse, panel_rows, diag_inverse)
+    across = lax.ppermute(own, "col", SWAP)
     near = lax.ppermute(own, "rep", SWAP)
-    across = lax.ppermute(own, "col", SWAP)
-    far = lax.ppermute(across, "rep", SWAP)
-
-    *own_white, base = whiten(panel_rows, diag_inverse)
-    out = products((own, near, across, far), whites, own_white)
+    whites = {j: lax.ppermute(quarter, "row", rows_apart(j)) for j in (2, 1)}
+    whites[3] = lax.ppermute(whites[2], "row", rows_apart(1))
+    own_white, base, split_quarter, seps = whiten(panel_rows, diag_inverse, quarter, own, near)
+    across, own_white, base = lax.optimization_barrier((across, own_white, base))
+    count = across.shape[0] // 3
+    far = [
+        lax.ppermute(lax.slice_in_dim(across, i * count, (i + 1) * count), "rep", SWAP)
+        for i in range(3)
+    ]
+    out = products(seps, across, split_quarter, far, [whites[j] for j in ORDER], own_white)
     terms, pieces = out[:4], out[4:]
-
-    block = terms[0]
-    for j in (1, 2, 3):
-        block = block + lax.ppermute(terms[j], "row", rows_apart(j))
-    blocks = [block] + [lax.ppermute(block, "row", rows_apart(j)) for j in (1, 2, 3)]
+    got = [lax.ppermute(terms[j], "row", rows_apart(j)) for j in (2, 1, 3)]
+    mine = [
+        pieces[0],
+        lax.ppermute(pieces[1], "rep", SWAP),
+        lax.ppermute(pieces[2], "col", SWAP),
+        lax.ppermute(pieces[3], ("col", "rep"), rows_apart(3)),
+    ]
+    got, mine = lax.optimization_barrier((got, mine))
+    block = terms[0] + got[0] + got[1] + got[2]
+    blocks = [block] + [lax.ppermute(block, "row", rows_apart(j)) for j in (2, 3, 1)]
+    sigma_rows = rows_of(mine)
+    blocks, sigma_rows = lax.optimization_barrier((blocks, sigma_rows))
     sigma_diag, variances = diagonal(blocks, base)
-
-    sigma_rows = rows_of(
-        [
-            pieces[0],
-            lax.ppermute(pieces[1], "rep", SWAP),
-            lax.ppermute(pieces[2], "col", SWAP),
-            lax.ppermute(pieces[3], ("col", "rep"), rows_apart(3)),
-        ]
-    )
     return sigma_rows, sigma_diag, variances.reshape(-1)
 
 

time: 64.2 us -> 47 us (0.73)
  waiting for transfers between devices: 37.5 us -> 18.4 us
  Pallas kernels: 5.45 us -> 7.21 us
    ppermute x1, waiting for transfers between devices: 13.3 us -> 0.01 us  [four_by_four(): across = lax.ppermute(own, 'col', SWAP)]
    ppermute x7 -> x9, waiting for transfers between devices: 20.5 us -> 10.4 us  [the longest x2 8.24 us: four_by_four(): whites = {j: lax.ppermute(quarter, 'row', rows_apart(j)) for j in (2, 1)}]
    ppermute x3, waiting for transfers between devices: 0.01 us -> 4.58 us  [four_by_four(): lax.ppermute(block, 'row', rows_apart(j))]
    pallas_call x3 -> x2, Pallas kernels: 2.23 us -> 4.19 us  [the longest x1 2.94 us: first(): pl.pallas_call(first_kernel, out_shape=(f32(panel_rows.shape[0], TILE), f...]
    ppermute x7 -> x9, starting transfers between devices: 9.01 us -> 10.2 us  [the longest x3 4.68 us: four_by_four(): got = [lax.ppermute(terms[j], 'row', rows_apart(j)) for j in (2, 1, 3)]]
    ppermute x1, waiting for transfers between devices: 1.05 us -> 0.01 us  [four_by_four(): lax.ppermute(pieces[3], ('col', 'rep'), rows_apart(3))]
    ppermute x1, starting transfers between devices: 1.49 us -> 0.53 us  [four_by_four(): lax.ppermute(pieces[2], 'col', SWAP)]
    ppermute x1, waiting for transfers between devices: 2.6 us -> 3.43 us  [four_by_four(): lax.ppermute(pieces[2], 'col', SWAP)]
  transfers between devices with their start and end apart: 15 -> 17, of which waited for: 8 -> 7; matrix products, arithmetic and copies ran while one was open for 0% -> 0% of each run, Pallas kernels for 3% -> 4%
where the time goes in v2:
time: 47 us; the launch traced here: 46.8 us
  starting transfers between devices  18.4 us (39%)
  waiting for transfers between devices  18.4 us (39%)
  Pallas kernels  7.21 us (15%)
  local copies, waits for them, and re-layouts  2.03 us (4%)
  between operations  0.73 us (2%)
    ppermute x2, waiting for transfers between devices, four_by_four(): whites = {j: lax.ppermute(quarter, 'row', rows_apart(j)) for j in (2, 1)}  8.24 us
    ppermute x3, starting transfers between devices, four_by_four(): got = [lax.ppermute(terms[j], 'row', rows_apart(j)) for j in (2, 1, 3)]  4.68 us
    ppermute x3, waiting for transfers between devices, four_by_four(): lax.ppermute(block, 'row', rows_apart(j))  4.58 us
    ppermute x2, starting transfers between devices, four_by_four(): whites = {j: lax.ppermute(quarter, 'row', rows_apart(j)) for j in (2, 1)}  4.17 us
    ppermute x3, starting transfers between devices, four_by_four(): lax.ppermute(block, 'row', rows_apart(j))  3.75 us
    ppermute x1, waiting for transfers between devices, four_by_four(): lax.ppermute(pieces[2], 'col', SWAP)  3.43 us
    pallas_call x1, Pallas kernels, first(): pl.pallas_call(first_kernel, out_shape=(f32(panel_rows.shape[0], TILE), f...  2.94 us
    ppermute x1, starting transfers between devices, four_by_four(): across = lax.ppermute(own, 'col', SWAP)  2.56 us
  transfers between devices with their start and end apart: 17, of which 7 were waited for; matrix products, arithmetic and copies ran while one was open for 0% of the time, Pallas kernels for 4%

profile of v2, /device:TPU:0, one launch (start us, length us, event | category | flops | bytes accessed | tf_op | source)
XLA Modules:
  0.0 46.8 jit_solution(5850540689145425923)
XLA Ops:
  0.7 2.9 %shard_map.67 = (f32[384,128]{1,0:T(8,128)}, f32[384,384]{1,0:T(8,128)}) custom-call(s32[12]{0:T(128)} %tiles_hbm.1, f32[768,768]{1,0:T(8,128)} %sep_hbm.1, f32[384,512]{1,0:T(8,128)} %refs_0_.1, f32[512,512]{1,0:T(8,128)} %refs_1_.1), custom_call_target="tpu_custom_call" | custom-call | tf_op jit(solution)/shard_map/pallas_call | solution.py:129
  3.6 0.5 %collective-permute-start = (f32[384,384]{1,0:T(8,128)}, f32[384,384]{1,0:T(8,128)S(1)}, u32[]{:S(2)}, u32[]{:S(2)}) collective-permute-start(f32[384,384]{1,0:T(8,128)} %get-tuple-element.40.refs_3_), channel_id=1, source_target_pairs={{0,1},{1,0},{2,3},{3,2},{4,5},{5,4},{6,7},{7,6},{8,9},{9,8},{10,11... | collective-permute-start | bytes 1769480 | tf_op jit(solution)/shard_map/ppermute | solution.py:268
  4.1 2.6 %collective-permute-start.1 = (f32[384,384]{1,0:T(8,128)}, f32[384,384]{1,0:T(8,128)S(1)}, u32[]{:S(2)}, u32[]{:S(2)}) collective-permute-start(f32[384,384]{1,0:T(8,128)} %get-tuple-element.40.refs_3_), channel_id=1, source_target_pairs={{0,2},{2,0},{1,3},{3,1},{4,6},{6,4},{5,7},{7,5},{8,10},{10,8},{9,1... | collective-permute-start | bytes 1769480 | tf_op jit(solution)/shard_map/ppermute | solution.py:267
  6.7 2.6 %collective-permute-start.5 = (f32[384,128]{1,0:T(8,128)}, f32[384,128]{1,0:T(8,128)S(1)}, u32[]{:S(2)}, u32[]{:S(2)}) collective-permute-start(f32[384,128]{1,0:T(8,128)} %get-tuple-element.39.refs_2_), channel_id=1, source_target_pairs={{0,8},{4,12},{8,0},{12,4},{1,9},{5,13},{9,1},{13,5},{2,10},{6,14},... | collective-permute-start | bytes 589832 | tf_op jit(solution)/shard_map/ppermute | solution.py:269
  9.3 1.6 %collective-permute-start.7 = (f32[384,128]{1,0:T(8,128)}, f32[384,128]{1,0:T(8,128)S(1)}, u32[]{:S(2)}, u32[]{:S(2)}) collective-permute-start(f32[384,128]{1,0:T(8,128)} %get-tuple-element.39.refs_2_), channel_id=1, source_target_pairs={{0,4},{4,0},{8,12},{12,8},{1,5},{5,1},{9,13},{13,9},{2,6},{6,2},{1... | collective-permute-start | bytes 589832 | tf_op jit(solution)/shard_map/ppermute | solution.py:269
  10.9 8.2 %collective-permute-done.5.refs_9_ = f32[384,128]{1,0:T(8,128)S(1)} collective-permute-done((f32[384,128]{1,0:T(8,128)}, f32[384,128]{1,0:T(8,128)S(1)}, u32[]{:S(2)}, u32[]{:S(2)}) %collective-permute-start.5) | collective-permute-done | bytes 196640 | tf_op jit(solution)/shard_map/ppermute | solution.py:269
  19.1 0.7 %collective-permute-start.6 = (f32[384,128]{1,0:T(8,128)S(1)}, f32[384,128]{1,0:T(8,128)S(1)}, u32[]{:S(2)}, u32[]{:S(2)}) collective-permute-start(f32[384,128]{1,0:T(8,128)S(1)} %collective-permute-done.5.refs_9_), channel_id=1, source_target_pairs={{0,4},{4,0},{8,12},{12,8},{1,5},{5,1},{9,13},{13,9},{2,6},{6,2},{1... | collective-permute-start | bytes 589832 | tf_op jit(solution)/shard_map/ppermute | solution.py:270
  19.8 1.1 %copy-done.2 = f32[384,384]{1,0:T(8,128)S(1)} copy-done((f32[384,384]{1,0:T(8,128)S(1)}, f32[384,384]{1,0:T(8,128)}, u32[]{:S(2)}) %copy-start.2) | copy-done | bytes 589848
  20.8 0.9 %copy-done.3 = f32[384,128]{1,0:T(8,128)S(1)} copy-done((f32[384,128]{1,0:T(8,128)S(1)}, f32[384,128]{1,0:T(8,128)}, u32[]{:S(2)}) %copy-start.3) | copy-done | bytes 196632
  21.8 1.2 %shard_map.68 = (bf16[384,512]{1,0:T(8,128)(2,1)S(1)}, bf16[384,512]{1,0:T(8,128)(2,1)S(1)}, f32[128,512]{1,0:T(8,128)S(1)}, bf16[384,256]{1,0:T(8,128)(2,1)S(1)...) custom-call(f32[384,512]{1,0:T(8,128)S(1)} %copy-done.1, ...), custom_call_target="tpu_custom_call" | custom-call | tf_op jit(solution)/shard_map/pallas_call | solution.py:161
  23.7 1.4 %collective-permute-done.6.refs_10_ = f32[384,128]{1,0:T(8,128)S(1)} collective-permute-done((f32[384,128]{1,0:T(8,128)S(1)}, f32[384,128]{1,0:T(8,128)S(1)}, u32[]{:S(2)}, u32[]{:S(2)}) %collective-permute-start.6) | collective-permute-done | bytes 196640 | tf_op jit(solution)/shard_map/ppermute | solution.py:270
  25.2 1.6 %shard_map.69 = (f32[128,128]{1,0:T(8,128)S(1)}, f32[128,128]{1,0:T(8,128)S(1)}, f32[128,128]{1,0:T(8,128)S(1)}, f32[128,128]{1,0:T(8,128)S(1)}, f32[96,128]{1,0...) custom-call(bf16[384,384]{1,0:T(8,128)(2,1)S(1)} %get-tuple-element.41.refs_0_, ...), custom_call_target="tpu_custom_call" | custom-call | tf_op jit(solution)/shard_map/pallas_call | solution.py:207
  27.0 4.0 %collective-permute-start.10 = (f32[128,128]{1,0:T(8,128)S(1)}, f32[128,128]{1,0:T(8,128)S(1)}, u32[]{:S(2)}, u32[]{:S(2)}) collective-permute-start(f32[128,128]{1,0:T(8,128)S(1)} %get-tuple-element.55), channel_id=1, source_target_pairs={{0,12},{4,8},{8,4},{12,0},{1,13},{5,9},{9,5},{13,1},{2,14},{6,10},... | collective-permute-start | bytes 196616 | tf_op jit(solution)/shard_map/ppermute | solution.py:280
  31.0 0.6 %collective-permute-start.9 = (f32[128,128]{1,0:T(8,128)S(1)}, f32[128,128]{1,0:T(8,128)S(1)}, u32[]{:S(2)}, u32[]{:S(2)}) collective-permute-start(f32[128,128]{1,0:T(8,128)S(1)} %get-tuple-element.54), channel_id=1, source_target_pairs={{0,4},{4,0},{8,12},{12,8},{1,5},{5,1},{9,13},{13,9},{2,6},{6,2},{1... | collective-permute-start | bytes 196616 | tf_op jit(solution)/shard_map/ppermute | solution.py:280
  31.7 0.5 %collective-permute-start.12 = (f32[96,128]{1,0:T(8,128)S(1)}, f32[96,128]{1,0:T(8,128)S(1)}, u32[]{:S(2)}, u32[]{:S(2)}) collective-permute-start(f32[96,128]{1,0:T(8,128)S(1)} %get-tuple-element.58), channel_id=1, source_target_pairs={{0,2},{2,0},{1,3},{3,1},{4,6},{6,4},{5,7},{7,5},{8,10},{10,8},{9,1... | collective-permute-start | bytes 147464 | tf_op jit(solution)/shard_map/ppermute | solution.py:284
  32.2 0.6 %collective-permute-start.13 = (f32[96,128]{1,0:T(8,128)S(1)}, f32[96,128]{1,0:T(8,128)S(1)}, u32[]{:S(2)}, u32[]{:S(2)}) collective-permute-start(f32[96,128]{1,0:T(8,128)S(1)} %get-tuple-element.59), channel_id=1, source_target_pairs={{0,3},{1,2},{2,1},{3,0},{4,7},{5,6},{6,5},{7,4},{8,11},{9,10},{10,... | collective-permute-start | bytes 147464 | tf_op jit(solution)/shard_map/ppermute | solution.py:285
  32.8 3.4 %collective-permute-done.12.across = f32[96,128]{1,0:T(8,128)S(1)} collective-permute-done((f32[96,128]{1,0:T(8,128)S(1)}, f32[96,128]{1,0:T(8,128)S(1)}, u32[]{:S(2)}, u32[]{:S(2)}) %collective-permute-start.12) | collective-permute-done | bytes 49184 | tf_op jit(solution)/shard_map/ppermute | solution.py:284
  36.3 0.7 %collective-permute-done.8 = f32[128,128]{1,0:T(8,128)S(1)} collective-permute-done((f32[128,128]{1,0:T(8,128)S(1)}, f32[128,128]{1,0:T(8,128)S(1)}, u32[]{:S(2)}, u32[]{:S(2)}) %collective-permute-start.8) | collective-permute-done | bytes 65568 | tf_op jit(solution)/shard_map/ppermute | solution.py:280
  37.0 1.6 %collective-permute-start.14 = (f32[128,128]{1,0:T(8,128)S(1)}, f32[128,128]{1,0:T(8,128)S(1)}, u32[]{:S(2)}, u32[]{:S(2)}) collective-permute-start(f32[128,128]{1,0:T(8,128)S(1)} %add_add_fusion.own), channel_id=1, source_target_pairs={{0,8},{4,12},{8,0},{12,4},{1,9},{5,13},{9,1},{13,5},{2,10},{6,14},... | collective-permute-start | bytes 196616 | tf_op jit(solution)/shard_map/ppermute | solution.py:289
  38.7 2.1 %collective-permute-start.15 = (f32[128,128]{1,0:T(8,128)S(1)}, f32[128,128]{1,0:T(8,128)S(1)}, u32[]{:S(2)}, u32[]{:S(2)}) collective-permute-start(f32[128,128]{1,0:T(8,128)S(1)} %add_add_fusion.own), channel_id=1, source_target_pairs={{0,12},{4,8},{8,4},{12,0},{1,13},{5,9},{9,5},{13,1},{2,14},{6,10},... | collective-permute-start | bytes 196616 | tf_op jit(solution)/shard_map/ppermute | solution.py:289
  40.8 0.7 %shard_map.70 = f32[96,512]{1,0:T(8,128)} custom-call(f32[96,128]{1,0:T(8,128)S(1)} %get-tuple-element.63.own, f32[96,128]{1,0:T(8,128)S(1)} %collective-permute-done.11.near, f32[96,128]{1,0:T(8,128)S(1)} %collective-permute-done.12.across, f32[96,128]{1,0:T(8,128)S(1)} %collective-permute-done.13.far), custom_call_target="tpu_custom_call" | custom-call | tf_op jit(solution)/shard_map/pallas_call | solution.py:228
  41.5 3.6 %collective-permute-done.14.first = f32[128,128]{1,0:T(8,128)S(1)} collective-permute-done((f32[128,128]{1,0:T(8,128)S(1)}, f32[128,128]{1,0:T(8,128)S(1)}, u32[]{:S(2)}, u32[]{:S(2)}) %collective-permute-start.14) | collective-permute-done | bytes 65568 | tf_op jit(solution)/shard_map/ppermute | solution.py:289
  45.4 0.7 %collective-permute-done.16.third = f32[128,128]{1,0:T(8,128)S(1)} collective-permute-done((f32[128,128]{1,0:T(8,128)S(1)}, f32[128,128]{1,0:T(8,128)S(1)}, u32[]{:S(2)}, u32[]{:S(2)}) %collective-permute-start.16) | collective-permute-done | bytes 65568 | tf_op jit(solution)/shard_map/ppermute | solution.py:289
  46.1 0.8 %shard_map.71 = (f32[128,512]{1,0:T(8,128)}, f32[1,128]{1,0:T(1,128)}) custom-call(f32[128,128]{1,0:T(8,128)S(1)} %add_add_fusion.own, f32[128,128]{1,0:T(8,128)S(1)} %collective-permute-done.14.first, f32[128,128]{1,0:T(8,128)S(1)} %collective-permute-done.15.second, f32[128,128]{1,0:T(8,128)S(1)} %collective-permute-done.16.third, ...), custom_call_target="tpu_custom_call" | custom-call | tf_op jit(solution)/shard_map/pallas_call | solution.py:249
  (25 shorter events, 1.3 us)
Async XLA Ops:
  0.6 19.1 %copy-start.1 = (f32[384,512]{1,0:T(8,128)S(1)}, f32[384,512]{1,0:T(8,128)}, u32[]{:S(2)}) copy-start(f32[384,512]{1,0:T(8,128)} %refs_0_.1) | copy-start | bytes 2359300
  0.6 19.1 %copy-start = (f32[512,512]{1,0:T(8,128)S(1)}, f32[512,512]{1,0:T(8,128)}, u32[]{:S(2)}) copy-start(f32[512,512]{1,0:T(8,128)} %refs_1_.1) | copy-start | bytes 3145732
  3.6 16.2 %collective-permute-start = (f32[384,384]{1,0:T(8,128)}, f32[384,384]{1,0:T(8,128)S(1)}, u32[]{:S(2)}, u32[]{:S(2)}) collective-permute-start(f32[384,384]{1,0:T(8,128)} %get-tuple-element.40.refs_3_), channel_id=1, source_target_pairs={{0,1},{1,0},{2,3},{3,2},{4,5},{5,4},{6,7},{7,6},{8,9},{9,8},{10,11... | collective-permute-start | bytes 1769480 | tf_op jit(solution)/shard_map/ppermute | solution.py:268
  4.1 18.9 %collective-permute-start.1 = (f32[384,384]{1,0:T(8,128)}, f32[384,384]{1,0:T(8,128)S(1)}, u32[]{:S(2)}, u32[]{:S(2)}) collective-permute-start(f32[384,384]{1,0:T(8,128)} %get-tuple-element.40.refs_3_), channel_id=1, source_target_pairs={{0,2},{2,0},{1,3},{3,1},{4,6},{6,4},{5,7},{7,5},{8,10},{10,8},{9,1... | collective-permute-start | bytes 1769480 | tf_op jit(solution)/shard_map/ppermute | solution.py:267
  6.7 12.4 %collective-permute-start.5 = (f32[384,128]{1,0:T(8,128)}, f32[384,128]{1,0:T(8,128)S(1)}, u32[]{:S(2)}, u32[]{:S(2)}) collective-permute-start(f32[384,128]{1,0:T(8,128)} %get-tuple-element.39.refs_2_), channel_id=1, source_target_pairs={{0,8},{4,12},{8,0},{12,4},{1,9},{5,13},{9,1},{13,5},{2,10},{6,14},... | collective-permute-start | bytes 589832 | tf_op jit(solution)/shard_map/ppermute | solution.py:269
  9.3 14.5 %collective-permute-start.7 = (f32[384,128]{1,0:T(8,128)}, f32[384,128]{1,0:T(8,128)S(1)}, u32[]{:S(2)}, u32[]{:S(2)}) collective-permute-start(f32[384,128]{1,0:T(8,128)} %get-tuple-element.39.refs_2_), channel_id=1, source_target_pairs={{0,4},{4,0},{8,12},{12,8},{1,5},{5,1},{9,13},{13,9},{2,6},{6,2},{1... | collective-permute-start | bytes 589832 | tf_op jit(solution)/shard_map/ppermute | solution.py:269
  19.1 6.1 %collective-permute-start.6 = (f32[384,128]{1,0:T(8,128)S(1)}, f32[384,128]{1,0:T(8,128)S(1)}, u32[]{:S(2)}, u32[]{:S(2)}) collective-permute-start(f32[384,128]{1,0:T(8,128)S(1)} %collective-permute-done.5.refs_9_), channel_id=1, source_target_pairs={{0,4},{4,0},{8,12},{12,8},{1,5},{5,1},{9,13},{13,9},{2,6},{6,2},{1... | collective-permute-start | bytes 589832 | tf_op jit(solution)/shard_map/ppermute | solution.py:270
  19.8 1.1 %copy-start.2 = (f32[384,384]{1,0:T(8,128)S(1)}, f32[384,384]{1,0:T(8,128)}, u32[]{:S(2)}) copy-start(f32[384,384]{1,0:T(8,128)} %get-tuple-element.40.refs_3_) | copy-start | bytes 1769476
  20.8 0.9 %copy-start.3 = (f32[384,128]{1,0:T(8,128)S(1)}, f32[384,128]{1,0:T(8,128)}, u32[]{:S(2)}) copy-start(f32[384,128]{1,0:T(8,128)} %get-tuple-element.39.refs_2_) | copy-start | bytes 589828
  23.1 2.1 %collective-permute-start.2 = (f32[128,384]{1,0:T(8,128)S(1)}, f32[128,384]{1,0:T(8,128)S(1)}, u32[]{:S(2)}, u32[]{:S(2)}) collective-permute-start(f32[128,384]{1,0:T(8,128)S(1)} %get-tuple-element.77), channel_id=1, source_target_pairs={{0,1},{1,0},{2,3},{3,2},{4,5},{5,4},{6,7},{7,6},{8,9},{9,8},{10,11... | collective-permute-start | bytes 589832 | tf_op jit(solution)/shard_map/ppermute | solution.py:275
  23.2 2.0 %collective-permute-start.3 = (f32[128,384]{1,0:T(8,128)S(1)}, f32[128,384]{1,0:T(8,128)S(1)}, u32[]{:S(2)}, u32[]{:S(2)}) collective-permute-start(f32[128,384]{1,0:T(8,128)S(1)} %get-tuple-element.76), channel_id=1, source_target_pairs={{0,1},{1,0},{2,3},{3,2},{4,5},{5,4},{6,7},{7,6},{8,9},{9,8},{10,11... | collective-permute-start | bytes 589832 | tf_op jit(solution)/shard_map/ppermute | solution.py:275
  23.7 1.5 %collective-permute-start.4 = (f32[128,384]{1,0:T(8,128)S(1)}, f32[128,384]{1,0:T(8,128)S(1)}, u32[]{:S(2)}, u32[]{:S(2)}) collective-permute-start(f32[128,384]{1,0:T(8,128)S(1)} %get-tuple-element.75), channel_id=1, source_target_pairs={{0,1},{1,0},{2,3},{3,2},{4,5},{5,4},{6,7},{7,6},{8,9},{9,8},{10,11... | collective-permute-start | bytes 589832 | tf_op jit(solution)/shard_map/ppermute | solution.py:275
  26.8 5.5 %collective-permute-start.11 = (f32[96,128]{1,0:T(8,128)S(1)}, f32[96,128]{1,0:T(8,128)S(1)}, u32[]{:S(2)}, u32[]{:S(2)}) collective-permute-start(f32[96,128]{1,0:T(8,128)S(1)} %get-tuple-element.57), channel_id=1, source_target_pairs={{0,1},{1,0},{2,3},{3,2},{4,5},{5,4},{6,7},{7,6},{8,9},{9,8},{10,11... | collective-permute-start | bytes 147464 | tf_op jit(solution)/shard_map/ppermute | solution.py:283
  27.0 9.3 %collective-permute-start.10 = (f32[128,128]{1,0:T(8,128)S(1)}, f32[128,128]{1,0:T(8,128)S(1)}, u32[]{:S(2)}, u32[]{:S(2)}) collective-permute-start(f32[128,128]{1,0:T(8,128)S(1)} %get-tuple-element.55), channel_id=1, source_target_pairs={{0,12},{4,8},{8,4},{12,0},{1,13},{5,9},{9,5},{13,1},{2,14},{6,10},... | collective-permute-start | bytes 196616 | tf_op jit(solution)/shard_map/ppermute | solution.py:280
  31.0 6.0 %collective-permute-start.8 = (f32[128,128]{1,0:T(8,128)S(1)}, f32[128,128]{1,0:T(8,128)S(1)}, u32[]{:S(2)}, u32[]{:S(2)}) collective-permute-start(f32[128,128]{1,0:T(8,128)S(1)} %get-tuple-element.53), channel_id=1, source_target_pairs={{0,8},{4,12},{8,0},{12,4},{1,9},{5,13},{9,1},{13,5},{2,10},{6,14},... | collective-permute-start | bytes 196616 | tf_op jit(solution)/shard_map/ppermute | solution.py:280
  31.0 6.0 %collective-permute-start.9 = (f32[128,128]{1,0:T(8,128)S(1)}, f32[128,128]{1,0:T(8,128)S(1)}, u32[]{:S(2)}, u32[]{:S(2)}) collective-permute-start(f32[128,128]{1,0:T(8,128)S(1)} %get-tuple-element.54), channel_id=1, source_target_pairs={{0,4},{4,0},{8,12},{12,8},{1,5},{5,1},{9,13},{13,9},{2,6},{6,2},{1... | collective-permute-start | bytes 196616 | tf_op jit(solution)/shard_map/ppermute | solution.py:280
  31.7 4.6 %collective-permute-start.12 = (f32[96,128]{1,0:T(8,128)S(1)}, f32[96,128]{1,0:T(8,128)S(1)}, u32[]{:S(2)}, u32[]{:S(2)}) collective-permute-start(f32[96,128]{1,0:T(8,128)S(1)} %get-tuple-element.58), channel_id=1, source_target_pairs={{0,2},{2,0},{1,3},{3,1},{4,6},{6,4},{5,7},{7,5},{8,10},{10,8},{9,1... | collective-permute-start | bytes 147464 | tf_op jit(solution)/shard_map/ppermute | solution.py:284
  32.2 4.0 %collective-permute-start.13 = (f32[96,128]{1,0:T(8,128)S(1)}, f32[96,128]{1,0:T(8,128)S(1)}, u32[]{:S(2)}, u32[]{:S(2)}) collective-permute-start(f32[96,128]{1,0:T(8,128)S(1)} %get-tuple-element.59), channel_id=1, source_target_pairs={{0,3},{1,2},{2,1},{3,0},{4,7},{5,6},{6,5},{7,4},{8,11},{9,10},{10,... | collective-permute-start | bytes 147464 | tf_op jit(solution)/shard_map/ppermute | solution.py:285
  37.0 8.0 %collective-permute-start.14 = (f32[128,128]{1,0:T(8,128)S(1)}, f32[128,128]{1,0:T(8,128)S(1)}, u32[]{:S(2)}, u32[]{:S(2)}) collective-permute-start(f32[128,128]{1,0:T(8,128)S(1)} %add_add_fusion.own), channel_id=1, source_target_pairs={{0,8},{4,12},{8,0},{12,4},{1,9},{5,13},{9,1},{13,5},{2,10},{6,14},... | collective-permute-start | bytes 196616 | tf_op jit(solution)/shard_map/ppermute | solution.py:289
  38.7 6.7 %collective-permute-start.15 = (f32[128,128]{1,0:T(8,128)S(1)}, f32[128,128]{1,0:T(8,128)S(1)}, u32[]{:S(2)}, u32[]{:S(2)}) collective-permute-start(f32[128,128]{1,0:T(8,128)S(1)} %add_add_fusion.own), channel_id=1, source_target_pairs={{0,12},{4,8},{8,4},{12,0},{1,13},{5,9},{9,5},{13,1},{2,14},{6,10},... | collective-permute-start | bytes 196616 | tf_op jit(solution)/shard_map/ppermute | solution.py:289
  40.8 5.3 %collective-permute-start.16 = (f32[128,128]{1,0:T(8,128)S(1)}, f32[128,128]{1,0:T(8,128)S(1)}, u32[]{:S(2)}, u32[]{:S(2)}) collective-permute-start(f32[128,128]{1,0:T(8,128)S(1)} %add_add_fusion.own), channel_id=1, source_target_pairs={{0,4},{4,0},{8,12},{12,8},{1,5},{5,1},{9,13},{13,9},{2,6},{6,2},{1... | collective-permute-start | bytes 196616 | tf_op jit(solution)/shard_map/ppermute | solution.py:289

commit v3 on v2

--- a/solution.py
+++ b/solution.py
@@ -175,10 +175,10 @@
 
 
 def product_kernel(*refs):
-    count = len(refs) - 21
+    count = len(refs) - 19
     own_high, own_low, near_high, near_low, across, quarter = refs[:6]
     far, whites, (white_high, white_low) = refs[6 : 6 + count], refs[6 + count : 9 + count], refs[9 + count : 11 + count]
-    terms, pieces, (joined, product) = refs[-10:-6], refs[-6:-2], refs[-2:]
+    terms, pieces, (joined, product) = refs[-8:-4], refs[-4:-2], refs[-2:]
     row, member = lax.axis_index("row"), lax.axis_index(("col", "rep"))
     joined[row] = quarter[...]
     for j, ref in zip(ORDER, whites):
@@ -195,20 +195,21 @@
         rows = slice(n * depth, (n + 1) * depth)
         product[rows, :] = -(total[rows, :] + times(*split(ref[...]), 3))
     flipped = split(-product[...].T)
-    depth = pieces[0].shape[0]
+    depth = pieces[0].shape[0] // 2
     for j in range(4):
         columns = pl.ds(pl.multiple_of((row ^ j) * TILE, TILE), TILE)
         terms[j][...] = dot3(flipped, (white_high[:, columns], white_low[:, columns]))
-        pieces[j][...] = product[pl.ds(pl.multiple_of((member ^ j) * depth, 8), depth), :]
+        mine = pl.ds(pl.multiple_of((member ^ j) * depth, 8), depth)
+        pieces[j % 2][j // 2 * depth : (j // 2 + 1) * depth, :] = product[mine, :]
 
 
 def products(seps, across, quarter, far, whites, own_white):
     depth, width = whites[0].shape
     return pl.pallas_call(
         product_kernel,
-        out_shape=(f32(width, TILE),) * 4 + (f32(depth // 4, width),) * 4,
+        out_shape=(f32(width, TILE),) * 4 + (f32(depth // 2, width),) * 2,
         in_specs=[VMEM] * (11 + len(far)),
-        out_specs=(VMEM,) * 8,
+        out_specs=(VMEM,) * 6,
         scratch_shapes=[
             pltpu.VMEM((4, depth, 2 * width), jnp.bfloat16),
             pltpu.VMEM((depth, width), jnp.float32),
@@ -218,20 +219,21 @@
 
 
 def rows_kernel(own, near, across, far, out_ref):
-    member = lax.axis_index(("col", "rep"))
-    for j, ref in enumerate((own, near, across, far)):
-        out_ref[:, pl.ds(pl.multiple_of((member ^ j) * TILE, TILE), TILE)] = ref[...]
-
-
-def rows_of(pieces):
-    count, width = pieces[0].shape
+    member, count = lax.axis_index(("col", "rep")), out_ref.shape[0]
+    blocks = (own[:count, :], near[:count, :], across[...], far[...])
+    for j, block in enumerate(blocks):
+        out_ref[:, pl.ds(pl.multiple_of((member ^ j) * TILE, TILE), TILE)] = block
+
+
+def rows_of(own, near, across, far):
+    count, width = own.shape
     return pl.pallas_call(
         rows_kernel,
-        out_shape=f32(count, 4 * width),
+        out_shape=f32(count // 2, 4 * width),
         in_specs=[VMEM] * 4,
         out_specs=VMEM,
         compiler_params=PARAMS,
-    )(*pieces)
+    )(own, near, across, far)
 
 
 def diagonal_kernel(own, first, second, third, base_ref, out_ref, variances_ref):
@@ -276,18 +278,16 @@
         for i in range(3)
     ]
     out = products(seps, across, split_quarter, far, [whites[j] for j in ORDER], own_white)
-    terms, pieces = out[:4], out[4:]
+    terms, (mine, others) = out[:4], out[4:]
+    near = lax.ppermute(others, "rep", SWAP)
     got = [lax.ppermute(terms[j], "row", rows_apart(j)) for j in (2, 1, 3)]
-    mine = [
-        pieces[0],
-        lax.ppermute(pieces[1], "rep", SWAP),
-        lax.ppermute(pieces[2], "col", SWAP),
-        lax.ppermute(pieces[3], ("col", "rep"), rows_apart(3)),
-    ]
-    got, mine = lax.optimization_barrier((got, mine))
+    count = mine.shape[0] // 2
+    across = lax.ppermute(mine[count:], "col", SWAP)
+    far = lax.ppermute(near[count:], "col", SWAP)
     block = terms[0] + got[0] + got[1] + got[2]
-    blocks = [block] + [lax.ppermute(block, "row", rows_apart(j)) for j in (2, 3, 1)]
-    sigma_rows = rows_of(mine)
+    again, across, far = lax.optimization_barrier((block, across, far))
+    blocks = [block] + [lax.ppermute(block, "row", rows_apart(j)) for j in (2, 3)] + [lax.ppermute(again, "row", rows_apart(1))]
+    sigma_rows = rows_of(mine, near, across, far)
     blocks, sigma_rows = lax.optimization_barrier((blocks, sigma_rows))
     sigma_diag, variances = diagonal(blocks, base)
     return sigma_rows, sigma_diag, variances.reshape(-1)

time: 47 us -> 46.6 us (level)
  waiting for transfers between devices: 18.4 us -> 17.1 us
  starting transfers between devices: 18.4 us -> 19.3 us
    ppermute x3 -> x4, waiting for transfers between devices: 3.44 us -> 0.33 us  [the longest x1 0.33 us: four_by_four(): lax.ppermute(again, 'row', rows_apart(1))]
    ppermute x3, waiting for transfers between devices: 0.75 us -> 3.24 us  [four_by_four(): got = [lax.ppermute(terms[j], 'row', rows_apart(j)) for j in (2, 1, 3)]]
    ppermute x3 -> x4, starting transfers between devices: 1.39 us -> 2.34 us  [the longest x1 1.55 us: four_by_four(): far = lax.ppermute(near[count:], 'col', SWAP)]
    ppermute x3 -> x2, waiting for transfers between devices: 4.58 us -> 3.82 us  [four_by_four(): lax.ppermute(block, 'row', rows_apart(j))]
    ppermute x3 -> x2, starting transfers between devices: 3.75 us -> 3.74 us  [four_by_four(): lax.ppermute(block, 'row', rows_apart(j))]
  transfers between devices with their start and end apart: 17 -> 17, of which waited for: 7 -> 5; matrix products, arithmetic and copies ran while one was open for 0% -> 0% of each run, Pallas kernels for 4% -> 4%
where the time goes in v3:
time: 46.6 us; the launch traced here: 46.4 us
  starting transfers between devices  19.3 us (41%)
  waiting for transfers between devices  17.1 us (37%)
  Pallas kernels  7.22 us (15%)
  local copies, waits for them, and re-layouts  2.04 us (4%)
  between operations  0.74 us (2%)
    ppermute x2, waiting for transfers between devices, four_by_four(): whites = {j: lax.ppermute(quarter, 'row', rows_apart(j)) for j in (2, 1)}  8.24 us
    ppermute x3, starting transfers between devices, four_by_four(): got = [lax.ppermute(terms[j], 'row', rows_apart(j)) for j in (2, 1, 3)]  4.68 us
    ppermute x2, starting transfers between devices, four_by_four(): whites = {j: lax.ppermute(quarter, 'row', rows_apart(j)) for j in (2, 1)}  4.17 us
    ppermute x2, waiting for transfers between devices, four_by_four(): lax.ppermute(block, 'row', rows_apart(j))  3.82 us
    ppermute x2, starting transfers between devices, four_by_four(): lax.ppermute(block, 'row', rows_apart(j))  3.74 us
    ppermute x3, waiting for transfers between devices, four_by_four(): got = [lax.ppermute(terms[j], 'row', rows_apart(j)) for j in (2, 1, 3)]  3.24 us
    pallas_call x1, Pallas kernels, first(): pl.pallas_call(first_kernel, out_shape=(f32(panel_rows.shape[0], TILE), f...  2.94 us
    ppermute x1, starting transfers between devices, four_by_four(): across = lax.ppermute(own, 'col', SWAP)  2.56 us
  transfers between devices with their start and end apart: 17, of which 5 were waited for; matrix products, arithmetic and copies ran while one was open for 0% of the time, Pallas kernels for 4%

profile of v3, /device:TPU:0, one launch (start us, length us, event | category | flops | bytes accessed | tf_op | source)
XLA Modules:
  0.0 46.4 jit_solution(5390813850828787206)
XLA Ops:
  0.7 2.9 %shard_map.67 = (f32[384,128]{1,0:T(8,128)}, f32[384,384]{1,0:T(8,128)}) custom-call(s32[12]{0:T(128)} %tiles_hbm.1, f32[768,768]{1,0:T(8,128)} %sep_hbm.1, f32[384,512]{1,0:T(8,128)} %refs_0_.1, f32[512,512]{1,0:T(8,128)} %refs_1_.1), custom_call_target="tpu_custom_call" | custom-call | tf_op jit(solution)/shard_map/pallas_call | solution.py:129
  3.6 0.5 %collective-permute-start = (f32[384,384]{1,0:T(8,128)}, f32[384,384]{1,0:T(8,128)S(1)}, u32[]{:S(2)}, u32[]{:S(2)}) collective-permute-start(f32[384,384]{1,0:T(8,128)} %get-tuple-element.34.refs_3_), channel_id=1, source_target_pairs={{0,1},{1,0},{2,3},{3,2},{4,5},{5,4},{6,7},{7,6},{8,9},{9,8},{10,11... | collective-permute-start | bytes 1769480 | tf_op jit(solution)/shard_map/ppermute | solution.py:270
  4.1 2.6 %collective-permute-start.1 = (f32[384,384]{1,0:T(8,128)}, f32[384,384]{1,0:T(8,128)S(1)}, u32[]{:S(2)}, u32[]{:S(2)}) collective-permute-start(f32[384,384]{1,0:T(8,128)} %get-tuple-element.34.refs_3_), channel_id=1, source_target_pairs={{0,2},{2,0},{1,3},{3,1},{4,6},{6,4},{5,7},{7,5},{8,10},{10,8},{9,1... | collective-permute-start | bytes 1769480 | tf_op jit(solution)/shard_map/ppermute | solution.py:269
  6.7 2.6 %collective-permute-start.5 = (f32[384,128]{1,0:T(8,128)}, f32[384,128]{1,0:T(8,128)S(1)}, u32[]{:S(2)}, u32[]{:S(2)}) collective-permute-start(f32[384,128]{1,0:T(8,128)} %get-tuple-element.33.refs_2_), channel_id=1, source_target_pairs={{0,8},{4,12},{8,0},{12,4},{1,9},{5,13},{9,1},{13,5},{2,10},{6,14},... | collective-permute-start | bytes 589832 | tf_op jit(solution)/shard_map/ppermute | solution.py:271
  9.3 1.6 %collective-permute-start.7 = (f32[384,128]{1,0:T(8,128)}, f32[384,128]{1,0:T(8,128)S(1)}, u32[]{:S(2)}, u32[]{:S(2)}) collective-permute-start(f32[384,128]{1,0:T(8,128)} %get-tuple-element.33.refs_2_), channel_id=1, source_target_pairs={{0,4},{4,0},{8,12},{12,8},{1,5},{5,1},{9,13},{13,9},{2,6},{6,2},{1... | collective-permute-start | bytes 589832 | tf_op jit(solution)/shard_map/ppermute | solution.py:271
  10.9 8.2 %collective-permute-done.5.refs_9_ = f32[384,128]{1,0:T(8,128)S(1)} collective-permute-done((f32[384,128]{1,0:T(8,128)}, f32[384,128]{1,0:T(8,128)S(1)}, u32[]{:S(2)}, u32[]{:S(2)}) %collective-permute-start.5) | collective-permute-done | bytes 196640 | tf_op jit(solution)/shard_map/ppermute | solution.py:271
  19.1 0.7 %collective-permute-start.6 = (f32[384,128]{1,0:T(8,128)S(1)}, f32[384,128]{1,0:T(8,128)S(1)}, u32[]{:S(2)}, u32[]{:S(2)}) collective-permute-start(f32[384,128]{1,0:T(8,128)S(1)} %collective-permute-done.5.refs_9_), channel_id=1, source_target_pairs={{0,4},{4,0},{8,12},{12,8},{1,5},{5,1},{9,13},{13,9},{2,6},{6,2},{1... | collective-permute-start | bytes 589832 | tf_op jit(solution)/shard_map/ppermute | solution.py:272
  19.8 1.1 %copy-done.2 = f32[384,384]{1,0:T(8,128)S(1)} copy-done((f32[384,384]{1,0:T(8,128)S(1)}, f32[384,384]{1,0:T(8,128)}, u32[]{:S(2)}) %copy-start.2) | copy-done | bytes 589848
  20.8 0.9 %copy-done.3 = f32[384,128]{1,0:T(8,128)S(1)} copy-done((f32[384,128]{1,0:T(8,128)S(1)}, f32[384,128]{1,0:T(8,128)}, u32[]{:S(2)}) %copy-start.3) | copy-done | bytes 196632
  21.8 1.2 %shard_map.68 = (bf16[384,512]{1,0:T(8,128)(2,1)S(1)}, bf16[384,512]{1,0:T(8,128)(2,1)S(1)}, f32[128,512]{1,0:T(8,128)S(1)}, bf16[384,256]{1,0:T(8,128)(2,1)S(1)...) custom-call(f32[384,512]{1,0:T(8,128)S(1)} %copy-done.1, ...), custom_call_target="tpu_custom_call" | custom-call | tf_op jit(solution)/shard_map/pallas_call | solution.py:161
  23.2 0.5 %collective-permute-start.3 = (f32[128,384]{1,0:T(8,128)S(1)}, f32[128,384]{1,0:T(8,128)S(1)}, u32[]{:S(2)}, u32[]{:S(2)}) collective-permute-start(f32[128,384]{1,0:T(8,128)S(1)} %get-tuple-element.64), channel_id=1, source_target_pairs={{0,1},{1,0},{2,3},{3,2},{4,5},{5,4},{6,7},{7,6},{8,9},{9,8},{10,11... | collective-permute-start | bytes 589832 | tf_op jit(solution)/shard_map/ppermute | solution.py:277
  23.7 1.4 %collective-permute-done.6.refs_10_ = f32[384,128]{1,0:T(8,128)S(1)} collective-permute-done((f32[384,128]{1,0:T(8,128)S(1)}, f32[384,128]{1,0:T(8,128)S(1)}, u32[]{:S(2)}, u32[]{:S(2)}) %collective-permute-start.6) | collective-permute-done | bytes 196640 | tf_op jit(solution)/shard_map/ppermute | solution.py:272
  25.2 1.6 %shard_map.69 = (f32[128,128]{1,0:T(8,128)S(1)}, f32[128,128]{1,0:T(8,128)S(1)}, f32[128,128]{1,0:T(8,128)S(1)}, f32[128,128]{1,0:T(8,128)S(1)}, f32[192,128]{1,0:T(8,128)S(1)}, /*index=5*/f32[192,128]{1,0:T(8,128)S(1)}) custom-call(bf16[384,384]{1,0:T(8,128)(2,1)S(1)} %get-tuple-element.35.refs_0_, bf16[384,384]{1,0:T(8,128)(2,1)S(1)} %get-tuple-element.36.refs_1_, ...), custom_call_target="tpu_custom_call" | custom-call | tf_op jit(solution)/shard_map/pallas_call | solution.py:208
  27.0 4.0 %collective-permute-start.10 = (f32[128,128]{1,0:T(8,128)S(1)}, f32[128,128]{1,0:T(8,128)S(1)}, u32[]{:S(2)}, u32[]{:S(2)}) collective-permute-start(f32[128,128]{1,0:T(8,128)S(1)} %get-tuple-element.49), channel_id=1, source_target_pairs={{0,12},{4,8},{8,4},{12,0},{1,13},{5,9},{9,5},{13,1},{2,14},{6,10},... | collective-permute-start | bytes 196616 | tf_op jit(solution)/shard_map/ppermute | solution.py:283
  31.0 0.6 %collective-permute-start.9 = (f32[128,128]{1,0:T(8,128)S(1)}, f32[128,128]{1,0:T(8,128)S(1)}, u32[]{:S(2)}, u32[]{:S(2)}) collective-permute-start(f32[128,128]{1,0:T(8,128)S(1)} %get-tuple-element.48), channel_id=1, source_target_pairs={{0,4},{4,0},{8,12},{12,8},{1,5},{5,1},{9,13},{13,9},{2,6},{6,2},{1... | collective-permute-start | bytes 196616 | tf_op jit(solution)/shard_map/ppermute | solution.py:283
  31.7 0.5 %collective-permute-start.13 = (f32[96,128]{1,0:T(8,128)S(1)}, f32[96,128]{1,0:T(8,128)S(1)}, u32[]{:S(2)}, u32[]{:S(2)}) collective-permute-start(f32[96,128]{1,0:T(8,128)S(1)} %slice.18), channel_id=1, source_target_pairs={{0,2},{2,0},{1,3},{3,1},{4,6},{6,4},{5,7},{7,5},{8,10},{10,8},{9,1... | collective-permute-start | bytes 147464 | tf_op jit(solution)/shard_map/ppermute | solution.py:285
  32.2 1.6 %collective-permute-start.15 = (f32[96,128]{1,0:T(8,128)S(1)}, f32[96,128]{1,0:T(8,128)S(1)}, u32[]{:S(2)}, u32[]{:S(2)}) collective-permute-start(f32[96,128]{1,0:T(8,128)S(1)} %slice.20), channel_id=1, source_target_pairs={{0,2},{2,0},{1,3},{3,1},{4,6},{6,4},{5,7},{7,5},{8,10},{10,8},{9,1... | collective-permute-start | bytes 147464 | tf_op jit(solution)/shard_map/ppermute | solution.py:286
  33.8 3.2 %collective-permute-done.8 = f32[128,128]{1,0:T(8,128)S(1)} collective-permute-done((f32[128,128]{1,0:T(8,128)S(1)}, f32[128,128]{1,0:T(8,128)S(1)}, u32[]{:S(2)}, u32[]{:S(2)}) %collective-permute-start.8) | collective-permute-done | bytes 65568 | tf_op jit(solution)/shard_map/ppermute | solution.py:283
  37.0 1.3 %collective-permute-start.11 = (f32[128,128]{1,0:T(8,128)S(1)}, f32[128,128]{1,0:T(8,128)S(1)}, u32[]{:S(2)}, u32[]{:S(2)}) collective-permute-start(f32[128,128]{1,0:T(8,128)S(1)} %add_add_fusion.own), channel_id=1, source_target_pairs={{0,8},{4,12},{8,0},{12,4},{1,9},{5,13},{9,1},{13,5},{2,10},{6,14},... | collective-permute-start | bytes 196616 | tf_op jit(solution)/shard_map/ppermute | solution.py:289
  38.4 2.4 %collective-permute-start.12 = (f32[128,128]{1,0:T(8,128)S(1)}, f32[128,128]{1,0:T(8,128)S(1)}, u32[]{:S(2)}, u32[]{:S(2)}) collective-permute-start(f32[128,128]{1,0:T(8,128)S(1)} %add_add_fusion.own), channel_id=1, source_target_pairs={{0,12},{4,8},{8,4},{12,0},{1,13},{5,9},{9,5},{13,1},{2,14},{6,10},... | collective-permute-start | bytes 196616 | tf_op jit(solution)/shard_map/ppermute | solution.py:289
  40.8 0.7 %shard_map.70 = f32[96,512]{1,0:T(8,128)} custom-call(f32[192,128]{1,0:T(8,128)S(1)} %get-tuple-element.50.own, f32[192,128]{1,0:T(8,128)S(1)} %collective-permute-done.14.near, f32[96,128]{1,0:T(8,128)S(1)} %collective-permute-done.13.across, f32[96,128]{1,0:T(8,128)S(1)} %collective-permute-done.15.far), custom_call_target="tpu_custom_call" | custom-call | tf_op jit(solution)/shard_map/pallas_call | solution.py:230
  41.5 3.8 %collective-permute-done.11.first = f32[128,128]{1,0:T(8,128)S(1)} collective-permute-done((f32[128,128]{1,0:T(8,128)S(1)}, f32[128,128]{1,0:T(8,128)S(1)}, u32[]{:S(2)}, u32[]{:S(2)}) %collective-permute-start.11) | collective-permute-done | bytes 65568 | tf_op jit(solution)/shard_map/ppermute | solution.py:289
  45.3 0.3 collective-permute-done.16.third
  45.7 0.8 %shard_map.71 = (f32[128,512]{1,0:T(8,128)}, f32[1,128]{1,0:T(1,128)}) custom-call(f32[128,128]{1,0:T(8,128)S(1)} %add_add_fusion.own, f32[128,128]{1,0:T(8,128)S(1)} %collective-permute-done.11.first, f32[128,128]{1,0:T(8,128)S(1)} %collective-permute-done.12.second, f32[128,128]{1,0:T(8,128)S(1)} %collective-permute-done.16.third, ...), custom_call_target="tpu_custom_call" | custom-call | tf_op jit(solution)/shard_map/pallas_call | solution.py:251
  (27 shorter events, 0.6 us)
Async XLA Ops:
  0.6 19.1 %copy-start.1 = (f32[384,512]{1,0:T(8,128)S(1)}, f32[384,512]{1,0:T(8,128)}, u32[]{:S(2)}) copy-start(f32[384,512]{1,0:T(8,128)} %refs_0_.1) | copy-start | bytes 2359300
  0.6 19.1 %copy-start = (f32[512,512]{1,0:T(8,128)S(1)}, f32[512,512]{1,0:T(8,128)}, u32[]{:S(2)}) copy-start(f32[512,512]{1,0:T(8,128)} %refs_1_.1) | copy-start | bytes 3145732
  3.6 16.2 %collective-permute-start = (f32[384,384]{1,0:T(8,128)}, f32[384,384]{1,0:T(8,128)S(1)}, u32[]{:S(2)}, u32[]{:S(2)}) collective-permute-start(f32[384,384]{1,0:T(8,128)} %get-tuple-element.34.refs_3_), channel_id=1, source_target_pairs={{0,1},{1,0},{2,3},{3,2},{4,5},{5,4},{6,7},{7,6},{8,9},{9,8},{10,11... | collective-permute-start | bytes 1769480 | tf_op jit(solution)/shard_map/ppermute | solution.py:270
  4.1 18.9 %collective-permute-start.1 = (f32[384,384]{1,0:T(8,128)}, f32[384,384]{1,0:T(8,128)S(1)}, u32[]{:S(2)}, u32[]{:S(2)}) collective-permute-start(f32[384,384]{1,0:T(8,128)} %get-tuple-element.34.refs_3_), channel_id=1, source_target_pairs={{0,2},{2,0},{1,3},{3,1},{4,6},{6,4},{5,7},{7,5},{8,10},{10,8},{9,1... | collective-permute-start | bytes 1769480 | tf_op jit(solution)/shard_map/ppermute | solution.py:269
  6.7 12.4 %collective-permute-start.5 = (f32[384,128]{1,0:T(8,128)}, f32[384,128]{1,0:T(8,128)S(1)}, u32[]{:S(2)}, u32[]{:S(2)}) collective-permute-start(f32[384,128]{1,0:T(8,128)} %get-tuple-element.33.refs_2_), channel_id=1, source_target_pairs={{0,8},{4,12},{8,0},{12,4},{1,9},{5,13},{9,1},{13,5},{2,10},{6,14},... | collective-permute-start | bytes 589832 | tf_op jit(solution)/shard_map/ppermute | solution.py:271
  9.3 14.5 %collective-permute-start.7 = (f32[384,128]{1,0:T(8,128)}, f32[384,128]{1,0:T(8,128)S(1)}, u32[]{:S(2)}, u32[]{:S(2)}) collective-permute-start(f32[384,128]{1,0:T(8,128)} %get-tuple-element.33.refs_2_), channel_id=1, source_target_pairs={{0,4},{4,0},{8,12},{12,8},{1,5},{5,1},{9,13},{13,9},{2,6},{6,2},{1... | collective-permute-start | bytes 589832 | tf_op jit(solution)/shard_map/ppermute | solution.py:271
  19.1 6.1 %collective-permute-start.6 = (f32[384,128]{1,0:T(8,128)S(1)}, f32[384,128]{1,0:T(8,128)S(1)}, u32[]{:S(2)}, u32[]{:S(2)}) collective-permute-start(f32[384,128]{1,0:T(8,128)S(1)} %collective-permute-done.5.refs_9_), channel_id=1, source_target_pairs={{0,4},{4,0},{8,12},{12,8},{1,5},{5,1},{9,13},{13,9},{2,6},{6,2},{1... | collective-permute-start | bytes 589832 | tf_op jit(solution)/shard_map/ppermute | solution.py:272
  19.8 1.1 %copy-start.2 = (f32[384,384]{1,0:T(8,128)S(1)}, f32[384,384]{1,0:T(8,128)}, u32[]{:S(2)}) copy-start(f32[384,384]{1,0:T(8,128)} %get-tuple-element.34.refs_3_) | copy-start | bytes 1769476
  20.8 0.9 %copy-start.3 = (f32[384,128]{1,0:T(8,128)S(1)}, f32[384,128]{1,0:T(8,128)}, u32[]{:S(2)}) copy-start(f32[384,128]{1,0:T(8,128)} %get-tuple-element.33.refs_2_) | copy-start | bytes 589828
  23.1 2.1 %collective-permute-start.2 = (f32[128,384]{1,0:T(8,128)S(1)}, f32[128,384]{1,0:T(8,128)S(1)}, u32[]{:S(2)}, u32[]{:S(2)}) collective-permute-start(f32[128,384]{1,0:T(8,128)S(1)} %get-tuple-element.65), channel_id=1, source_target_pairs={{0,1},{1,0},{2,3},{3,2},{4,5},{5,4},{6,7},{7,6},{8,9},{9,8},{10,11... | collective-permute-start | bytes 589832 | tf_op jit(solution)/shard_map/ppermute | solution.py:277
  23.2 2.0 %collective-permute-start.3 = (f32[128,384]{1,0:T(8,128)S(1)}, f32[128,384]{1,0:T(8,128)S(1)}, u32[]{:S(2)}, u32[]{:S(2)}) collective-permute-start(f32[128,384]{1,0:T(8,128)S(1)} %get-tuple-element.64), channel_id=1, source_target_pairs={{0,1},{1,0},{2,3},{3,2},{4,5},{5,4},{6,7},{7,6},{8,9},{9,8},{10,11... | collective-permute-start | bytes 589832 | tf_op jit(solution)/shard_map/ppermute | solution.py:277
  23.7 1.5 %collective-permute-start.4 = (f32[128,384]{1,0:T(8,128)S(1)}, f32[128,384]{1,0:T(8,128)S(1)}, u32[]{:S(2)}, u32[]{:S(2)}) collective-permute-start(f32[128,384]{1,0:T(8,128)S(1)} %get-tuple-element.63), channel_id=1, source_target_pairs={{0,1},{1,0},{2,3},{3,2},{4,5},{5,4},{6,7},{7,6},{8,9},{9,8},{10,11... | collective-permute-start | bytes 589832 | tf_op jit(solution)/shard_map/ppermute | solution.py:277
  26.8 5.5 %collective-permute-start.14 = (f32[192,128]{1,0:T(8,128)S(1)}, f32[192,128]{1,0:T(8,128)S(1)}, u32[]{:S(2)}, u32[]{:S(2)}) collective-permute-start(f32[192,128]{1,0:T(8,128)S(1)} %get-tuple-element.51), channel_id=1, source_target_pairs={{0,1},{1,0},{2,3},{3,2},{4,5},{5,4},{6,7},{7,6},{8,9},{9,8},{10,11... | collective-permute-start | bytes 294920 | tf_op jit(solution)/shard_map/ppermute | solution.py:282
  27.0 6.8 %collective-permute-start.10 = (f32[128,128]{1,0:T(8,128)S(1)}, f32[128,128]{1,0:T(8,128)S(1)}, u32[]{:S(2)}, u32[]{:S(2)}) collective-permute-start(f32[128,128]{1,0:T(8,128)S(1)} %get-tuple-element.49), channel_id=1, source_target_pairs={{0,12},{4,8},{8,4},{12,0},{1,13},{5,9},{9,5},{13,1},{2,14},{6,10},... | collective-permute-start | bytes 196616 | tf_op jit(solution)/shard_map/ppermute | solution.py:283
  31.0 6.0 %collective-permute-start.8 = (f32[128,128]{1,0:T(8,128)S(1)}, f32[128,128]{1,0:T(8,128)S(1)}, u32[]{:S(2)}, u32[]{:S(2)}) collective-permute-start(f32[128,128]{1,0:T(8,128)S(1)} %get-tuple-element.47), channel_id=1, source_target_pairs={{0,8},{4,12},{8,0},{12,4},{1,9},{5,13},{9,1},{13,5},{2,10},{6,14},... | collective-permute-start | bytes 196616 | tf_op jit(solution)/shard_map/ppermute | solution.py:283
  31.0 6.0 %collective-permute-start.9 = (f32[128,128]{1,0:T(8,128)S(1)}, f32[128,128]{1,0:T(8,128)S(1)}, u32[]{:S(2)}, u32[]{:S(2)}) collective-permute-start(f32[128,128]{1,0:T(8,128)S(1)} %get-tuple-element.48), channel_id=1, source_target_pairs={{0,4},{4,0},{8,12},{12,8},{1,5},{5,1},{9,13},{13,9},{2,6},{6,2},{1... | collective-permute-start | bytes 196616 | tf_op jit(solution)/shard_map/ppermute | solution.py:283
  31.7 9.1 %collective-permute-start.13 = (f32[96,128]{1,0:T(8,128)S(1)}, f32[96,128]{1,0:T(8,128)S(1)}, u32[]{:S(2)}, u32[]{:S(2)}) collective-permute-start(f32[96,128]{1,0:T(8,128)S(1)} %slice.18), channel_id=1, source_target_pairs={{0,2},{2,0},{1,3},{3,1},{4,6},{6,4},{5,7},{7,5},{8,10},{10,8},{9,1... | collective-permute-start | bytes 147464 | tf_op jit(solution)/shard_map/ppermute | solution.py:285
  32.2 8.6 %collective-permute-start.15 = (f32[96,128]{1,0:T(8,128)S(1)}, f32[96,128]{1,0:T(8,128)S(1)}, u32[]{:S(2)}, u32[]{:S(2)}) collective-permute-start(f32[96,128]{1,0:T(8,128)S(1)} %slice.20), channel_id=1, source_target_pairs={{0,2},{2,0},{1,3},{3,1},{4,6},{6,4},{5,7},{7,5},{8,10},{10,8},{9,1... | collective-permute-start | bytes 147464 | tf_op jit(solution)/shard_map/ppermute | solution.py:286
  37.0 8.3 %collective-permute-start.11 = (f32[128,128]{1,0:T(8,128)S(1)}, f32[128,128]{1,0:T(8,128)S(1)}, u32[]{:S(2)}, u32[]{:S(2)}) collective-permute-start(f32[128,128]{1,0:T(8,128)S(1)} %add_add_fusion.own), channel_id=1, source_target_pairs={{0,8},{4,12},{8,0},{12,4},{1,9},{5,13},{9,1},{13,5},{2,10},{6,14},... | collective-permute-start | bytes 196616 | tf_op jit(solution)/shard_map/ppermute | solution.py:289
  38.4 7.0 %collective-permute-start.12 = (f32[128,128]{1,0:T(8,128)S(1)}, f32[128,128]{1,0:T(8,128)S(1)}, u32[]{:S(2)}, u32[]{:S(2)}) collective-permute-start(f32[128,128]{1,0:T(8,128)S(1)} %add_add_fusion.own), channel_id=1, source_target_pairs={{0,12},{4,8},{8,4},{12,0},{1,13},{5,9},{9,5},{13,1},{2,14},{6,10},... | collective-permute-start | bytes 196616 | tf_op jit(solution)/shard_map/ppermute | solution.py:289
  40.8 4.9 %collective-permute-start.16 = (f32[128,128]{1,0:T(8,128)S(1)}, f32[128,128]{1,0:T(8,128)S(1)}, u32[]{:S(2)}, u32[]{:S(2)}) collective-permute-start(f32[128,128]{1,0:T(8,128)S(1)} %add_add_fusion.own), channel_id=1, source_target_pairs={{0,4},{4,0},{8,12},{12,8},{1,5},{5,1},{9,13},{13,9},{2,6},{6,2},{1... | collective-permute-start | bytes 196616 | tf_op jit(solution)/shard_map/ppermute | solution.py:289

commit v4 on v3

--- a/solution.py
+++ b/solution.py
@@ -142,22 +142,23 @@
 
 def whiten_kernel(*refs):
     panel_ref, inverse_ref, quarter_ref, own_ref, near_ref = refs[:5]
-    high_ref, low_ref, base_ref, quarter_out, own_high, own_low, near_high, near_low = refs[5:]
+    high_ref, low_ref, base_ref, quarter_out, sep_high, sep_low = refs[5:]
     member = lax.axis_index(("col", "rep"))
     columns = pl.ds(pl.multiple_of(member * TILE, TILE), TILE)
     inverse = split(inverse_ref[...])
     high_ref[...], low_ref[...] = split(dot3(split(panel_ref[...]), inverse))
     base_ref[...] = dot3(split(inverse_ref[:, columns].T), inverse)
     quarter_out[:, :TILE], quarter_out[:, TILE:] = split(quarter_ref[...])
-    own_high[...], own_low[...] = split(own_ref[...])
-    near_high[...], near_low[...] = split(near_ref[...])
+    depth = own_ref.shape[1]
+    sep_high[:, :depth], sep_low[:, :depth] = split(own_ref[...])
+    sep_high[:, depth:], sep_low[:, depth:] = split(near_ref[...])
 
 
 def whiten(panel_rows, diag_inverse, quarter, own, near):
     def part(*shape):
         return jax.ShapeDtypeStruct(shape, jnp.bfloat16)
 
-    white, sep = part(*panel_rows.shape), part(*own.shape)
+    white, sep = part(*panel_rows.shape), part(own.shape[0], 2 * own.shape[1])
     out = pl.pallas_call(
         whiten_kernel,
         out_shape=(
@@ -165,40 +166,47 @@
             white,
             f32(TILE, diag_inverse.shape[1]),
             part(quarter.shape[0], 2 * TILE),
-            *[sep] * 4,
+            *[sep] * 2,
         ),
         in_specs=[VMEM] * 5,
-        out_specs=(VMEM,) * 8,
+        out_specs=(VMEM,) * 6,
         compiler_params=PARAMS,
     )(panel_rows, diag_inverse, quarter, own, near)
     return out[:2], out[2], out[3], out[4:]
 
 
 def product_kernel(*refs):
-    count = len(refs) - 19
-    own_high, own_low, near_high, near_low, across, quarter = refs[:6]
-    far, whites, (white_high, white_low) = refs[6 : 6 + count], refs[6 + count : 9 + count], refs[9 + count : 11 + count]
-    terms, pieces, (joined, product) = refs[-8:-4], refs[-4:-2], refs[-2:]
+    sep_high, sep_low, across, quarter, *far = refs[:-15]
+    whites, (white_high, white_low) = refs[-15:-12], refs[-12:-10]
+    terms, pieces, (joined, product, other_high, other_low) = refs[-10:-6], refs[-6:-4], refs[-4:]
     row, member = lax.axis_index("row"), lax.axis_index(("col", "rep"))
-    joined[row] = quarter[...]
+    depth = across.shape[1]
+
+    def place(j):
+        return pl.ds(pl.multiple_of((row ^ j ^ member) * depth, TILE), depth)
+
+    joined[place(0), :] = quarter[...]
     for j, ref in zip(ORDER, whites):
-        joined[row ^ j, :, :TILE], joined[row ^ j, :, TILE:] = split(ref[...])
-
-    def times(high, low, i):
-        wide = dot(high, joined[member ^ i])
-        return wide[:, :TILE] + (wide[:, TILE:] + dot(low, joined[member ^ i, :, :TILE]))
-
-    total = times(own_high[...], own_low[...], 0) + times(near_high[...], near_low[...], 1)
-    total += times(*split(across[...]), 2)
-    depth = far[0].shape[0]
+        joined[place(j), :TILE], joined[place(j), TILE:] = split(ref[...])
+    other_high[:, :depth], other_low[:, :depth] = split(across[...])
+    count = far[0].shape[0]
     for n, ref in enumerate(far):
-        rows = slice(n * depth, (n + 1) * depth)
-        product[rows, :] = -(total[rows, :] + times(*split(ref[...]), 3))
-    flipped = split(-product[...].T)
+        rows = slice(n * count, (n + 1) * count)
+        other_high[rows, depth:], other_low[rows, depth:] = split(ref[...])
+    wide = dot(sep_high[...], joined[: 2 * depth, :]) + dot(other_high[...], joined[2 * depth :, :])
+    low = dot(sep_low[...], joined[: 2 * depth, :TILE]) + dot(other_low[...], joined[2 * depth :, :TILE])
+    total = wide[:, :TILE] + (wide[:, TILE:] + low)
+    product[...] = -total
+    flipped = split(total.T)
+    stacked = jnp.concatenate(flipped)
     depth = pieces[0].shape[0] // 2
+    both = dot(stacked, white_high[...])
+    full = both[:TILE] + (both[TILE:] + dot(flipped[0], white_low[...]))
     for j in range(4):
-        columns = pl.ds(pl.multiple_of((row ^ j) * TILE, TILE), TILE)
-        terms[j][...] = dot3(flipped, (white_high[:, columns], white_low[:, columns]))
+        value = full[:, :TILE]
+        for n in range(1, 4):
+            value = jnp.where((row ^ j) == n, full[:, n * TILE : (n + 1) * TILE], value)
+        terms[j][...] = value
         mine = pl.ds(pl.multiple_of((member ^ j) * depth, 8), depth)
         pieces[j % 2][j // 2 * depth : (j // 2 + 1) * depth, :] = product[mine, :]
 
@@ -208,11 +216,13 @@
     return pl.pallas_call(
         product_kernel,
         out_shape=(f32(width, TILE),) * 4 + (f32(depth // 2, width),) * 2,
-        in_specs=[VMEM] * (11 + len(far)),
+        in_specs=[VMEM] * (9 + len(far)),
         out_specs=(VMEM,) * 6,
         scratch_shapes=[
-            pltpu.VMEM((4, depth, 2 * width), jnp.bfloat16),
+            pltpu.VMEM((4 * depth, 2 * width), jnp.bfloat16),
             pltpu.VMEM((depth, width), jnp.float32),
+            pltpu.VMEM((depth, 2 * depth), jnp.bfloat16),
+            pltpu.VMEM((depth, 2 * depth), jnp.bfloat16),
         ],
         compiler_params=PARAMS,
     )(*seps, across, quarter, *far, *whites, *own_white)
@@ -268,8 +278,8 @@
     quarter, own = first(row_tiles, sep_inverse, panel_rows, diag_inverse)
     across = lax.ppermute(own, "col", SWAP)
     near = lax.ppermute(own, "rep", SWAP)
-    whites = {j: lax.ppermute(quarter, "row", rows_apart(j)) for j in (2, 1)}
-    whites[3] = lax.ppermute(whites[2], "row", rows_apart(1))
+    whites = {j: lax.ppermute(quarter, "row", rows_apart(j)) for j in (3, 1)}
+    whites[2] = lax.ppermute(whites[3], "row", rows_apart(1))
     own_white, base, split_quarter, seps = whiten(panel_rows, diag_inverse, quarter, own, near)
     across, own_white, base = lax.optimization_barrier((across, own_white, base))
     count = across.shape[0] // 3

time: 46.6 us -> 45 us (0.966)
  waiting for transfers between devices: 17.1 us -> 14.2 us
  starting transfers between devices: 19.3 us -> 20.8 us
    ppermute x3, waiting for transfers between devices: 9.67 us -> 6.81 us  [the longest x2 6.19 us: four_by_four(): whites = {j: lax.ppermute(quarter, 'row', rows_apart(j)) for j in (3, 1)}]
    ppermute x3, starting transfers between devices: 4.84 us -> 6.78 us  [the longest x2 3.6 us: four_by_four(): whites = {j: lax.ppermute(quarter, 'row', rows_apart(j)) for j in (3, 1)}]
    ppermute x3, waiting for transfers between devices: 3.24 us -> 2.4 us  [four_by_four(): got = [lax.ppermute(terms[j], 'row', rows_apart(j)) for j in (2, 1, 3)]]
    ppermute x3, waiting for transfers between devices: 0.01 us -> 0.79 us  [four_by_four(): lax.ppermute(lax.slice_in_dim(across, i * count, (i + 1) * count), 'rep',...]
    ppermute x2, starting transfers between devices: 3.74 us -> 3.14 us  [four_by_four(): lax.ppermute(block, 'row', rows_apart(j))]
  transfers between devices with their start and end apart: 17 -> 17, of which waited for: 5 -> 9; matrix products, arithmetic and copies ran while one was open for 0% -> 0% of each run, Pallas kernels for 4% -> 4%
where the time goes in v4:
time: 45 us; the launch traced here: 44.8 us
  starting transfers between devices  20.8 us (46%)
  waiting for transfers between devices  14.2 us (32%)
  Pallas kernels  6.94 us (15%)
  local copies, waits for them, and re-layouts  2.04 us (5%)
  between operations  0.73 us (2%)
    ppermute x2, waiting for transfers between devices, four_by_four(): whites = {j: lax.ppermute(quarter, 'row', rows_apart(j)) for j in (3, 1)}  6.19 us
    ppermute x3, starting transfers between devices, four_by_four(): got = [lax.ppermute(terms[j], 'row', rows_apart(j)) for j in (2, 1, 3)]  4.39 us
    ppermute x2, waiting for transfers between devices, four_by_four(): lax.ppermute(block, 'row', rows_apart(j))  3.77 us
    ppermute x2, starting transfers between devices, four_by_four(): whites = {j: lax.ppermute(quarter, 'row', rows_apart(j)) for j in (3, 1)}  3.6 us
    ppermute x1, starting transfers between devices, four_by_four(): whites[2] = lax.ppermute(whites[3], 'row', rows_apart(1))  3.18 us
    ppermute x2, starting transfers between devices, four_by_four(): lax.ppermute(block, 'row', rows_apart(j))  3.14 us
    pallas_call x1, Pallas kernels, first(): pl.pallas_call(first_kernel, out_shape=(f32(panel_rows.shape[0], TILE), f...  2.94 us
    ppermute x1, starting transfers between devices, four_by_four(): across = lax.ppermute(own, 'col', SWAP)  2.56 us
  transfers between devices with their start and end apart: 17, of which 9 were waited for; matrix products, arithmetic and copies ran while one was open for 0% of the time, Pallas kernels for 4%

profile of v4, /device:TPU:0, one launch (start us, length us, event | category | flops | bytes accessed | tf_op | source)
XLA Modules:
  0.0 44.8 jit_solution(11153533898955695947)
XLA Ops:
  0.7 2.9 %shard_map.67 = (f32[384,128]{1,0:T(8,128)}, f32[384,384]{1,0:T(8,128)}) custom-call(s32[12]{0:T(128)} %tiles_hbm.1, f32[768,768]{1,0:T(8,128)} %sep_hbm.1, f32[384,512]{1,0:T(8,128)} %refs_0_.1, f32[512,512]{1,0:T(8,128)} %refs_1_.1), custom_call_target="tpu_custom_call" | custom-call | tf_op jit(solution)/shard_map/pallas_call | solution.py:129
  3.6 0.5 %collective-permute-start = (f32[384,384]{1,0:T(8,128)}, f32[384,384]{1,0:T(8,128)S(1)}, u32[]{:S(2)}, u32[]{:S(2)}) collective-permute-start(f32[384,384]{1,0:T(8,128)} %get-tuple-element.32.refs_3_), channel_id=1, source_target_pairs={{0,1},{1,0},{2,3},{3,2},{4,5},{5,4},{6,7},{7,6},{8,9},{9,8},{10,11... | collective-permute-start | bytes 1769480 | tf_op jit(solution)/shard_map/ppermute | solution.py:280
  4.1 2.6 %collective-permute-start.1 = (f32[384,384]{1,0:T(8,128)}, f32[384,384]{1,0:T(8,128)S(1)}, u32[]{:S(2)}, u32[]{:S(2)}) collective-permute-start(f32[384,384]{1,0:T(8,128)} %get-tuple-element.32.refs_3_), channel_id=1, source_target_pairs={{0,2},{2,0},{1,3},{3,1},{4,6},{6,4},{5,7},{7,5},{8,10},{10,8},{9,1... | collective-permute-start | bytes 1769480 | tf_op jit(solution)/shard_map/ppermute | solution.py:279
  6.7 3.6 %collective-permute-start.5 = (f32[384,128]{1,0:T(8,128)}, f32[384,128]{1,0:T(8,128)S(1)}, u32[]{:S(2)}, u32[]{:S(2)}) collective-permute-start(f32[384,128]{1,0:T(8,128)} %get-tuple-element.31.refs_2_), channel_id=1, source_target_pairs={{0,12},{4,8},{8,4},{12,0},{1,13},{5,9},{9,5},{13,1},{2,14},{6,10},... | collective-permute-start | bytes 589832 | tf_op jit(solution)/shard_map/ppermute | solution.py:281
  10.3 6.2 %collective-permute-done.5.refs_8_ = f32[384,128]{1,0:T(8,128)S(1)} collective-permute-done((f32[384,128]{1,0:T(8,128)}, f32[384,128]{1,0:T(8,128)S(1)}, u32[]{:S(2)}, u32[]{:S(2)}) %collective-permute-start.5) | collective-permute-done | bytes 196640 | tf_op jit(solution)/shard_map/ppermute | solution.py:281
  16.5 3.2 %collective-permute-start.6 = (f32[384,128]{1,0:T(8,128)S(1)}, f32[384,128]{1,0:T(8,128)S(1)}, u32[]{:S(2)}, u32[]{:S(2)}) collective-permute-start(f32[384,128]{1,0:T(8,128)S(1)} %collective-permute-done.5.refs_8_), channel_id=1, source_target_pairs={{0,4},{4,0},{8,12},{12,8},{1,5},{5,1},{9,13},{13,9},{2,6},{6,2},{1... | collective-permute-start | bytes 589832 | tf_op jit(solution)/shard_map/ppermute | solution.py:282
  19.7 1.1 %copy-done.2 = f32[384,384]{1,0:T(8,128)S(1)} copy-done((f32[384,384]{1,0:T(8,128)S(1)}, f32[384,384]{1,0:T(8,128)}, u32[]{:S(2)}) %copy-start.2) | copy-done | bytes 589848
  20.7 0.9 %copy-done.3 = f32[384,128]{1,0:T(8,128)S(1)} copy-done((f32[384,128]{1,0:T(8,128)S(1)}, f32[384,128]{1,0:T(8,128)}, u32[]{:S(2)}) %copy-start.3) | copy-done | bytes 196632
  21.7 1.2 %shard_map.68 = (bf16[384,512]{1,0:T(8,128)(2,1)S(1)}, bf16[384,512]{1,0:T(8,128)(2,1)S(1)}, f32[128,512]{1,0:T(8,128)S(1)}, bf16[384,256]{1,0:T(8,128)(2,1)S(1)...) custom-call(f32[384,512]{1,0:T(8,128)S(1)} %copy-done.1, f32[512,512]{1,0:T(8,128)S(1)} %copy-done, ...), custom_call_target="tpu_custom_call" | custom-call | tf_op jit(solution)/shard_map/pallas_call | solution.py:162
  23.1 0.5 %collective-permute-start.3 = (f32[128,384]{1,0:T(8,128)S(1)}, f32[128,384]{1,0:T(8,128)S(1)}, u32[]{:S(2)}, u32[]{:S(2)}) collective-permute-start(f32[128,384]{1,0:T(8,128)S(1)} %get-tuple-element.60), channel_id=1, source_target_pairs={{0,1},{1,0},{2,3},{3,2},{4,5},{5,4},{6,7},{7,6},{8,9},{9,8},{10,11... | collective-permute-start | bytes 589832 | tf_op jit(solution)/shard_map/ppermute | solution.py:287
  23.6 0.6 %collective-permute-done.6.refs_7_ = f32[384,128]{1,0:T(8,128)S(1)} collective-permute-done((f32[384,128]{1,0:T(8,128)S(1)}, f32[384,128]{1,0:T(8,128)S(1)}, u32[]{:S(2)}, u32[]{:S(2)}) %collective-permute-start.6) | collective-permute-done | bytes 196640 | tf_op jit(solution)/shard_map/ppermute | solution.py:282
  25.0 1.3 %shard_map.69 = (f32[128,128]{1,0:T(8,128)S(1)}, f32[128,128]{1,0:T(8,128)S(1)}, f32[128,128]{1,0:T(8,128)S(1)}, f32[128,128]{1,0:T(8,128)S(1)}, f32[192,128]{1,0:T(8,128)S(1)}, /*index=5*/f32[192,128]{1,0:T(8,128)S(1)}) custom-call(bf16[384,768]{1,0:T(8,128)(2,1)S(1)} %get-tuple-element.33.refs_0_, bf16[384,768]{1,0:T(8,128)(2,1)S(1)} %get-tuple-element.34.refs_1_, ...), custom_call_target="tpu_custom_call" | custom-call | tf_op jit(solution)/shard_map/pallas_call | solution.py:216
  26.6 2.5 %collective-permute-start.10 = (f32[128,128]{1,0:T(8,128)S(1)}, f32[128,128]{1,0:T(8,128)S(1)}, u32[]{:S(2)}, u32[]{:S(2)}) collective-permute-start(f32[128,128]{1,0:T(8,128)S(1)} %get-tuple-element.45), channel_id=1, source_target_pairs={{0,12},{4,8},{8,4},{12,0},{1,13},{5,9},{9,5},{13,1},{2,14},{6,10},... | collective-permute-start | bytes 196616 | tf_op jit(solution)/shard_map/ppermute | solution.py:293
  29.1 1.9 %collective-permute-start.9 = (f32[128,128]{1,0:T(8,128)S(1)}, f32[128,128]{1,0:T(8,128)S(1)}, u32[]{:S(2)}, u32[]{:S(2)}) collective-permute-start(f32[128,128]{1,0:T(8,128)S(1)} %get-tuple-element.44), channel_id=1, source_target_pairs={{0,4},{4,0},{8,12},{12,8},{1,5},{5,1},{9,13},{13,9},{2,6},{6,2},{1... | collective-permute-start | bytes 196616 | tf_op jit(solution)/shard_map/ppermute | solution.py:293
  31.0 0.6 %collective-permute-start.13 = (f32[96,128]{1,0:T(8,128)S(1)}, f32[96,128]{1,0:T(8,128)S(1)}, u32[]{:S(2)}, u32[]{:S(2)}) collective-permute-start(f32[96,128]{1,0:T(8,128)S(1)} %slice.18), channel_id=1, source_target_pairs={{0,2},{2,0},{1,3},{3,1},{4,6},{6,4},{5,7},{7,5},{8,10},{10,8},{9,1... | collective-permute-start | bytes 147464 | tf_op jit(solution)/shard_map/ppermute | solution.py:295
  31.6 1.5 %collective-permute-start.15 = (f32[96,128]{1,0:T(8,128)S(1)}, f32[96,128]{1,0:T(8,128)S(1)}, u32[]{:S(2)}, u32[]{:S(2)}) collective-permute-start(f32[96,128]{1,0:T(8,128)S(1)} %slice.20), channel_id=1, source_target_pairs={{0,2},{2,0},{1,3},{3,1},{4,6},{6,4},{5,7},{7,5},{8,10},{10,8},{9,1... | collective-permute-start | bytes 147464 | tf_op jit(solution)/shard_map/ppermute | solution.py:296
  33.5 2.1 %collective-permute-done.8 = f32[128,128]{1,0:T(8,128)S(1)} collective-permute-done((f32[128,128]{1,0:T(8,128)S(1)}, f32[128,128]{1,0:T(8,128)S(1)}, u32[]{:S(2)}, u32[]{:S(2)}) %collective-permute-start.8) | collective-permute-done | bytes 65568 | tf_op jit(solution)/shard_map/ppermute | solution.py:293
  35.6 0.9 %collective-permute-start.11 = (f32[128,128]{1,0:T(8,128)S(1)}, f32[128,128]{1,0:T(8,128)S(1)}, u32[]{:S(2)}, u32[]{:S(2)}) collective-permute-start(f32[128,128]{1,0:T(8,128)S(1)} %add_add_fusion.own), channel_id=1, source_target_pairs={{0,8},{4,12},{8,0},{12,4},{1,9},{5,13},{9,1},{13,5},{2,10},{6,14},... | collective-permute-start | bytes 196616 | tf_op jit(solution)/shard_map/ppermute | solution.py:299
  36.5 2.2 %collective-permute-start.12 = (f32[128,128]{1,0:T(8,128)S(1)}, f32[128,128]{1,0:T(8,128)S(1)}, u32[]{:S(2)}, u32[]{:S(2)}) collective-permute-start(f32[128,128]{1,0:T(8,128)S(1)} %add_add_fusion.own), channel_id=1, source_target_pairs={{0,12},{4,8},{8,4},{12,0},{1,13},{5,9},{9,5},{13,1},{2,14},{6,10},... | collective-permute-start | bytes 196616 | tf_op jit(solution)/shard_map/ppermute | solution.py:299
  38.7 0.4 collective-permute-start.16
  39.1 0.7 %shard_map.70 = f32[96,512]{1,0:T(8,128)} custom-call(f32[192,128]{1,0:T(8,128)S(1)} %get-tuple-element.46.own, f32[192,128]{1,0:T(8,128)S(1)} %collective-permute-done.14.near, f32[96,128]{1,0:T(8,128)S(1)} %collective-permute-done.13.across, f32[96,128]{1,0:T(8,128)S(1)} %collective-permute-done.15.far), custom_call_target="tpu_custom_call" | custom-call | tf_op jit(solution)/shard_map/pallas_call | solution.py:240
  39.8 3.8 %collective-permute-done.11.first = f32[128,128]{1,0:T(8,128)S(1)} collective-permute-done((f32[128,128]{1,0:T(8,128)S(1)}, f32[128,128]{1,0:T(8,128)S(1)}, u32[]{:S(2)}, u32[]{:S(2)}) %collective-permute-start.11) | collective-permute-done | bytes 65568 | tf_op jit(solution)/shard_map/ppermute | solution.py:299
  43.6 0.4 collective-permute-done.16.third
  44.0 0.8 %shard_map.71 = (f32[128,512]{1,0:T(8,128)}, f32[1,128]{1,0:T(1,128)}) custom-call(f32[128,128]{1,0:T(8,128)S(1)} %add_add_fusion.own, f32[128,128]{1,0:T(8,128)S(1)} %collective-permute-done.11.first, f32[128,128]{1,0:T(8,128)S(1)} %collective-permute-done.12.second, f32[128,128]{1,0:T(8,128)S(1)} %collective-permute-done.16.third, ...), custom_call_target="tpu_custom_call" | custom-call | tf_op jit(solution)/shard_map/pallas_call | solution.py:261
  (27 shorter events, 1.7 us)
Async XLA Ops:
  0.6 19.0 %copy-start.1 = (f32[384,512]{1,0:T(8,128)S(1)}, f32[384,512]{1,0:T(8,128)}, u32[]{:S(2)}) copy-start(f32[384,512]{1,0:T(8,128)} %refs_0_.1) | copy-start | bytes 2359300
  0.6 19.0 %copy-start = (f32[512,512]{1,0:T(8,128)S(1)}, f32[512,512]{1,0:T(8,128)}, u32[]{:S(2)}) copy-start(f32[512,512]{1,0:T(8,128)} %refs_1_.1) | copy-start | bytes 3145732
  3.6 16.1 %collective-permute-start = (f32[384,384]{1,0:T(8,128)}, f32[384,384]{1,0:T(8,128)S(1)}, u32[]{:S(2)}, u32[]{:S(2)}) collective-permute-start(f32[384,384]{1,0:T(8,128)} %get-tuple-element.32.refs_3_), channel_id=1, source_target_pairs={{0,1},{1,0},{2,3},{3,2},{4,5},{5,4},{6,7},{7,6},{8,9},{9,8},{10,11... | collective-permute-start | bytes 1769480 | tf_op jit(solution)/shard_map/ppermute | solution.py:280
  4.1 18.8 %collective-permute-start.1 = (f32[384,384]{1,0:T(8,128)}, f32[384,384]{1,0:T(8,128)S(1)}, u32[]{:S(2)}, u32[]{:S(2)}) collective-permute-start(f32[384,384]{1,0:T(8,128)} %get-tuple-element.32.refs_3_), channel_id=1, source_target_pairs={{0,2},{2,0},{1,3},{3,1},{4,6},{6,4},{5,7},{7,5},{8,10},{10,8},{9,1... | collective-permute-start | bytes 1769480 | tf_op jit(solution)/shard_map/ppermute | solution.py:279
  6.7 9.8 %collective-permute-start.5 = (f32[384,128]{1,0:T(8,128)}, f32[384,128]{1,0:T(8,128)S(1)}, u32[]{:S(2)}, u32[]{:S(2)}) collective-permute-start(f32[384,128]{1,0:T(8,128)} %get-tuple-element.31.refs_2_), channel_id=1, source_target_pairs={{0,12},{4,8},{8,4},{12,0},{1,13},{5,9},{9,5},{13,1},{2,14},{6,10},... | collective-permute-start | bytes 589832 | tf_op jit(solution)/shard_map/ppermute | solution.py:281
  10.3 13.3 %collective-permute-start.7 = (f32[384,128]{1,0:T(8,128)}, f32[384,128]{1,0:T(8,128)S(1)}, u32[]{:S(2)}, u32[]{:S(2)}) collective-permute-start(f32[384,128]{1,0:T(8,128)} %get-tuple-element.31.refs_2_), channel_id=1, source_target_pairs={{0,4},{4,0},{8,12},{12,8},{1,5},{5,1},{9,13},{13,9},{2,6},{6,2},{1... | collective-permute-start | bytes 589832 | tf_op jit(solution)/shard_map/ppermute | solution.py:281
  16.5 7.8 %collective-permute-start.6 = (f32[384,128]{1,0:T(8,128)S(1)}, f32[384,128]{1,0:T(8,128)S(1)}, u32[]{:S(2)}, u32[]{:S(2)}) collective-permute-start(f32[384,128]{1,0:T(8,128)S(1)} %collective-permute-done.5.refs_8_), channel_id=1, source_target_pairs={{0,4},{4,0},{8,12},{12,8},{1,5},{5,1},{9,13},{13,9},{2,6},{6,2},{1... | collective-permute-start | bytes 589832 | tf_op jit(solution)/shard_map/ppermute | solution.py:282
  19.7 1.1 %copy-start.2 = (f32[384,384]{1,0:T(8,128)S(1)}, f32[384,384]{1,0:T(8,128)}, u32[]{:S(2)}) copy-start(f32[384,384]{1,0:T(8,128)} %get-tuple-element.32.refs_3_) | copy-start | bytes 1769476
  20.7 0.9 %copy-start.3 = (f32[384,128]{1,0:T(8,128)S(1)}, f32[384,128]{1,0:T(8,128)}, u32[]{:S(2)}) copy-start(f32[384,128]{1,0:T(8,128)} %get-tuple-element.31.refs_2_) | copy-start | bytes 589828
  23.0 1.5 %collective-permute-start.2 = (f32[128,384]{1,0:T(8,128)S(1)}, f32[128,384]{1,0:T(8,128)S(1)}, u32[]{:S(2)}, u32[]{:S(2)}) collective-permute-start(f32[128,384]{1,0:T(8,128)S(1)} %get-tuple-element.61), channel_id=1, source_target_pairs={{0,1},{1,0},{2,3},{3,2},{4,5},{5,4},{6,7},{7,6},{8,9},{9,8},{10,11... | collective-permute-start | bytes 589832 | tf_op jit(solution)/shard_map/ppermute | solution.py:287
  23.1 1.7 %collective-permute-start.3 = (f32[128,384]{1,0:T(8,128)S(1)}, f32[128,384]{1,0:T(8,128)S(1)}, u32[]{:S(2)}, u32[]{:S(2)}) collective-permute-start(f32[128,384]{1,0:T(8,128)S(1)} %get-tuple-element.60), channel_id=1, source_target_pairs={{0,1},{1,0},{2,3},{3,2},{4,5},{5,4},{6,7},{7,6},{8,9},{9,8},{10,11... | collective-permute-start | bytes 589832 | tf_op jit(solution)/shard_map/ppermute | solution.py:287
  23.6 1.5 %collective-permute-start.4 = (f32[128,384]{1,0:T(8,128)S(1)}, f32[128,384]{1,0:T(8,128)S(1)}, u32[]{:S(2)}, u32[]{:S(2)}) collective-permute-start(f32[128,384]{1,0:T(8,128)S(1)} %get-tuple-element.59), channel_id=1, source_target_pairs={{0,1},{1,0},{2,3},{3,2},{4,5},{5,4},{6,7},{7,6},{8,9},{9,8},{10,11... | collective-permute-start | bytes 589832 | tf_op jit(solution)/shard_map/ppermute | solution.py:287
  26.4 5.2 %collective-permute-start.14 = (f32[192,128]{1,0:T(8,128)S(1)}, f32[192,128]{1,0:T(8,128)S(1)}, u32[]{:S(2)}, u32[]{:S(2)}) collective-permute-start(f32[192,128]{1,0:T(8,128)S(1)} %get-tuple-element.47), channel_id=1, source_target_pairs={{0,1},{1,0},{2,3},{3,2},{4,5},{5,4},{6,7},{7,6},{8,9},{9,8},{10,11... | collective-permute-start | bytes 294920 | tf_op jit(solution)/shard_map/ppermute | solution.py:292
  26.6 6.8 %collective-permute-start.10 = (f32[128,128]{1,0:T(8,128)S(1)}, f32[128,128]{1,0:T(8,128)S(1)}, u32[]{:S(2)}, u32[]{:S(2)}) collective-permute-start(f32[128,128]{1,0:T(8,128)S(1)} %get-tuple-element.45), channel_id=1, source_target_pairs={{0,12},{4,8},{8,4},{12,0},{1,13},{5,9},{9,5},{13,1},{2,14},{6,10},... | collective-permute-start | bytes 196616 | tf_op jit(solution)/shard_map/ppermute | solution.py:293
  29.1 6.4 %collective-permute-start.8 = (f32[128,128]{1,0:T(8,128)S(1)}, f32[128,128]{1,0:T(8,128)S(1)}, u32[]{:S(2)}, u32[]{:S(2)}) collective-permute-start(f32[128,128]{1,0:T(8,128)S(1)} %get-tuple-element.43), channel_id=1, source_target_pairs={{0,8},{4,12},{8,0},{12,4},{1,9},{5,13},{9,1},{13,5},{2,10},{6,14},... | collective-permute-start | bytes 196616 | tf_op jit(solution)/shard_map/ppermute | solution.py:293
  29.1 6.4 %collective-permute-start.9 = (f32[128,128]{1,0:T(8,128)S(1)}, f32[128,128]{1,0:T(8,128)S(1)}, u32[]{:S(2)}, u32[]{:S(2)}) collective-permute-start(f32[128,128]{1,0:T(8,128)S(1)} %get-tuple-element.44), channel_id=1, source_target_pairs={{0,4},{4,0},{8,12},{12,8},{1,5},{5,1},{9,13},{13,9},{2,6},{6,2},{1... | collective-permute-start | bytes 196616 | tf_op jit(solution)/shard_map/ppermute | solution.py:293
  31.0 7.7 %collective-permute-start.13 = (f32[96,128]{1,0:T(8,128)S(1)}, f32[96,128]{1,0:T(8,128)S(1)}, u32[]{:S(2)}, u32[]{:S(2)}) collective-permute-start(f32[96,128]{1,0:T(8,128)S(1)} %slice.18), channel_id=1, source_target_pairs={{0,2},{2,0},{1,3},{3,1},{4,6},{6,4},{5,7},{7,5},{8,10},{10,8},{9,1... | collective-permute-start | bytes 147464 | tf_op jit(solution)/shard_map/ppermute | solution.py:295
  31.6 7.1 %collective-permute-start.15 = (f32[96,128]{1,0:T(8,128)S(1)}, f32[96,128]{1,0:T(8,128)S(1)}, u32[]{:S(2)}, u32[]{:S(2)}) collective-permute-start(f32[96,128]{1,0:T(8,128)S(1)} %slice.20), channel_id=1, source_target_pairs={{0,2},{2,0},{1,3},{3,1},{4,6},{6,4},{5,7},{7,5},{8,10},{10,8},{9,1... | collective-permute-start | bytes 147464 | tf_op jit(solution)/shard_map/ppermute | solution.py:296
  35.6 8.0 %collective-permute-start.11 = (f32[128,128]{1,0:T(8,128)S(1)}, f32[128,128]{1,0:T(8,128)S(1)}, u32[]{:S(2)}, u32[]{:S(2)}) collective-permute-start(f32[128,128]{1,0:T(8,128)S(1)} %add_add_fusion.own), channel_id=1, source_target_pairs={{0,8},{4,12},{8,0},{12,4},{1,9},{5,13},{9,1},{13,5},{2,10},{6,14},... | collective-permute-start | bytes 196616 | tf_op jit(solution)/shard_map/ppermute | solution.py:299
  36.5 7.1 %collective-permute-start.12 = (f32[128,128]{1,0:T(8,128)S(1)}, f32[128,128]{1,0:T(8,128)S(1)}, u32[]{:S(2)}, u32[]{:S(2)}) collective-permute-start(f32[128,128]{1,0:T(8,128)S(1)} %add_add_fusion.own), channel_id=1, source_target_pairs={{0,12},{4,8},{8,4},{12,0},{1,13},{5,9},{9,5},{13,1},{2,14},{6,10},... | collective-permute-start | bytes 196616 | tf_op jit(solution)/shard_map/ppermute | solution.py:299
  38.7 5.3 %collective-permute-start.16 = (f32[128,128]{1,0:T(8,128)S(1)}, f32[128,128]{1,0:T(8,128)S(1)}, u32[]{:S(2)}, u32[]{:S(2)}) collective-permute-start(f32[128,128]{1,0:T(8,128)S(1)} %add_add_fusion.own), channel_id=1, source_target_pairs={{0,4},{4,0},{8,12},{12,8},{1,5},{5,1},{9,13},{13,9},{2,6},{6,2},{1... | collective-permute-start | bytes 196616 | tf_op jit(solution)/shard_map/ppermute | solution.py:299

commit v5 on v4

--- a/solution.py
+++ b/solution.py
@@ -7,7 +7,6 @@
 
 TILE = 128
 ORDER = (2, 3, 1)
-NS = 7
 VMEM = pl.BlockSpec(memory_space=pltpu.VMEM)
 ANY = pl.BlockSpec(memory_space=pl.ANY)
 PARAMS = pltpu.CompilerParams(vmem_limit_bytes=16 * 1024 * 1024)
@@ -119,7 +118,10 @@
         copy.start()
     fetch[1].wait()
     fetch[2].wait()
-    white_ref[...] = dot3(split(panel[...]), split(inverse[...]))
+    high, low = split(panel[...])
+    parts = split(inverse[...])
+    wide = dot(high, jnp.concatenate(parts, axis=1))
+    white_ref[...] = wide[:, :TILE] + (wide[:, TILE:] + dot(low, parts[0]))
     for copy in picks:
         copy.wait()
 
@@ -248,7 +250,7 @@
 
 def diagonal_kernel(own, first, second, third, base_ref, out_ref, variances_ref):
     row, member = lax.axis_index("row"), lax.axis_index(("col", "rep"))
-    for j, ref in zip((0,) + (2, 3, 1), (own, first, second, third)):
+    for j, ref in zip((0,) + ORDER, (own, first, second, third)):
         columns = pl.ds(pl.multiple_of((row ^ j) * TILE, TILE), TILE)
         out_ref[:, columns] = base_ref[:, columns] + ref[...]
     square = out_ref[:, pl.ds(pl.multiple_of(member * TILE, TILE), TILE)]
@@ -296,7 +298,8 @@
     far = lax.ppermute(near[count:], "col", SWAP)
     block = terms[0] + got[0] + got[1] + got[2]
     again, across, far = lax.optimization_barrier((block, across, far))
-    blocks = [block] + [lax.ppermute(block, "row", rows_apart(j)) for j in (2, 3)] + [lax.ppermute(again, "row", rows_apart(1))]
+    sent = zip(ORDER, (block, block, again))
+    blocks = [block] + [lax.ppermute(x, "row", rows_apart(j)) for j, x in sent]
     sigma_rows = rows_of(mine, near, across, far)
     blocks, sigma_rows = lax.optimization_barrier((blocks, sigma_rows))
     sigma_diag, variances = diagonal(blocks, base)
@@ -308,7 +311,7 @@
 
     def per_device(sep_inverse, row_tiles, panel_rows, diag_inverse):
         square = (shape["row"], shape["col"], shape["rep"]) == (4, 2, 2)
-        fits = diag_inverse.shape == (4 * TILE, 4 * TILE) and panel_rows.shape[0] % TILE == 0
+        fits = diag_inverse.shape == (4 * TILE, 4 * TILE) and panel_rows.shape[0] % (3 * TILE) == 0
         form = four_by_four if square and fits else any_mesh
         return form(sep_inverse, row_tiles, panel_rows, diag_inverse)
 

time: 45 us -> 45 us (level)
  no operation moved by 1% of the time
where the time goes in v5:
time: 45 us; the launch traced here: 44.8 us
  starting transfers between devices  20.8 us (46%)
  waiting for transfers between devices  14.2 us (32%)
  Pallas kernels  6.94 us (15%)
  local copies, waits for them, and re-layouts  2.04 us (5%)
  between operations  0.73 us (2%)
    ppermute x2, waiting for transfers between devices, four_by_four(): whites = {j: lax.ppermute(quarter, 'row', rows_apart(j)) for j in (3, 1)}  6.19 us
    ppermute x3, starting transfers between devices, four_by_four(): got = [lax.ppermute(terms[j], 'row', rows_apart(j)) for j in (2, 1, 3)]  4.39 us
    ppermute x3, waiting for transfers between devices, four_by_four(): blocks = [block] + [lax.ppermute(x, 'row', rows_apart(j)) for j, x in sent]  4.21 us
    ppermute x2, starting transfers between devices, four_by_four(): whites = {j: lax.ppermute(quarter, 'row', rows_apart(j)) for j in (3, 1)}  3.6 us
    ppermute x3, starting transfers between devices, four_by_four(): blocks = [block] + [lax.ppermute(x, 'row', rows_apart(j)) for j, x in sent]  3.56 us
    ppermute x1, starting transfers between devices, four_by_four(): whites[2] = lax.ppermute(whites[3], 'row', rows_apart(1))  3.18 us
    pallas_call x1, Pallas kernels, first(): pl.pallas_call(first_kernel, out_shape=(f32(panel_rows.shape[0], TILE), f...  2.94 us
    ppermute x1, starting transfers between devices, four_by_four(): across = lax.ppermute(own, 'col', SWAP)  2.56 us
  transfers between devices with their start and end apart: 17, of which 9 were waited for; matrix products, arithmetic and copies ran while one was open for 0% of the time, Pallas kernels for 4%

profile of v5, /device:TPU:0, one launch (start us, length us, event | category | flops | bytes accessed | tf_op | source)
XLA Modules:
  0.0 44.8 jit_solution(2996293367333729671)
XLA Ops:
  0.7 2.9 %shard_map.67 = (f32[384,128]{1,0:T(8,128)}, f32[384,384]{1,0:T(8,128)}) custom-call(s32[12]{0:T(128)} %tiles_hbm.1, f32[768,768]{1,0:T(8,128)} %sep_hbm.1, f32[384,512]{1,0:T(8,128)} %refs_0_.1, f32[512,512]{1,0:T(8,128)} %refs_1_.1), custom_call_target="tpu_custom_call" | custom-call | tf_op jit(solution)/shard_map/pallas_call | solution.py:131
  3.6 0.5 %collective-permute-start = (f32[384,384]{1,0:T(8,128)}, f32[384,384]{1,0:T(8,128)S(1)}, u32[]{:S(2)}, u32[]{:S(2)}) collective-permute-start(f32[384,384]{1,0:T(8,128)} %get-tuple-element.32.refs_3_), channel_id=1, source_target_pairs={{0,1},{1,0},{2,3},{3,2},{4,5},{5,4},{6,7},{7,6},{8,9},{9,8},{10,11... | collective-permute-start | bytes 1769480 | tf_op jit(solution)/shard_map/ppermute | solution.py:282
  4.1 2.6 %collective-permute-start.1 = (f32[384,384]{1,0:T(8,128)}, f32[384,384]{1,0:T(8,128)S(1)}, u32[]{:S(2)}, u32[]{:S(2)}) collective-permute-start(f32[384,384]{1,0:T(8,128)} %get-tuple-element.32.refs_3_), channel_id=1, source_target_pairs={{0,2},{2,0},{1,3},{3,1},{4,6},{6,4},{5,7},{7,5},{8,10},{10,8},{9,1... | collective-permute-start | bytes 1769480 | tf_op jit(solution)/shard_map/ppermute | solution.py:281
  6.7 3.6 %collective-permute-start.5 = (f32[384,128]{1,0:T(8,128)}, f32[384,128]{1,0:T(8,128)S(1)}, u32[]{:S(2)}, u32[]{:S(2)}) collective-permute-start(f32[384,128]{1,0:T(8,128)} %get-tuple-element.31.refs_2_), channel_id=1, source_target_pairs={{0,12},{4,8},{8,4},{12,0},{1,13},{5,9},{9,5},{13,1},{2,14},{6,10},... | collective-permute-start | bytes 589832 | tf_op jit(solution)/shard_map/ppermute | solution.py:283
  10.3 6.2 %collective-permute-done.5.refs_8_ = f32[384,128]{1,0:T(8,128)S(1)} collective-permute-done((f32[384,128]{1,0:T(8,128)}, f32[384,128]{1,0:T(8,128)S(1)}, u32[]{:S(2)}, u32[]{:S(2)}) %collective-permute-start.5) | collective-permute-done | bytes 196640 | tf_op jit(solution)/shard_map/ppermute | solution.py:283
  16.5 3.2 %collective-permute-start.6 = (f32[384,128]{1,0:T(8,128)S(1)}, f32[384,128]{1,0:T(8,128)S(1)}, u32[]{:S(2)}, u32[]{:S(2)}) collective-permute-start(f32[384,128]{1,0:T(8,128)S(1)} %collective-permute-done.5.refs_8_), channel_id=1, source_target_pairs={{0,4},{4,0},{8,12},{12,8},{1,5},{5,1},{9,13},{13,9},{2,6},{6,2},{1... | collective-permute-start | bytes 589832 | tf_op jit(solution)/shard_map/ppermute | solution.py:284
  19.7 1.1 %copy-done.2 = f32[384,384]{1,0:T(8,128)S(1)} copy-done((f32[384,384]{1,0:T(8,128)S(1)}, f32[384,384]{1,0:T(8,128)}, u32[]{:S(2)}) %copy-start.2) | copy-done | bytes 589848
  20.7 0.9 %copy-done.3 = f32[384,128]{1,0:T(8,128)S(1)} copy-done((f32[384,128]{1,0:T(8,128)S(1)}, f32[384,128]{1,0:T(8,128)}, u32[]{:S(2)}) %copy-start.3) | copy-done | bytes 196632
  21.7 1.2 %shard_map.68 = (bf16[384,512]{1,0:T(8,128)(2,1)S(1)}, bf16[384,512]{1,0:T(8,128)(2,1)S(1)}, f32[128,512]{1,0:T(8,128)S(1)}, bf16[384,256]{1,0:T(8,128)(2,1)S(1)...) custom-call(f32[384,512]{1,0:T(8,128)S(1)} %copy-done.1, f32[512,512]{1,0:T(8,128)S(1)} %copy-done, ...), custom_call_target="tpu_custom_call" | custom-call | tf_op jit(solution)/shard_map/pallas_call | solution.py:164
  23.1 0.5 %collective-permute-start.3 = (f32[128,384]{1,0:T(8,128)S(1)}, f32[128,384]{1,0:T(8,128)S(1)}, u32[]{:S(2)}, u32[]{:S(2)}) collective-permute-start(f32[128,384]{1,0:T(8,128)S(1)} %get-tuple-element.60), channel_id=1, source_target_pairs={{0,1},{1,0},{2,3},{3,2},{4,5},{5,4},{6,7},{7,6},{8,9},{9,8},{10,11... | collective-permute-start | bytes 589832 | tf_op jit(solution)/shard_map/ppermute | solution.py:289
  23.6 0.6 %collective-permute-done.6.refs_7_ = f32[384,128]{1,0:T(8,128)S(1)} collective-permute-done((f32[384,128]{1,0:T(8,128)S(1)}, f32[384,128]{1,0:T(8,128)S(1)}, u32[]{:S(2)}, u32[]{:S(2)}) %collective-permute-start.6) | collective-permute-done | bytes 196640 | tf_op jit(solution)/shard_map/ppermute | solution.py:284
  25.0 1.3 %shard_map.69 = (f32[128,128]{1,0:T(8,128)S(1)}, f32[128,128]{1,0:T(8,128)S(1)}, f32[128,128]{1,0:T(8,128)S(1)}, f32[128,128]{1,0:T(8,128)S(1)}, f32[192,128]{1,0:T(8,128)S(1)}, /*index=5*/f32[192,128]{1,0:T(8,128)S(1)}) custom-call(bf16[384,768]{1,0:T(8,128)(2,1)S(1)} %get-tuple-element.33.refs_0_, bf16[384,768]{1,0:T(8,128)(2,1)S(1)} %get-tuple-element.34.refs_1_, ...), custom_call_target="tpu_custom_call" | custom-call | tf_op jit(solution)/shard_map/pallas_call | solution.py:218
  26.6 2.5 %collective-permute-start.10 = (f32[128,128]{1,0:T(8,128)S(1)}, f32[128,128]{1,0:T(8,128)S(1)}, u32[]{:S(2)}, u32[]{:S(2)}) collective-permute-start(f32[128,128]{1,0:T(8,128)S(1)} %get-tuple-element.45), channel_id=1, source_target_pairs={{0,12},{4,8},{8,4},{12,0},{1,13},{5,9},{9,5},{13,1},{2,14},{6,10},... | collective-permute-start | bytes 196616 | tf_op jit(solution)/shard_map/ppermute | solution.py:295
  29.1 1.9 %collective-permute-start.9 = (f32[128,128]{1,0:T(8,128)S(1)}, f32[128,128]{1,0:T(8,128)S(1)}, u32[]{:S(2)}, u32[]{:S(2)}) collective-permute-start(f32[128,128]{1,0:T(8,128)S(1)} %get-tuple-element.44), channel_id=1, source_target_pairs={{0,4},{4,0},{8,12},{12,8},{1,5},{5,1},{9,13},{13,9},{2,6},{6,2},{1... | collective-permute-start | bytes 196616 | tf_op jit(solution)/shard_map/ppermute | solution.py:295
  31.0 0.6 %collective-permute-start.13 = (f32[96,128]{1,0:T(8,128)S(1)}, f32[96,128]{1,0:T(8,128)S(1)}, u32[]{:S(2)}, u32[]{:S(2)}) collective-permute-start(f32[96,128]{1,0:T(8,128)S(1)} %slice.18), channel_id=1, source_target_pairs={{0,2},{2,0},{1,3},{3,1},{4,6},{6,4},{5,7},{7,5},{8,10},{10,8},{9,1... | collective-permute-start | bytes 147464 | tf_op jit(solution)/shard_map/ppermute | solution.py:297
  31.6 1.5 %collective-permute-start.15 = (f32[96,128]{1,0:T(8,128)S(1)}, f32[96,128]{1,0:T(8,128)S(1)}, u32[]{:S(2)}, u32[]{:S(2)}) collective-permute-start(f32[96,128]{1,0:T(8,128)S(1)} %slice.20), channel_id=1, source_target_pairs={{0,2},{2,0},{1,3},{3,1},{4,6},{6,4},{5,7},{7,5},{8,10},{10,8},{9,1... | collective-permute-start | bytes 147464 | tf_op jit(solution)/shard_map/ppermute | solution.py:298
  33.5 2.1 %collective-permute-done.8 = f32[128,128]{1,0:T(8,128)S(1)} collective-permute-done((f32[128,128]{1,0:T(8,128)S(1)}, f32[128,128]{1,0:T(8,128)S(1)}, u32[]{:S(2)}, u32[]{:S(2)}) %collective-permute-start.8) | collective-permute-done | bytes 65568 | tf_op jit(solution)/shard_map/ppermute | solution.py:295
  35.6 0.9 %collective-permute-start.11 = (f32[128,128]{1,0:T(8,128)S(1)}, f32[128,128]{1,0:T(8,128)S(1)}, u32[]{:S(2)}, u32[]{:S(2)}) collective-permute-start(f32[128,128]{1,0:T(8,128)S(1)} %add_add_fusion.own), channel_id=1, source_target_pairs={{0,8},{4,12},{8,0},{12,4},{1,9},{5,13},{9,1},{13,5},{2,10},{6,14},... | collective-permute-start | bytes 196616 | tf_op jit(solution)/shard_map/ppermute | solution.py:302
  36.5 2.2 %collective-permute-start.12 = (f32[128,128]{1,0:T(8,128)S(1)}, f32[128,128]{1,0:T(8,128)S(1)}, u32[]{:S(2)}, u32[]{:S(2)}) collective-permute-start(f32[128,128]{1,0:T(8,128)S(1)} %add_add_fusion.own), channel_id=1, source_target_pairs={{0,12},{4,8},{8,4},{12,0},{1,13},{5,9},{9,5},{13,1},{2,14},{6,10},... | collective-permute-start | bytes 196616 | tf_op jit(solution)/shard_map/ppermute | solution.py:302
  38.7 0.4 collective-permute-start.16
  39.1 0.7 %shard_map.70 = f32[96,512]{1,0:T(8,128)} custom-call(f32[192,128]{1,0:T(8,128)S(1)} %get-tuple-element.46.own, f32[192,128]{1,0:T(8,128)S(1)} %collective-permute-done.14.near, f32[96,128]{1,0:T(8,128)S(1)} %collective-permute-done.13.across, f32[96,128]{1,0:T(8,128)S(1)} %collective-permute-done.15.far), custom_call_target="tpu_custom_call" | custom-call | tf_op jit(solution)/shard_map/pallas_call | solution.py:242
  39.8 3.8 %collective-permute-done.11.first = f32[128,128]{1,0:T(8,128)S(1)} collective-permute-done((f32[128,128]{1,0:T(8,128)S(1)}, f32[128,128]{1,0:T(8,128)S(1)}, u32[]{:S(2)}, u32[]{:S(2)}) %collective-permute-start.11) | collective-permute-done | bytes 65568 | tf_op jit(solution)/shard_map/ppermute | solution.py:302
  43.6 0.4 collective-permute-done.16.third
  44.0 0.8 %shard_map.71 = (f32[128,512]{1,0:T(8,128)}, f32[1,128]{1,0:T(1,128)}) custom-call(f32[128,128]{1,0:T(8,128)S(1)} %add_add_fusion.own, f32[128,128]{1,0:T(8,128)S(1)} %collective-permute-done.11.first, f32[128,128]{1,0:T(8,128)S(1)} %collective-permute-done.12.second, f32[128,128]{1,0:T(8,128)S(1)} %collective-permute-done.16.third, ...), custom_call_target="tpu_custom_call" | custom-call | tf_op jit(solution)/shard_map/pallas_call | solution.py:263
  (27 shorter events, 1.7 us)
Async XLA Ops:
  0.6 19.0 %copy-start.1 = (f32[384,512]{1,0:T(8,128)S(1)}, f32[384,512]{1,0:T(8,128)}, u32[]{:S(2)}) copy-start(f32[384,512]{1,0:T(8,128)} %refs_0_.1) | copy-start | bytes 2359300
  0.6 19.0 %copy-start = (f32[512,512]{1,0:T(8,128)S(1)}, f32[512,512]{1,0:T(8,128)}, u32[]{:S(2)}) copy-start(f32[512,512]{1,0:T(8,128)} %refs_1_.1) | copy-start | bytes 3145732
  3.6 16.1 %collective-permute-start = (f32[384,384]{1,0:T(8,128)}, f32[384,384]{1,0:T(8,128)S(1)}, u32[]{:S(2)}, u32[]{:S(2)}) collective-permute-start(f32[384,384]{1,0:T(8,128)} %get-tuple-element.32.refs_3_), channel_id=1, source_target_pairs={{0,1},{1,0},{2,3},{3,2},{4,5},{5,4},{6,7},{7,6},{8,9},{9,8},{10,11... | collective-permute-start | bytes 1769480 | tf_op jit(solution)/shard_map/ppermute | solution.py:282
  4.1 18.8 %collective-permute-start.1 = (f32[384,384]{1,0:T(8,128)}, f32[384,384]{1,0:T(8,128)S(1)}, u32[]{:S(2)}, u32[]{:S(2)}) collective-permute-start(f32[384,384]{1,0:T(8,128)} %get-tuple-element.32.refs_3_), channel_id=1, source_target_pairs={{0,2},{2,0},{1,3},{3,1},{4,6},{6,4},{5,7},{7,5},{8,10},{10,8},{9,1... | collective-permute-start | bytes 1769480 | tf_op jit(solution)/shard_map/ppermute | solution.py:281
  6.7 9.8 %collective-permute-start.5 = (f32[384,128]{1,0:T(8,128)}, f32[384,128]{1,0:T(8,128)S(1)}, u32[]{:S(2)}, u32[]{:S(2)}) collective-permute-start(f32[384,128]{1,0:T(8,128)} %get-tuple-element.31.refs_2_), channel_id=1, source_target_pairs={{0,12},{4,8},{8,4},{12,0},{1,13},{5,9},{9,5},{13,1},{2,14},{6,10},... | collective-permute-start | bytes 589832 | tf_op jit(solution)/shard_map/ppermute | solution.py:283
  10.3 13.3 %collective-permute-start.7 = (f32[384,128]{1,0:T(8,128)}, f32[384,128]{1,0:T(8,128)S(1)}, u32[]{:S(2)}, u32[]{:S(2)}) collective-permute-start(f32[384,128]{1,0:T(8,128)} %get-tuple-element.31.refs_2_), channel_id=1, source_target_pairs={{0,4},{4,0},{8,12},{12,8},{1,5},{5,1},{9,13},{13,9},{2,6},{6,2},{1... | collective-permute-start | bytes 589832 | tf_op jit(solution)/shard_map/ppermute | solution.py:283
  16.5 7.8 %collective-permute-start.6 = (f32[384,128]{1,0:T(8,128)S(1)}, f32[384,128]{1,0:T(8,128)S(1)}, u32[]{:S(2)}, u32[]{:S(2)}) collective-permute-start(f32[384,128]{1,0:T(8,128)S(1)} %collective-permute-done.5.refs_8_), channel_id=1, source_target_pairs={{0,4},{4,0},{8,12},{12,8},{1,5},{5,1},{9,13},{13,9},{2,6},{6,2},{1... | collective-permute-start | bytes 589832 | tf_op jit(solution)/shard_map/ppermute | solution.py:284
  19.7 1.1 %copy-start.2 = (f32[384,384]{1,0:T(8,128)S(1)}, f32[384,384]{1,0:T(8,128)}, u32[]{:S(2)}) copy-start(f32[384,384]{1,0:T(8,128)} %get-tuple-element.32.refs_3_) | copy-start | bytes 1769476
  20.7 0.9 %copy-start.3 = (f32[384,128]{1,0:T(8,128)S(1)}, f32[384,128]{1,0:T(8,128)}, u32[]{:S(2)}) copy-start(f32[384,128]{1,0:T(8,128)} %get-tuple-element.31.refs_2_) | copy-start | bytes 589828
  23.0 1.5 %collective-permute-start.2 = (f32[128,384]{1,0:T(8,128)S(1)}, f32[128,384]{1,0:T(8,128)S(1)}, u32[]{:S(2)}, u32[]{:S(2)}) collective-permute-start(f32[128,384]{1,0:T(8,128)S(1)} %get-tuple-element.61), channel_id=1, source_target_pairs={{0,1},{1,0},{2,3},{3,2},{4,5},{5,4},{6,7},{7,6},{8,9},{9,8},{10,11... | collective-permute-start | bytes 589832 | tf_op jit(solution)/shard_map/ppermute | solution.py:289
  23.1 1.7 %collective-permute-start.3 = (f32[128,384]{1,0:T(8,128)S(1)}, f32[128,384]{1,0:T(8,128)S(1)}, u32[]{:S(2)}, u32[]{:S(2)}) collective-permute-start(f32[128,384]{1,0:T(8,128)S(1)} %get-tuple-element.60), channel_id=1, source_target_pairs={{0,1},{1,0},{2,3},{3,2},{4,5},{5,4},{6,7},{7,6},{8,9},{9,8},{10,11... | collective-permute-start | bytes 589832 | tf_op jit(solution)/shard_map/ppermute | solution.py:289
  23.6 1.5 %collective-permute-start.4 = (f32[128,384]{1,0:T(8,128)S(1)}, f32[128,384]{1,0:T(8,128)S(1)}, u32[]{:S(2)}, u32[]{:S(2)}) collective-permute-start(f32[128,384]{1,0:T(8,128)S(1)} %get-tuple-element.59), channel_id=1, source_target_pairs={{0,1},{1,0},{2,3},{3,2},{4,5},{5,4},{6,7},{7,6},{8,9},{9,8},{10,11... | collective-permute-start | bytes 589832 | tf_op jit(solution)/shard_map/ppermute | solution.py:289
  26.4 5.2 %collective-permute-start.14 = (f32[192,128]{1,0:T(8,128)S(1)}, f32[192,128]{1,0:T(8,128)S(1)}, u32[]{:S(2)}, u32[]{:S(2)}) collective-permute-start(f32[192,128]{1,0:T(8,128)S(1)} %get-tuple-element.47), channel_id=1, source_target_pairs={{0,1},{1,0},{2,3},{3,2},{4,5},{5,4},{6,7},{7,6},{8,9},{9,8},{10,11... | collective-permute-start | bytes 294920 | tf_op jit(solution)/shard_map/ppermute | solution.py:294
  26.6 6.8 %collective-permute-start.10 = (f32[128,128]{1,0:T(8,128)S(1)}, f32[128,128]{1,0:T(8,128)S(1)}, u32[]{:S(2)}, u32[]{:S(2)}) collective-permute-start(f32[128,128]{1,0:T(8,128)S(1)} %get-tuple-element.45), channel_id=1, source_target_pairs={{0,12},{4,8},{8,4},{12,0},{1,13},{5,9},{9,5},{13,1},{2,14},{6,10},... | collective-permute-start | bytes 196616 | tf_op jit(solution)/shard_map/ppermute | solution.py:295
  29.1 6.4 %collective-permute-start.8 = (f32[128,128]{1,0:T(8,128)S(1)}, f32[128,128]{1,0:T(8,128)S(1)}, u32[]{:S(2)}, u32[]{:S(2)}) collective-permute-start(f32[128,128]{1,0:T(8,128)S(1)} %get-tuple-element.43), channel_id=1, source_target_pairs={{0,8},{4,12},{8,0},{12,4},{1,9},{5,13},{9,1},{13,5},{2,10},{6,14},... | collective-permute-start | bytes 196616 | tf_op jit(solution)/shard_map/ppermute | solution.py:295
  29.1 6.4 %collective-permute-start.9 = (f32[128,128]{1,0:T(8,128)S(1)}, f32[128,128]{1,0:T(8,128)S(1)}, u32[]{:S(2)}, u32[]{:S(2)}) collective-permute-start(f32[128,128]{1,0:T(8,128)S(1)} %get-tuple-element.44), channel_id=1, source_target_pairs={{0,4},{4,0},{8,12},{12,8},{1,5},{5,1},{9,13},{13,9},{2,6},{6,2},{1... | collective-permute-start | bytes 196616 | tf_op jit(solution)/shard_map/ppermute | solution.py:295
  31.0 7.7 %collective-permute-start.13 = (f32[96,128]{1,0:T(8,128)S(1)}, f32[96,128]{1,0:T(8,128)S(1)}, u32[]{:S(2)}, u32[]{:S(2)}) collective-permute-start(f32[96,128]{1,0:T(8,128)S(1)} %slice.18), channel_id=1, source_target_pairs={{0,2},{2,0},{1,3},{3,1},{4,6},{6,4},{5,7},{7,5},{8,10},{10,8},{9,1... | collective-permute-start | bytes 147464 | tf_op jit(solution)/shard_map/ppermute | solution.py:297
  31.6 7.1 %collective-permute-start.15 = (f32[96,128]{1,0:T(8,128)S(1)}, f32[96,128]{1,0:T(8,128)S(1)}, u32[]{:S(2)}, u32[]{:S(2)}) collective-permute-start(f32[96,128]{1,0:T(8,128)S(1)} %slice.20), channel_id=1, source_target_pairs={{0,2},{2,0},{1,3},{3,1},{4,6},{6,4},{5,7},{7,5},{8,10},{10,8},{9,1... | collective-permute-start | bytes 147464 | tf_op jit(solution)/shard_map/ppermute | solution.py:298
  35.6 8.0 %collective-permute-start.11 = (f32[128,128]{1,0:T(8,128)S(1)}, f32[128,128]{1,0:T(8,128)S(1)}, u32[]{:S(2)}, u32[]{:S(2)}) collective-permute-start(f32[128,128]{1,0:T(8,128)S(1)} %add_add_fusion.own), channel_id=1, source_target_pairs={{0,8},{4,12},{8,0},{12,4},{1,9},{5,13},{9,1},{13,5},{2,10},{6,14},... | collective-permute-start | bytes 196616 | tf_op jit(solution)/shard_map/ppermute | solution.py:302
  36.5 7.1 %collective-permute-start.12 = (f32[128,128]{1,0:T(8,128)S(1)}, f32[128,128]{1,0:T(8,128)S(1)}, u32[]{:S(2)}, u32[]{:S(2)}) collective-permute-start(f32[128,128]{1,0:T(8,128)S(1)} %add_add_fusion.own), channel_id=1, source_target_pairs={{0,12},{4,8},{8,4},{12,0},{1,13},{5,9},{9,5},{13,1},{2,14},{6,10},... | collective-permute-start | bytes 196616 | tf_op jit(solution)/shard_map/ppermute | solution.py:302
  38.7 5.3 %collective-permute-start.16 = (f32[128,128]{1,0:T(8,128)S(1)}, f32[128,128]{1,0:T(8,128)S(1)}, u32[]{:S(2)}, u32[]{:S(2)}) collective-permute-start(f32[128,128]{1,0:T(8,128)S(1)} %add_add_fusion.own), channel_id=1, source_target_pairs={{0,4},{4,0},{8,12},{12,8},{1,5},{5,1},{9,13},{13,9},{2,6},{6,2},{1... | collective-permute-start | bytes 196616 | tf_op jit(solution)/shard_map/ppermute | solution.py:302

commit v6 on v5

--- a/solution.py
+++ b/solution.py
@@ -86,8 +86,9 @@
 
 
 def first_kernel(
-    tiles_hbm, sep_hbm, panel_hbm, inverse_hbm, white_ref, picked_ref, tiles, panel, inverse, sems
+    tiles_hbm, sep_hbm, panel_hbm, inverse_hbm, white_hbm, picked_hbm, *scratch
 ):
+    tiles, panel, inverse, white_ref, picked_ref, sems, out_sems = scratch
     row, member = lax.axis_index("row"), lax.axis_index(("col", "rep"))
     columns = pl.ds(pl.multiple_of(member * TILE, TILE), TILE)
     slots, block = picked_ref.shape[0] // TILE, sep_hbm.shape[0] // TILE
@@ -122,7 +123,17 @@
     parts = split(inverse[...])
     wide = dot(high, jnp.concatenate(parts, axis=1))
     white_ref[...] = wide[:, :TILE] + (wide[:, TILE:] + dot(low, parts[0]))
-    for copy in picks:
+    out = [pltpu.make_async_copy(white_ref, white_hbm, out_sems.at[0])]
+    out[0].start()
+    for i in range(slots):
+        for copy in picks[i * slots : (i + 1) * slots]:
+            copy.wait()
+        rows = pl.ds(i * TILE, TILE)
+        out.append(
+            pltpu.make_async_copy(picked_ref.at[rows, :], picked_hbm.at[rows, :], out_sems.at[1 + i])
+        )
+        out[-1].start()
+    for copy in out:
         copy.wait()
 
 
@@ -132,12 +143,15 @@
         first_kernel,
         out_shape=(f32(panel_rows.shape[0], TILE), f32(slots * TILE, slots * TILE)),
         in_specs=[ANY] * 4,
-        out_specs=(VMEM, VMEM),
+        out_specs=(ANY, ANY),
         scratch_shapes=[
             pltpu.SMEM(row_tiles.shape, jnp.int32),
             pltpu.VMEM(panel_rows.shape, jnp.float32),
             pltpu.VMEM((diag_inverse.shape[0], TILE), jnp.float32),
+            pltpu.VMEM((panel_rows.shape[0], TILE), jnp.float32),
+            pltpu.VMEM((slots * TILE, slots * TILE), jnp.float32),
             pltpu.SemaphoreType.DMA((3 + slots * slots,)),
+            pltpu.SemaphoreType.DMA((1 + slots,)),
         ],
     )(row_tiles, sep_inverse, panel_rows, diag_inverse)
 
@@ -178,7 +192,7 @@
 
 
 def product_kernel(*refs):
-    sep_high, sep_low, across, quarter, *far = refs[:-15]
+    base, sep_high, sep_low, across, quarter, *far = refs[:-15]
     whites, (white_high, white_low) = refs[-15:-12], refs[-12:-10]
     terms, pieces, (joined, product, other_high, other_low) = refs[-10:-6], refs[-6:-4], refs[-4:]
     row, member = lax.axis_index("row"), lax.axis_index(("col", "rep"))
@@ -208,17 +222,19 @@
         value = full[:, :TILE]
         for n in range(1, 4):
             value = jnp.where((row ^ j) == n, full[:, n * TILE : (n + 1) * TILE], value)
+        if j == 0:
+            value += base[:, pl.ds(pl.multiple_of(row * TILE, TILE), TILE)]
         terms[j][...] = value
         mine = pl.ds(pl.multiple_of((member ^ j) * depth, 8), depth)
         pieces[j % 2][j // 2 * depth : (j // 2 + 1) * depth, :] = product[mine, :]
 
 
-def products(seps, across, quarter, far, whites, own_white):
+def products(base, seps, across, quarter, far, whites, own_white):
     depth, width = whites[0].shape
     return pl.pallas_call(
         product_kernel,
         out_shape=(f32(width, TILE),) * 4 + (f32(depth // 2, width),) * 2,
-        in_specs=[VMEM] * (9 + len(far)),
+        in_specs=[VMEM] * (10 + len(far)),
         out_specs=(VMEM,) * 6,
         scratch_shapes=[
             pltpu.VMEM((4 * depth, 2 * width), jnp.bfloat16),
@@ -227,7 +243,7 @@
             pltpu.VMEM((depth, 2 * depth), jnp.bfloat16),
         ],
         compiler_params=PARAMS,
-    )(*seps, across, quarter, *far, *whites, *own_white)
+    )(base, *seps, across, quarter, *far, *whites, *own_white)
 
 
 def rows_kernel(own, near, across, far, out_ref):
@@ -248,25 +264,25 @@
     )(own, near, across, far)
 
 
-def diagonal_kernel(own, first, second, third, base_ref, out_ref, variances_ref):
+def diagonal_kernel(own, first, second, third, out_ref, variances_ref):
     row, member = lax.axis_index("row"), lax.axis_index(("col", "rep"))
     for j, ref in zip((0,) + ORDER, (own, first, second, third)):
         columns = pl.ds(pl.multiple_of((row ^ j) * TILE, TILE), TILE)
-        out_ref[:, columns] = base_ref[:, columns] + ref[...]
+        out_ref[:, columns] = ref[...]
     square = out_ref[:, pl.ds(pl.multiple_of(member * TILE, TILE), TILE)]
     across = lax.broadcasted_iota(jnp.int32, square.shape, 0)
     down = lax.broadcasted_iota(jnp.int32, square.shape, 1)
     variances_ref[...] = jnp.sum(jnp.where(across == down, square, 0.0), axis=0, keepdims=True)
 
 
-def diagonal(blocks, base):
+def diagonal(blocks):
     return pl.pallas_call(
         diagonal_kernel,
-        out_shape=(f32(*base.shape), f32(1, TILE)),
-        in_specs=[VMEM] * 5,
+        out_shape=(f32(TILE, 4 * TILE), f32(1, TILE)),
+        in_specs=[VMEM] * 4,
         out_specs=(VMEM, VMEM),
         compiler_params=PARAMS,
-    )(*blocks, base)
+    )(*blocks)
 
 
 def rows_apart(j):
@@ -289,7 +305,7 @@
         lax.ppermute(lax.slice_in_dim(across, i * count, (i + 1) * count), "rep", SWAP)
         for i in range(3)
     ]
-    out = products(seps, across, split_quarter, far, [whites[j] for j in ORDER], own_white)
+    out = products(base, seps, across, split_quarter, far, [whites[j] for j in ORDER], own_white)
     terms, (mine, others) = out[:4], out[4:]
     near = lax.ppermute(others, "rep", SWAP)
     got = [lax.ppermute(terms[j], "row", rows_apart(j)) for j in (2, 1, 3)]
@@ -302,7 +318,7 @@
     blocks = [block] + [lax.ppermute(x, "row", rows_apart(j)) for j, x in sent]
     sigma_rows = rows_of(mine, near, across, far)
     blocks, sigma_rows = lax.optimization_barrier((blocks, sigma_rows))
-    sigma_diag, variances = diagonal(blocks, base)
+    sigma_diag, variances = diagonal(blocks)
     return sigma_rows, sigma_diag, variances.reshape(-1)
 
 

time: 45 us -> 44.8 us (level)
  no operation moved by 1% of the time
where the time goes in v6:
time: 44.8 us; the launch traced here: 44.6 us
  starting transfers between devices  20.8 us (46%)
  waiting for transfers between devices  14.2 us (32%)
  Pallas kernels  6.75 us (15%)
  local copies, waits for them, and re-layouts  2.04 us (5%)
  between operations  0.73 us (2%)
    ppermute x2, waiting for transfers between devices, four_by_four(): whites = {j: lax.ppermute(quarter, 'row', rows_apart(j)) for j in (3, 1)}  6.19 us
    ppermute x3, starting transfers between devices, four_by_four(): got = [lax.ppermute(terms[j], 'row', rows_apart(j)) for j in (2, 1, 3)]  4.39 us
    ppermute x3, waiting for transfers between devices, four_by_four(): blocks = [block] + [lax.ppermute(x, 'row', rows_apart(j)) for j, x in sent]  4.21 us
    ppermute x2, starting transfers between devices, four_by_four(): whites = {j: lax.ppermute(quarter, 'row', rows_apart(j)) for j in (3, 1)}  3.6 us
    ppermute x3, starting transfers between devices, four_by_four(): blocks = [block] + [lax.ppermute(x, 'row', rows_apart(j)) for j, x in sent]  3.56 us
    ppermute x1, starting transfers between devices, four_by_four(): whites[2] = lax.ppermute(whites[3], 'row', rows_apart(1))  3.18 us
    pallas_call x1, Pallas kernels, first(): pl.pallas_call(first_kernel, out_shape=(f32(panel_rows.shape[0], TILE), f...  2.76 us
    ppermute x1, starting transfers between devices, four_by_four(): across = lax.ppermute(own, 'col', SWAP)  2.56 us
  transfers between devices with their start and end apart: 17, of which 9 were waited for; matrix products, arithmetic and copies ran while one was open for 0% of the time, Pallas kernels for 4%

profile of v6, /device:TPU:0, one launch (start us, length us, event | category | flops | bytes accessed | tf_op | source)
XLA Modules:
  0.0 44.6 jit_solution(16371657556843286307)
XLA Ops:
  0.7 2.8 %shard_map.67 = (f32[384,128]{1,0:T(8,128)}, f32[384,384]{1,0:T(8,128)}) custom-call(s32[12]{0:T(128)} %tiles_hbm.1, f32[768,768]{1,0:T(8,128)} %sep_hbm.1, f32[384,512]{1,0:T(8,128)} %refs_0_.1, f32[512,512]{1,0:T(8,128)} %refs_1_.1), custom_call_target="tpu_custom_call" | custom-call | tf_op jit(solution)/shard_map/pallas_call | solution.py:142
  3.4 0.5 %collective-permute-start.1 = (f32[384,384]{1,0:T(8,128)}, f32[384,384]{1,0:T(8,128)S(1)}, u32[]{:S(2)}, u32[]{:S(2)}) collective-permute-start(f32[384,384]{1,0:T(8,128)} %get-tuple-element.31.refs_3_), channel_id=1, source_target_pairs={{0,1},{1,0},{2,3},{3,2},{4,5},{5,4},{6,7},{7,6},{8,9},{9,8},{10,11... | collective-permute-start | bytes 1769480 | tf_op jit(solution)/shard_map/ppermute | solution.py:298
  3.9 2.6 %collective-permute-start = (f32[384,384]{1,0:T(8,128)}, f32[384,384]{1,0:T(8,128)S(1)}, u32[]{:S(2)}, u32[]{:S(2)}) collective-permute-start(f32[384,384]{1,0:T(8,128)} %get-tuple-element.31.refs_3_), channel_id=1, source_target_pairs={{0,2},{2,0},{1,3},{3,1},{4,6},{6,4},{5,7},{7,5},{8,10},{10,8},{9,1... | collective-permute-start | bytes 1769480 | tf_op jit(solution)/shard_map/ppermute | solution.py:297
  6.5 3.6 %collective-permute-start.5 = (f32[384,128]{1,0:T(8,128)}, f32[384,128]{1,0:T(8,128)S(1)}, u32[]{:S(2)}, u32[]{:S(2)}) collective-permute-start(f32[384,128]{1,0:T(8,128)} %get-tuple-element.32.refs_2_), channel_id=1, source_target_pairs={{0,12},{4,8},{8,4},{12,0},{1,13},{5,9},{9,5},{13,1},{2,14},{6,10},... | collective-permute-start | bytes 589832 | tf_op jit(solution)/shard_map/ppermute | solution.py:299
  10.1 6.2 %collective-permute-done.5.refs_9_ = f32[384,128]{1,0:T(8,128)S(1)} collective-permute-done((f32[384,128]{1,0:T(8,128)}, f32[384,128]{1,0:T(8,128)S(1)}, u32[]{:S(2)}, u32[]{:S(2)}) %collective-permute-start.5) | collective-permute-done | bytes 196640 | tf_op jit(solution)/shard_map/ppermute | solution.py:299
  16.3 3.2 %collective-permute-start.6 = (f32[384,128]{1,0:T(8,128)S(1)}, f32[384,128]{1,0:T(8,128)S(1)}, u32[]{:S(2)}, u32[]{:S(2)}) collective-permute-start(f32[384,128]{1,0:T(8,128)S(1)} %collective-permute-done.5.refs_9_), channel_id=1, source_target_pairs={{0,4},{4,0},{8,12},{12,8},{1,5},{5,1},{9,13},{13,9},{2,6},{6,2},{1... | collective-permute-start | bytes 589832 | tf_op jit(solution)/shard_map/ppermute | solution.py:300
  19.5 1.1 %copy-done.2 = f32[384,384]{1,0:T(8,128)S(1)} copy-done((f32[384,384]{1,0:T(8,128)S(1)}, f32[384,384]{1,0:T(8,128)}, u32[]{:S(2)}) %copy-start.2) | copy-done | bytes 589848
  20.6 0.9 %copy-done.3 = f32[384,128]{1,0:T(8,128)S(1)} copy-done((f32[384,128]{1,0:T(8,128)S(1)}, f32[384,128]{1,0:T(8,128)}, u32[]{:S(2)}) %copy-start.3) | copy-done | bytes 196632
  21.5 1.2 %shard_map.68 = (bf16[384,512]{1,0:T(8,128)(2,1)S(1)}, bf16[384,512]{1,0:T(8,128)(2,1)S(1)}, f32[128,512]{1,0:T(8,128)S(1)}, bf16[384,256]{1,0:T(8,128)(2,1)S(1)...) custom-call(f32[384,512]{1,0:T(8,128)S(1)} %copy-done.1, f32[512,512]{1,0:T(8,128)S(1)} %copy-done, ...), custom_call_target="tpu_custom_call" | custom-call | tf_op jit(solution)/shard_map/pallas_call | solution.py:178
  22.9 0.5 %collective-permute-start.3 = (f32[128,384]{1,0:T(8,128)S(1)}, f32[128,384]{1,0:T(8,128)S(1)}, u32[]{:S(2)}, u32[]{:S(2)}) collective-permute-start(f32[128,384]{1,0:T(8,128)S(1)} %get-tuple-element.60), channel_id=1, source_target_pairs={{0,1},{1,0},{2,3},{3,2},{4,5},{5,4},{6,7},{7,6},{8,9},{9,8},{10,11... | collective-permute-start | bytes 589832 | tf_op jit(solution)/shard_map/ppermute | solution.py:305
  23.5 0.6 %collective-permute-done.6.refs_8_ = f32[384,128]{1,0:T(8,128)S(1)} collective-permute-done((f32[384,128]{1,0:T(8,128)S(1)}, f32[384,128]{1,0:T(8,128)S(1)}, u32[]{:S(2)}, u32[]{:S(2)}) %collective-permute-start.6) | collective-permute-done | bytes 196640 | tf_op jit(solution)/shard_map/ppermute | solution.py:300
  24.9 1.3 %shard_map.69 = (f32[128,128]{1,0:T(8,128)S(1)}, f32[128,128]{1,0:T(8,128)S(1)}, f32[128,128]{1,0:T(8,128)S(1)}, f32[128,128]{1,0:T(8,128)S(1)}, f32[192,128]{1,0:T(8,128)S(1)}, /*index=5*/f32[192,128]{1,0:T(8,128)S(1)}) custom-call(f32[128,512]{1,0:T(8,128)S(1)} %get-tuple-element.36.refs_0_, bf16[384,768]{1,0:T(8,128)(2,1)S(1)} %get-tuple-element.37.refs_1_, ...), custom_call_target="tpu_custom_call" | custom-call | tf_op jit(solution)/shard_map/pallas_call | solution.py:234
  26.5 2.5 %collective-permute-start.10 = (f32[128,128]{1,0:T(8,128)S(1)}, f32[128,128]{1,0:T(8,128)S(1)}, u32[]{:S(2)}, u32[]{:S(2)}) collective-permute-start(f32[128,128]{1,0:T(8,128)S(1)} %get-tuple-element.46), channel_id=1, source_target_pairs={{0,12},{4,8},{8,4},{12,0},{1,13},{5,9},{9,5},{13,1},{2,14},{6,10},... | collective-permute-start | bytes 196616 | tf_op jit(solution)/shard_map/ppermute | solution.py:311
  28.9 1.9 %collective-permute-start.9 = (f32[128,128]{1,0:T(8,128)S(1)}, f32[128,128]{1,0:T(8,128)S(1)}, u32[]{:S(2)}, u32[]{:S(2)}) collective-permute-start(f32[128,128]{1,0:T(8,128)S(1)} %get-tuple-element.45), channel_id=1, source_target_pairs={{0,4},{4,0},{8,12},{12,8},{1,5},{5,1},{9,13},{13,9},{2,6},{6,2},{1... | collective-permute-start | bytes 196616 | tf_op jit(solution)/shard_map/ppermute | solution.py:311
  30.9 0.6 %collective-permute-start.13 = (f32[96,128]{1,0:T(8,128)S(1)}, f32[96,128]{1,0:T(8,128)S(1)}, u32[]{:S(2)}, u32[]{:S(2)}) collective-permute-start(f32[96,128]{1,0:T(8,128)S(1)} %slice.18), channel_id=1, source_target_pairs={{0,2},{2,0},{1,3},{3,1},{4,6},{6,4},{5,7},{7,5},{8,10},{10,8},{9,1... | collective-permute-start | bytes 147464 | tf_op jit(solution)/shard_map/ppermute | solution.py:313
  31.4 1.5 %collective-permute-start.15 = (f32[96,128]{1,0:T(8,128)S(1)}, f32[96,128]{1,0:T(8,128)S(1)}, u32[]{:S(2)}, u32[]{:S(2)}) collective-permute-start(f32[96,128]{1,0:T(8,128)S(1)} %slice.20), channel_id=1, source_target_pairs={{0,2},{2,0},{1,3},{3,1},{4,6},{6,4},{5,7},{7,5},{8,10},{10,8},{9,1... | collective-permute-start | bytes 147464 | tf_op jit(solution)/shard_map/ppermute | solution.py:314
  33.3 2.1 %collective-permute-done.8 = f32[128,128]{1,0:T(8,128)S(1)} collective-permute-done((f32[128,128]{1,0:T(8,128)S(1)}, f32[128,128]{1,0:T(8,128)S(1)}, u32[]{:S(2)}, u32[]{:S(2)}) %collective-permute-start.8) | collective-permute-done | bytes 65568 | tf_op jit(solution)/shard_map/ppermute | solution.py:311
  35.4 0.9 %collective-permute-start.11 = (f32[128,128]{1,0:T(8,128)S(1)}, f32[128,128]{1,0:T(8,128)S(1)}, u32[]{:S(2)}, u32[]{:S(2)}) collective-permute-start(f32[128,128]{1,0:T(8,128)S(1)} %add_add_fusion.own), channel_id=1, source_target_pairs={{0,8},{4,12},{8,0},{12,4},{1,9},{5,13},{9,1},{13,5},{2,10},{6,14},... | collective-permute-start | bytes 196616 | tf_op jit(solution)/shard_map/ppermute | solution.py:318
  36.3 2.2 %collective-permute-start.12 = (f32[128,128]{1,0:T(8,128)S(1)}, f32[128,128]{1,0:T(8,128)S(1)}, u32[]{:S(2)}, u32[]{:S(2)}) collective-permute-start(f32[128,128]{1,0:T(8,128)S(1)} %add_add_fusion.own), channel_id=1, source_target_pairs={{0,12},{4,8},{8,4},{12,0},{1,13},{5,9},{9,5},{13,1},{2,14},{6,10},... | collective-permute-start | bytes 196616 | tf_op jit(solution)/shard_map/ppermute | solution.py:318
  38.5 0.4 collective-permute-start.16
  38.9 0.7 %shard_map.70 = f32[96,512]{1,0:T(8,128)} custom-call(f32[192,128]{1,0:T(8,128)S(1)} %get-tuple-element.47.own, f32[192,128]{1,0:T(8,128)S(1)} %collective-permute-done.14.near, f32[96,128]{1,0:T(8,128)S(1)} %collective-permute-done.13.across, f32[96,128]{1,0:T(8,128)S(1)} %collective-permute-done.15.far), custom_call_target="tpu_custom_call" | custom-call | tf_op jit(solution)/shard_map/pallas_call | solution.py:258
  39.6 3.8 %collective-permute-done.11.first = f32[128,128]{1,0:T(8,128)S(1)} collective-permute-done((f32[128,128]{1,0:T(8,128)S(1)}, f32[128,128]{1,0:T(8,128)S(1)}, u32[]{:S(2)}, u32[]{:S(2)}) %collective-permute-start.11) | collective-permute-done | bytes 65568 | tf_op jit(solution)/shard_map/ppermute | solution.py:318
  43.4 0.4 %collective-permute-done.16.third = f32[128,128]{1,0:T(8,128)S(1)} collective-permute-done((f32[128,128]{1,0:T(8,128)S(1)}, f32[128,128]{1,0:T(8,128)S(1)}, u32[]{:S(2)}, u32[]{:S(2)}) %collective-permute-start.16) | collective-permute-done | bytes 65568 | tf_op jit(solution)/shard_map/ppermute | solution.py:318
  43.9 0.7 %shard_map.71 = (f32[128,512]{1,0:T(8,128)}, f32[1,128]{1,0:T(1,128)}) custom-call(f32[128,128]{1,0:T(8,128)S(1)} %add_add_fusion.own, f32[128,128]{1,0:T(8,128)S(1)} %collective-permute-done.11.first, f32[128,128]{1,0:T(8,128)S(1)} %collective-permute-done.12.second, f32[128,128]{1,0:T(8,128)S(1)} %collective-permute-done.16.third), custom_call_target="tpu_custom_call" | custom-call | tf_op jit(solution)/shard_map/pallas_call | solution.py:279
  (27 shorter events, 1.6 us)
Async XLA Ops:
  0.6 18.9 %copy-start.1 = (f32[384,512]{1,0:T(8,128)S(1)}, f32[384,512]{1,0:T(8,128)}, u32[]{:S(2)}) copy-start(f32[384,512]{1,0:T(8,128)} %refs_0_.1) | copy-start | bytes 2359300
  0.6 18.8 %copy-start = (f32[512,512]{1,0:T(8,128)S(1)}, f32[512,512]{1,0:T(8,128)}, u32[]{:S(2)}) copy-start(f32[512,512]{1,0:T(8,128)} %refs_1_.1) | copy-start | bytes 3145732
  3.4 16.1 %collective-permute-start.1 = (f32[384,384]{1,0:T(8,128)}, f32[384,384]{1,0:T(8,128)S(1)}, u32[]{:S(2)}, u32[]{:S(2)}) collective-permute-start(f32[384,384]{1,0:T(8,128)} %get-tuple-element.31.refs_3_), channel_id=1, source_target_pairs={{0,1},{1,0},{2,3},{3,2},{4,5},{5,4},{6,7},{7,6},{8,9},{9,8},{10,11... | collective-permute-start | bytes 1769480 | tf_op jit(solution)/shard_map/ppermute | solution.py:298
  3.9 18.8 %collective-permute-start = (f32[384,384]{1,0:T(8,128)}, f32[384,384]{1,0:T(8,128)S(1)}, u32[]{:S(2)}, u32[]{:S(2)}) collective-permute-start(f32[384,384]{1,0:T(8,128)} %get-tuple-element.31.refs_3_), channel_id=1, source_target_pairs={{0,2},{2,0},{1,3},{3,1},{4,6},{6,4},{5,7},{7,5},{8,10},{10,8},{9,1... | collective-permute-start | bytes 1769480 | tf_op jit(solution)/shard_map/ppermute | solution.py:297
  6.5 9.8 %collective-permute-start.5 = (f32[384,128]{1,0:T(8,128)}, f32[384,128]{1,0:T(8,128)S(1)}, u32[]{:S(2)}, u32[]{:S(2)}) collective-permute-start(f32[384,128]{1,0:T(8,128)} %get-tuple-element.32.refs_2_), channel_id=1, source_target_pairs={{0,12},{4,8},{8,4},{12,0},{1,13},{5,9},{9,5},{13,1},{2,14},{6,10},... | collective-permute-start | bytes 589832 | tf_op jit(solution)/shard_map/ppermute | solution.py:299
  10.1 13.3 %collective-permute-start.7 = (f32[384,128]{1,0:T(8,128)}, f32[384,128]{1,0:T(8,128)S(1)}, u32[]{:S(2)}, u32[]{:S(2)}) collective-permute-start(f32[384,128]{1,0:T(8,128)} %get-tuple-element.32.refs_2_), channel_id=1, source_target_pairs={{0,4},{4,0},{8,12},{12,8},{1,5},{5,1},{9,13},{13,9},{2,6},{6,2},{1... | collective-permute-start | bytes 589832 | tf_op jit(solution)/shard_map/ppermute | solution.py:299
  16.3 7.8 %collective-permute-start.6 = (f32[384,128]{1,0:T(8,128)S(1)}, f32[384,128]{1,0:T(8,128)S(1)}, u32[]{:S(2)}, u32[]{:S(2)}) collective-permute-start(f32[384,128]{1,0:T(8,128)S(1)} %collective-permute-done.5.refs_9_), channel_id=1, source_target_pairs={{0,4},{4,0},{8,12},{12,8},{1,5},{5,1},{9,13},{13,9},{2,6},{6,2},{1... | collective-permute-start | bytes 589832 | tf_op jit(solution)/shard_map/ppermute | solution.py:300
  19.5 1.1 %copy-start.2 = (f32[384,384]{1,0:T(8,128)S(1)}, f32[384,384]{1,0:T(8,128)}, u32[]{:S(2)}) copy-start(f32[384,384]{1,0:T(8,128)} %get-tuple-element.31.refs_3_) | copy-start | bytes 1769476
  20.6 0.9 %copy-start.3 = (f32[384,128]{1,0:T(8,128)S(1)}, f32[384,128]{1,0:T(8,128)}, u32[]{:S(2)}) copy-start(f32[384,128]{1,0:T(8,128)} %get-tuple-element.32.refs_2_) | copy-start | bytes 589828
  22.8 1.5 %collective-permute-start.2 = (f32[128,384]{1,0:T(8,128)S(1)}, f32[128,384]{1,0:T(8,128)S(1)}, u32[]{:S(2)}, u32[]{:S(2)}) collective-permute-start(f32[128,384]{1,0:T(8,128)S(1)} %get-tuple-element.61), channel_id=1, source_target_pairs={{0,1},{1,0},{2,3},{3,2},{4,5},{5,4},{6,7},{7,6},{8,9},{9,8},{10,11... | collective-permute-start | bytes 589832 | tf_op jit(solution)/shard_map/ppermute | solution.py:305
  22.9 1.7 %collective-permute-start.3 = (f32[128,384]{1,0:T(8,128)S(1)}, f32[128,384]{1,0:T(8,128)S(1)}, u32[]{:S(2)}, u32[]{:S(2)}) collective-permute-start(f32[128,384]{1,0:T(8,128)S(1)} %get-tuple-element.60), channel_id=1, source_target_pairs={{0,1},{1,0},{2,3},{3,2},{4,5},{5,4},{6,7},{7,6},{8,9},{9,8},{10,11... | collective-permute-start | bytes 589832 | tf_op jit(solution)/shard_map/ppermute | solution.py:305
  23.4 1.5 %collective-permute-start.4 = (f32[128,384]{1,0:T(8,128)S(1)}, f32[128,384]{1,0:T(8,128)S(1)}, u32[]{:S(2)}, u32[]{:S(2)}) collective-permute-start(f32[128,384]{1,0:T(8,128)S(1)} %get-tuple-element.59), channel_id=1, source_target_pairs={{0,1},{1,0},{2,3},{3,2},{4,5},{5,4},{6,7},{7,6},{8,9},{9,8},{10,11... | collective-permute-start | bytes 589832 | tf_op jit(solution)/shard_map/ppermute | solution.py:305
  26.2 5.2 %collective-permute-start.14 = (f32[192,128]{1,0:T(8,128)S(1)}, f32[192,128]{1,0:T(8,128)S(1)}, u32[]{:S(2)}, u32[]{:S(2)}) collective-permute-start(f32[192,128]{1,0:T(8,128)S(1)} %get-tuple-element.48), channel_id=1, source_target_pairs={{0,1},{1,0},{2,3},{3,2},{4,5},{5,4},{6,7},{7,6},{8,9},{9,8},{10,11... | collective-permute-start | bytes 294920 | tf_op jit(solution)/shard_map/ppermute | solution.py:310
  26.5 6.8 %collective-permute-start.10 = (f32[128,128]{1,0:T(8,128)S(1)}, f32[128,128]{1,0:T(8,128)S(1)}, u32[]{:S(2)}, u32[]{:S(2)}) collective-permute-start(f32[128,128]{1,0:T(8,128)S(1)} %get-tuple-element.46), channel_id=1, source_target_pairs={{0,12},{4,8},{8,4},{12,0},{1,13},{5,9},{9,5},{13,1},{2,14},{6,10},... | collective-permute-start | bytes 196616 | tf_op jit(solution)/shard_map/ppermute | solution.py:311
  28.9 6.4 %collective-permute-start.8 = (f32[128,128]{1,0:T(8,128)S(1)}, f32[128,128]{1,0:T(8,128)S(1)}, u32[]{:S(2)}, u32[]{:S(2)}) collective-permute-start(f32[128,128]{1,0:T(8,128)S(1)} %get-tuple-element.44), channel_id=1, source_target_pairs={{0,8},{4,12},{8,0},{12,4},{1,9},{5,13},{9,1},{13,5},{2,10},{6,14},... | collective-permute-start | bytes 196616 | tf_op jit(solution)/shard_map/ppermute | solution.py:311
  28.9 6.4 %collective-permute-start.9 = (f32[128,128]{1,0:T(8,128)S(1)}, f32[128,128]{1,0:T(8,128)S(1)}, u32[]{:S(2)}, u32[]{:S(2)}) collective-permute-start(f32[128,128]{1,0:T(8,128)S(1)} %get-tuple-element.45), channel_id=1, source_target_pairs={{0,4},{4,0},{8,12},{12,8},{1,5},{5,1},{9,13},{13,9},{2,6},{6,2},{1... | collective-permute-start | bytes 196616 | tf_op jit(solution)/shard_map/ppermute | solution.py:311
  30.9 7.7 %collective-permute-start.13 = (f32[96,128]{1,0:T(8,128)S(1)}, f32[96,128]{1,0:T(8,128)S(1)}, u32[]{:S(2)}, u32[]{:S(2)}) collective-permute-start(f32[96,128]{1,0:T(8,128)S(1)} %slice.18), channel_id=1, source_target_pairs={{0,2},{2,0},{1,3},{3,1},{4,6},{6,4},{5,7},{7,5},{8,10},{10,8},{9,1... | collective-permute-start | bytes 147464 | tf_op jit(solution)/shard_map/ppermute | solution.py:313
  31.4 7.1 %collective-permute-start.15 = (f32[96,128]{1,0:T(8,128)S(1)}, f32[96,128]{1,0:T(8,128)S(1)}, u32[]{:S(2)}, u32[]{:S(2)}) collective-permute-start(f32[96,128]{1,0:T(8,128)S(1)} %slice.20), channel_id=1, source_target_pairs={{0,2},{2,0},{1,3},{3,1},{4,6},{6,4},{5,7},{7,5},{8,10},{10,8},{9,1... | collective-permute-start | bytes 147464 | tf_op jit(solution)/shard_map/ppermute | solution.py:314
  35.4 8.0 %collective-permute-start.11 = (f32[128,128]{1,0:T(8,128)S(1)}, f32[128,128]{1,0:T(8,128)S(1)}, u32[]{:S(2)}, u32[]{:S(2)}) collective-permute-start(f32[128,128]{1,0:T(8,128)S(1)} %add_add_fusion.own), channel_id=1, source_target_pairs={{0,8},{4,12},{8,0},{12,4},{1,9},{5,13},{9,1},{13,5},{2,10},{6,14},... | collective-permute-start | bytes 196616 | tf_op jit(solution)/shard_map/ppermute | solution.py:318
  36.3 7.1 %collective-permute-start.12 = (f32[128,128]{1,0:T(8,128)S(1)}, f32[128,128]{1,0:T(8,128)S(1)}, u32[]{:S(2)}, u32[]{:S(2)}) collective-permute-start(f32[128,128]{1,0:T(8,128)S(1)} %add_add_fusion.own), channel_id=1, source_target_pairs={{0,12},{4,8},{8,4},{12,0},{1,13},{5,9},{9,5},{13,1},{2,14},{6,10},... | collective-permute-start | bytes 196616 | tf_op jit(solution)/shard_map/ppermute | solution.py:318
  38.5 5.3 %collective-permute-start.16 = (f32[128,128]{1,0:T(8,128)S(1)}, f32[128,128]{1,0:T(8,128)S(1)}, u32[]{:S(2)}, u32[]{:S(2)}) collective-permute-start(f32[128,128]{1,0:T(8,128)S(1)} %add_add_fusion.own), channel_id=1, source_target_pairs={{0,4},{4,0},{8,12},{12,8},{1,5},{5,1},{9,13},{13,9},{2,6},{6,2},{1... | collective-permute-start | bytes 196616 | tf_op jit(solution)/shard_map/ppermute | solution.py:318
